TPU v7x, 32 devices: a whole 2x2x4 slice. The times are simulated.
32 devices in a mesh: dp: 8 (over y, x, core), tensor: 4 (over z).
Axes of the slice: x: 2, y: 2, z: 4, core: 2. Of those that a mesh axis runs over, the one named last changes fastest.
Arguments:
- tokens: bfloat16 [8192, 2048], P(('dp', 'tensor')), may hold values from -6 to 6
- segment_ids: int32 [8, 1024], P('dp'), may hold values from 0 to 3, never falling along the last dimension, each value on 1 to 512 neighbouring positions
- attn_gain: bfloat16 [2048], P('dp'), may hold values from 0.5 to 1.5
- w_query: bfloat16 [2048, 2048], P('dp', 'tensor'), may hold values from -0.125 to 0.125
- w_key: bfloat16 [2048, 2048], P('dp', 'tensor'), may hold values from -0.125 to 0.125
- w_value: bfloat16 [2048, 4096], P('dp', 'tensor'), may hold values from -0.125 to 0.125
- w_gate: bfloat16 [2048, 4096], P('dp', 'tensor'), may hold values from -0.125 to 0.125
- w_out: bfloat16 [2048, 4096], P('dp', 'tensor'), may hold values from -0.09375 to 0.09375
- mlp_gain: bfloat16 [2048], P('dp'), may hold values from 0.5 to 1.5
- w_mlp_gate: bfloat16 [2048, 4096], P('dp', 'tensor'), may hold values from -0.125 to 0.125
- w_mlp_up: bfloat16 [2048, 4096], P('dp', 'tensor'), may hold values from -0.125 to 0.125
- w_down: bfloat16 [2048, 4096], P('dp', 'tensor'), may hold values from -0.09375 to 0.09375
- cotangent: bfloat16 [8192, 2048], P(('dp', 'tensor')), may hold values from -6 to 6
Outputs:
- output: bfloat16 [8192, 2048], P(('dp', 'tensor'))
- tokens_grad: bfloat16 [8192, 2048], P(('dp', 'tensor'))
- attn_gain_grad: float32 [2048], P('dp')
- w_query_grad: float32 [2048, 2048], P('dp', 'tensor')
- w_key_grad: float32 [2048, 2048], P('dp', 'tensor')
- w_value_grad: float32 [2048, 4096], P('dp', 'tensor')
- w_gate_grad: float32 [2048, 4096], P('dp', 'tensor')
- w_out_grad: float32 [2048, 4096], P('dp', 'tensor')
- mlp_gain_grad: float32 [2048], P('dp')
- w_mlp_gate_grad: float32 [2048, 4096], P('dp', 'tensor')
- w_mlp_up_grad: float32 [2048, 4096], P('dp', 'tensor')
- w_down_grad: float32 [2048, 4096], P('dp', 'tensor')
Inputs may be any that keep to these rules, and one draw needn't show every extreme that they name: `segment_ids`: along each sequence the document numbers never fall; a run of equal numbers is one document of at most 512 tokens, and one document of each sequence has exactly that length.
All inputs are finite; a program needn't handle non-finite values.
Results may differ from a plain program's by a relative error of at most 0.015.
Values may be sent and summed in bfloat16 or wider, within the bound.
A program may use at most 256 MiB of HBM per device.

v0:
```python
import jax
import jax.numpy as jnp
from jax import lax
from jax.sharding import PartitionSpec as P

HEADS = 8
KD = 256
VD = 512
BLOCK = 512


EPS_NORM = 1e-06
EPS_GROUP = 1.0
CONTRACT_ROWS = (((0,), (0,)), ((), ()))
CONTRACT_COLUMNS = (((1,), (1,)), ((), ()))


def normalize(row_block, gain_vec):
    inverse = lax.rsqrt(jnp.mean(row_block * row_block, axis=-1, keepdims=True) + EPS_NORM)
    return row_block * inverse * gain_vec


def rotary_tables(length, channel_count):
    positions = jnp.arange(length).astype(jnp.float32)[:, None]
    frequency = 10000.0 ** (
        -jnp.arange(channel_count // 2).astype(jnp.float32) * (2.0 / channel_count)
    )
    angles = positions * frequency[None, :]
    angles = jnp.concatenate([angles, angles], axis=1)
    return (jnp.cos(angles), jnp.sin(angles))


def rotate(values, cosine_table, sine_table):
    half_width = values.shape[-1] // 2
    turned = jnp.concatenate([-values[..., half_width:], values[..., :half_width]], axis=-1)
    return values * cosine_table[:, None, :] + turned * sine_table[:, None, :]


def gated_norm(heads_out, gate_pre):
    average = jnp.mean(heads_out, axis=-1, keepdims=True)
    centred = heads_out - average
    variance = jnp.mean(centred * centred, axis=-1, keepdims=True)
    normed = centred * lax.rsqrt(variance + EPS_GROUP)
    return jax.nn.silu(gate_pre) * normed.reshape(gate_pre.shape)


def decay_mask(seg_rows, seg_columns, start_row, logdecay):
    row_ids = start_row + jnp.arange(seg_rows.shape[0])
    col_ids = jnp.arange(seg_columns.shape[0])
    distance = row_ids[:, None] - col_ids[None, :]
    allowed = (distance >= 0) & (seg_rows[:, None] == seg_columns[None, :])
    spans_float = jnp.maximum(distance, 0).astype(jnp.float32)
    return jnp.where(allowed[None], jnp.exp(logdecay[:, None, None] * spans_float[None]), 0.0)


def block_terms(queries, keys_rot, start_row, logdecay, segments):
    end_row = start_row + BLOCK
    decay = decay_mask(segments[start_row:end_row], segments[:end_row], start_row, logdecay)
    scores = jnp.einsum(
        "bhk,mhk->hbm",
        queries[start_row:end_row],
        keys_rot[:end_row],
        preferred_element_type=jnp.float32,
    )
    return (decay, (scores * decay).astype(jnp.bfloat16))


def fetch_attention(attn_gain, w_query, w_key, w_value, w_gate, w_out):
    return (
        lax.all_gather(attn_gain, "dp", axis=0, tiled=True),
        lax.all_gather(w_query, "dp", axis=0, tiled=True),
        lax.all_gather(w_key, "dp", axis=0, tiled=True),
        lax.all_gather(w_value, "dp", axis=0, tiled=True),
        lax.all_gather(w_gate, "dp", axis=0, tiled=True),
        lax.all_gather(w_out, "dp", axis=0, tiled=True),
    )


def fetch_mlp(mlp_gain, w_mlp_gate, w_mlp_up, w_down):
    return (
        lax.all_gather(mlp_gain, "dp", axis=0, tiled=True),
        lax.all_gather(w_mlp_gate, "dp", axis=0, tiled=True),
        lax.all_gather(w_mlp_up, "dp", axis=0, tiled=True),
        lax.all_gather(w_down, "dp", axis=0, tiled=True),
    )


def shards(
    tokens,
    segment_ids,
    attn_gain,
    w_query,
    w_key,
    w_value,
    w_gate,
    w_out,
    mlp_gain,
    w_mlp_gate,
    w_mlp_up,
    w_down,
    cotangent,
):
    tensor_parts = lax.axis_size("tensor")
    local_rows = tokens.shape[0]
    length = local_rows * tensor_parts
    heads_dev = HEADS // tensor_parts
    key_cols = heads_dev * KD
    value_cols = heads_dev * VD
    hidden_cols = w_mlp_gate.shape[1]
    segments = segment_ids[0]
    gain_one, query_full, key_full, value_full, gate_full, out_full = fetch_attention(
        attn_gain, w_query, w_key, w_value, w_gate, w_out
    )
    w_in = jnp.concatenate([query_full, key_full, value_full, gate_full], axis=1)
    inputs = tokens.astype(jnp.float32)
    normed_one = lax.all_gather(
        normalize(inputs, gain_one.astype(jnp.float32)).astype(jnp.bfloat16),
        "tensor",
        axis=0,
        tiled=True,
    )
    projected = jnp.dot(normed_one, w_in, preferred_element_type=jnp.float32)
    query_pre = projected[:, :key_cols].reshape(length, heads_dev, KD)
    key_pre = projected[:, key_cols : 2 * key_cols].reshape(length, heads_dev, KD)
    values = (
        projected[:, 2 * key_cols : 2 * key_cols + value_cols]
        .reshape(length, heads_dev, VD)
        .astype(jnp.bfloat16)
    )
    gate_pre = projected[:, 2 * key_cols + value_cols :]
    cosine_table, sine_table = rotary_tables(length, KD)

    def turn_query(query_part):
        return rotate(query_part, cosine_table, sine_table)

    def turn_key(key_part):
        return rotate(key_part, cosine_table, sine_table) * KD ** (-0.5)

    queries = turn_query(query_pre).astype(jnp.bfloat16)
    keys_rot = turn_key(key_pre).astype(jnp.bfloat16)
    head_ids = lax.axis_index("tensor") * heads_dev + jnp.arange(heads_dev)
    logdecay = jnp.log(1.0 - 2.0 ** (-5.0 - head_ids.astype(jnp.float32)))
    pieces = []
    for block_index in range(length // BLOCK):
        start_row = block_index * BLOCK
        decay, weights = block_terms(queries, keys_rot, start_row, logdecay, segments)
        pieces.append(
            jnp.einsum(
                "hbm,mhv->bhv",
                weights,
                values[: start_row + BLOCK],
                preferred_element_type=jnp.float32,
            )
        )
    heads_out = jnp.concatenate(pieces, axis=0)
    mixed = gated_norm(heads_out, gate_pre).astype(jnp.bfloat16)
    part_rows = mixed
    residual = inputs + lax.psum_scatter(
        lax.dot_general(part_rows, out_full, CONTRACT_COLUMNS, preferred_element_type=jnp.float32),
        "tensor",
        scatter_dimension=0,
        tiled=True,
    )
    gain_two, gate_w_full, up_w_full, down_full = fetch_mlp(mlp_gain, w_mlp_gate, w_mlp_up, w_down)
    w_pair = jnp.concatenate([gate_w_full, up_w_full], axis=1)
    normed_two = lax.all_gather(
        normalize(residual, gain_two.astype(jnp.float32)).astype(jnp.bfloat16),
        "tensor",
        axis=0,
        tiled=True,
    )
    both_hidden = jnp.dot(normed_two, w_pair, preferred_element_type=jnp.float32)
    hidden_gate = both_hidden[:, :hidden_cols]
    hidden_up = both_hidden[:, hidden_cols:]
    hidden = (jax.nn.gelu(hidden_gate, approximate=True) * hidden_up).astype(jnp.bfloat16)
    part_rows = hidden
    result = residual + lax.psum_scatter(
        lax.dot_general(part_rows, down_full, CONTRACT_COLUMNS, preferred_element_type=jnp.float32),
        "tensor",
        scatter_dimension=0,
        tiled=True,
    )
    d_branch_two = lax.all_gather(cotangent, "tensor", axis=0, tiled=True)
    gain_two, gate_w_full, up_w_full, down_full = fetch_mlp(mlp_gain, w_mlp_gate, w_mlp_up, w_down)
    w_pair = jnp.concatenate([gate_w_full, up_w_full], axis=1)
    grad_down = lax.dot_general(
        d_branch_two, hidden, CONTRACT_ROWS, preferred_element_type=jnp.float32
    )
    d_hidden = jnp.dot(d_branch_two, down_full, preferred_element_type=jnp.float32)
    _, gelu_pull = jax.vjp(
        lambda gate_part, up_part: jax.nn.gelu(gate_part, approximate=True) * up_part,
        hidden_gate,
        hidden_up,
    )
    d_gate_hidden, d_up_hidden = gelu_pull(d_hidden)
    d_pair = jnp.concatenate([d_gate_hidden, d_up_hidden], axis=1).astype(jnp.bfloat16)
    grad_pair = lax.dot_general(
        normed_two, d_pair, CONTRACT_ROWS, preferred_element_type=jnp.float32
    )
    part_rows = d_pair
    d_normed_two = lax.psum_scatter(
        lax.dot_general(part_rows, w_pair, CONTRACT_COLUMNS, preferred_element_type=jnp.float32),
        "tensor",
        scatter_dimension=0,
        tiled=True,
    )
    _, norm_pull_two = jax.vjp(normalize, residual, gain_two.astype(jnp.float32))
    d_residual_norm, d_gain_two = norm_pull_two(d_normed_two)
    d_residual = cotangent.astype(jnp.float32) + d_residual_norm
    grad_mlp_gate = grad_pair[:, :hidden_cols]
    grad_mlp_up = grad_pair[:, hidden_cols:]
    mlp_grads = (
        lax.psum_scatter(d_gain_two, "dp", scatter_dimension=0, tiled=True),
        lax.psum_scatter(grad_mlp_gate, "dp", scatter_dimension=0, tiled=True),
        lax.psum_scatter(grad_mlp_up, "dp", scatter_dimension=0, tiled=True),
        lax.psum_scatter(grad_down, "dp", scatter_dimension=0, tiled=True),
    )
    d_branch_one = lax.all_gather(d_residual.astype(jnp.bfloat16), "tensor", axis=0, tiled=True)
    gain_one, query_full, key_full, value_full, gate_full, out_full = fetch_attention(
        attn_gain, w_query, w_key, w_value, w_gate, w_out
    )
    w_in = jnp.concatenate([query_full, key_full, value_full, gate_full], axis=1)
    grad_out = lax.dot_general(
        d_branch_one, mixed, CONTRACT_ROWS, preferred_element_type=jnp.float32
    )
    d_mixed = jnp.dot(d_branch_one, out_full, preferred_element_type=jnp.float32)
    _, gated_pull = jax.vjp(gated_norm, heads_out, gate_pre)
    d_heads_full, d_gate_pre = gated_pull(d_mixed)
    d_heads = d_heads_full.astype(jnp.bfloat16)
    d_query_parts = []
    d_keys = jnp.zeros((length, heads_dev, KD), jnp.float32)
    d_values = jnp.zeros((length, heads_dev, VD), jnp.float32)
    for block_index in range(length // BLOCK):
        start_row = block_index * BLOCK
        end_row = start_row + BLOCK
        decay, weights = block_terms(queries, keys_rot, start_row, logdecay, segments)
        d_probs = jnp.einsum(
            "bhv,mhv->hbm",
            d_heads[start_row:end_row],
            values[:end_row],
            preferred_element_type=jnp.float32,
        )
        d_scores = (d_probs * decay).astype(jnp.bfloat16)
        d_values = d_values.at[:end_row].add(
            jnp.einsum(
                "hbm,bhv->mhv",
                weights,
                d_heads[start_row:end_row],
                preferred_element_type=jnp.float32,
            )
        )
        d_query_parts.append(
            jnp.einsum(
                "hbm,mhk->bhk", d_scores, keys_rot[:end_row], preferred_element_type=jnp.float32
            )
        )
        d_keys = d_keys.at[:end_row].add(
            jnp.einsum(
                "hbm,bhk->mhk",
                d_scores,
                queries[start_row:end_row],
                preferred_element_type=jnp.float32,
            )
        )
    _, query_pull = jax.vjp(turn_query, query_pre)
    _, key_pull = jax.vjp(turn_key, key_pre)
    (d_query_pre,) = query_pull(jnp.concatenate(d_query_parts, axis=0))
    (d_key_pre,) = key_pull(d_keys)
    d_in = jnp.concatenate(
        [
            d_query_pre.reshape(length, key_cols),
            d_key_pre.reshape(length, key_cols),
            d_values.reshape(length, value_cols),
            d_gate_pre,
        ],
        axis=1,
    ).astype(jnp.bfloat16)
    grad_in = lax.dot_general(normed_one, d_in, CONTRACT_ROWS, preferred_element_type=jnp.float32)
    part_rows = d_in
    d_normed_one = lax.psum_scatter(
        lax.dot_general(part_rows, w_in, CONTRACT_COLUMNS, preferred_element_type=jnp.float32),
        "tensor",
        scatter_dimension=0,
        tiled=True,
    )
    _, norm_pull_one = jax.vjp(normalize, inputs, gain_one.astype(jnp.float32))
    d_inputs_norm, d_gain_one = norm_pull_one(d_normed_one)
    tokens_grad = (d_residual + d_inputs_norm).astype(jnp.bfloat16)
    grad_query = grad_in[:, :key_cols]
    grad_key = grad_in[:, key_cols : 2 * key_cols]
    grad_value = grad_in[:, 2 * key_cols : 2 * key_cols + value_cols]
    grad_gate = grad_in[:, 2 * key_cols + value_cols :]
    attn_grads = (
        lax.psum_scatter(d_gain_one, "dp", scatter_dimension=0, tiled=True),
        lax.psum_scatter(grad_query, "dp", scatter_dimension=0, tiled=True),
        lax.psum_scatter(grad_key, "dp", scatter_dimension=0, tiled=True),
        lax.psum_scatter(grad_value, "dp", scatter_dimension=0, tiled=True),
        lax.psum_scatter(grad_gate, "dp", scatter_dimension=0, tiled=True),
        lax.psum_scatter(grad_out, "dp", scatter_dimension=0, tiled=True),
    )
    gain_grads = lax.psum((attn_grads[0], mlp_grads[0]), "tensor")
    return (
        result.astype(jnp.bfloat16),
        tokens_grad,
        gain_grads[0],
        attn_grads[1],
        attn_grads[2],
        attn_grads[3],
        attn_grads[4],
        attn_grads[5],
        gain_grads[1],
        mlp_grads[1],
        mlp_grads[2],
        mlp_grads[3],
    )


def solution(mesh):
    return jax.shard_map(
        shards,
        mesh=mesh,
        in_specs=(
            P(("dp", "tensor"), None),
            P("dp", None),
            P("dp"),
            P("dp", "tensor"),
            P("dp", "tensor"),
            P("dp", "tensor"),
            P("dp", "tensor"),
            P("dp", "tensor"),
            P("dp"),
            P("dp", "tensor"),
            P("dp", "tensor"),
            P("dp", "tensor"),
            P(("dp", "tensor"), None),
        ),
        out_specs=(
            P(("dp", "tensor"), None),
            P(("dp", "tensor"), None),
            P("dp"),
            P("dp", "tensor"),
            P("dp", "tensor"),
            P("dp", "tensor"),
            P("dp", "tensor"),
            P("dp", "tensor"),
            P("dp"),
            P("dp", "tensor"),
            P("dp", "tensor"),
            P("dp", "tensor"),
        ),
        check_vma=False,
    )
```

profile of v0, /device:TPU:0, one launch (start us, length us, event | category | flops | bytes accessed | tf_op | source)
XLA Modules:
  0.0 1848.5 jit_solution(17029864616757107490)
XLA Ops:
  10.7 10.3 all-gather
  35.5 5.1 all-gather.17.cloned.1.call-done
  43.7 26.6 %all-gather.19.cloned.1.call-done = bf16[2048,512]{1,0:T(8,128)(2,1)} async-done(((bf16[256,512]{1,0:T(8,128)(2,1)}), bf16[2048,512]{1,0:T(8,128)(2,1)}) %all-gather.19.cloned.1.call-update) | async-done | bytes 2097168 | tf_op jit(solution)/shard_map/all_gather | solution.py:72
  73.5 35.5 %all-gather.21.cloned.1.call-done = bf16[2048,1024]{1,0:T(8,128)(2,1)} async-done(((bf16[256,1024]{1,0:T(8,128)(2,1)}), bf16[2048,1024]{1,0:T(8,128)(2,1)}) %all-gather.21.cloned.1.call-update) | async-done | bytes 4194320 | tf_op jit(solution)/shard_map/all_gather | solution.py:73
  109.0 4.8 constant_dynamic-update-slice_fusion.1
  113.8 33.7 %all-gather.23.cloned.1.call-done = bf16[2048,1024]{1,0:T(8,128)(2,1)} async-done(((bf16[256,1024]{1,0:T(8,128)(2,1)}), bf16[2048,1024]{1,0:T(8,128)(2,1)}) %all-gather.23.cloned.1.call-update) | async-done | bytes 4194320 | tf_op jit(solution)/shard_map/all_gather | solution.py:74
  147.5 4.8 constant_dynamic-update-slice_fusion
  152.2 78.0 %all-gather.15.cloned.1.call-done = bf16[1024,2048]{1,0:T(8,128)(2,1)} async-done(((bf16[256,2048]{1,0:T(8,128)(2,1)}), bf16[1024,2048]{1,0:T(8,128)(2,1)}) %all-gather.15.cloned.1.call-update) | async-done | bytes 4194320 | tf_op jit(solution)/shard_map/all_gather | solution.py:116
  230.3 17.2 fusion.77
  266.5 5.3 copy.106
  274.3 5.4 copy.105
  284.5 8.7 multiply_convert_fusion.3
  293.3 10.6 fusion.78
  305.5 9.0 all-gather.1
  314.5 132.8 %reduce-scatter.13.cloned.1.call-done = f32[256,2048]{1,0:T(8,128)} async-done(((f32[1024,2048]{1,0:T(8,128)}), f32[256,2048]{1,0:T(8,128)}) %reduce-scatter.13.cloned.1.call-update) | async-done | bytes 2097168 | tf_op jit(solution)/shard_map/reduce_scatter | solution.py:158
  453.1 33.5 %all-gather.29.cloned.1.call-done = bf16[2048,1024]{1,0:T(8,128)(2,1)} async-done(((bf16[256,1024]{1,0:T(8,128)(2,1)}), bf16[2048,1024]{1,0:T(8,128)(2,1)}) %all-gather.29.cloned.1.call-update) | async-done | bytes 4194320 | tf_op jit(solution)/shard_map/all_gather | solution.py:82
  491.3 34.0 %all-gather.31.cloned.1.call-done = bf16[2048,1024]{1,0:T(8,128)(2,1)} async-done(((bf16[256,1024]{1,0:T(8,128)(2,1)}), bf16[2048,1024]{1,0:T(8,128)(2,1)}) %all-gather.31.cloned.1.call-update) | async-done | bytes 4194320 | tf_op jit(solution)/shard_map/all_gather | solution.py:83
  530.0 78.1 %all-gather.27.cloned.1.call-done = bf16[1024,2048]{1,0:T(8,128)(2,1)} async-done(((bf16[256,2048]{1,0:T(8,128)(2,1)}), bf16[1024,2048]{1,0:T(8,128)(2,1)}) %all-gather.27.cloned.1.call-update) | async-done | bytes 4194320 | tf_op jit(solution)/shard_map/all_gather | solution.py:166
  608.1 14.4 fusion.79
  622.5 66.5 %all-gather.35.cloned.1.call-done = bf16[1024,2048]{1,0:T(8,128)(2,1)} async-done(((bf16[256,2048]{1,0:T(8,128)(2,1)}), bf16[1024,2048]{1,0:T(8,128)(2,1)}) %all-gather.35.cloned.1.call-update) | async-done | bytes 4194320 | tf_op jit(solution)/shard_map/all_gather | solution.py:183
  689.0 37.0 %all-gather.33.cloned.1.call-done = bf16[2048,1024]{1,0:T(8,128)(2,1)} async-done(((bf16[256,1024]{1,0:T(8,128)(2,1)}), bf16[2048,1024]{1,0:T(8,128)(2,1)}) %all-gather.33.cloned.1.call-update) | async-done | bytes 4194320 | tf_op jit(solution)/shard_map/all_gather | solution.py:84
  726.0 13.4 fusion.6
  741.4 11.1 fusion.14
  752.6 144.6 %reduce-scatter.17.cloned.1.call-done = f32[256,2048]{1,0:T(8,128)} async-done(((f32[1024,2048]{1,0:T(8,128)}), f32[256,2048]{1,0:T(8,128)}) %reduce-scatter.17.cloned.1.call-update) | async-done | bytes 2097168 | tf_op jit(solution)/shard_map/reduce_scatter | solution.py:201
  903.2 10.9 convolution_bitcast_fusion
  918.3 66.3 %all-gather.37.cloned.1.call-done = bf16[1024,2048]{1,0:T(8,128)(2,1)} async-done(((bf16[256,2048]{1,0:T(8,128)(2,1)}), bf16[1024,2048]{1,0:T(8,128)(2,1)}) %all-gather.37.cloned.1.call-update) | async-done | bytes 4194320 | tf_op jit(solution)/shard_map/all_gather | solution.py:218
  984.6 13.7 fusion.54
  998.3 6.0 copy.109
  1041.0 20.1 %fusion.39 = f32[1024,2048]{1,0:T(8,128)} fusion(bf16[2048,3072]{1,0:T(8,128)(2,1)} %constant_dynamic-update-slice_fusion, bf16[1024,1024]{1,0:T(8,128)(2,1)} %get-tuple-element.117, bf16[1024,1024]{1,0:T(8,128)(2,1)S(1)} %copy-done.33, bf16[1024,512]{1,0:T(8,128)(2,1)S(1)} %copy-done.36, bf16[1024,512]{1,0:T(8,128)(2,1)} %bitcast.119), kind=kOutput, calls=%fused_computation.89 | convolution fusion | flops 12910067712 | bytes 27262976 | tf_op jit(solution)/shard_map/dot_general | solution.py:281
  1061.2 10.7 fusion.80
  1071.9 12.3 fusion.13
  1084.3 6.7 fusion.72
  1091.7 20.3 %fusion.38 = f32[2048,3072]{1,0:T(8,128)} fusion(bf16[1024,2048]{1,0:T(8,128)(2,1)} %all-gather.15.cloned.1.call-done, bf16[1024,1024]{1,0:T(8,128)(2,1)} %get-tuple-element.117, bf16[1024,1024]{1,0:T(8,128)(2,1)S(1)} %copy-done.33, bf16[1024,512]{1,0:T(8,128)(2,1)S(1)} %copy-done.36, bf16[1024,512]{1,0:T(8,128)(2,1)} %bitcast.120), kind=kOutput, calls=%fused_computation.88 | convolution fusion | flops 12910067712 | bytes 35651584 | tf_op jit(solution)/shard_map/dot_general | solution.py:278
  1112.1 7.9 fusion.71
  1120.7 11.0 fusion.70
  1133.4 9.1 fusion.81
  1147.0 57.6 %reduce-scatter.19.cloned.1.call-done = f32[256,2048]{1,0:T(8,128)} async-done(((f32[1024,2048]{1,0:T(8,128)}), f32[256,2048]{1,0:T(8,128)}) %reduce-scatter.19.cloned.1.call-update) | async-done | bytes 2097168 | tf_op jit(solution)/shard_map/reduce_scatter | solution.py:280
  1206.9 24.0 %all-reduce.8 = (f32[2048]{0:T(1024)S(1)}, f32[2048]{0:T(1024)S(1)}) all-reduce(f32[2048]{0:T(1024)S(1)} %get-tuple-element.102, f32[2048]{0:T(1024)S(1)} %copy-done.43), channel_id=6, replica_groups=mesh['dp'=8,'tensor'=4] {'dp'}, use_global_device_ids=true, to_apply=%region_13.14.clone | all-reduce | flops 4096 | bytes 32768
  1231.0 12.8 all-reduce.9
  1243.8 108.6 %reduce-scatter.15.cloned.1.call-done = f32[256,2048]{1,0:T(8,128)} async-done(((f32[1024,2048]{1,0:T(8,128)}), f32[256,2048]{1,0:T(8,128)}) %reduce-scatter.15.cloned.1.call-update) | async-done | bytes 2097168 | tf_op jit(solution)/shard_map/reduce_scatter | solution.py:177
  1352.4 5.6 fusion.21
  1358.0 70.7 %reduce-scatter.31.cloned.1.call-done = f32[256,1024]{1,0:T(8,128)} async-done(((f32[2048,1024]{1,0:T(8,128)}), f32[256,1024]{1,0:T(8,128)}) %reduce-scatter.31.cloned.1.call-update) | async-done | bytes 1048592 | tf_op jit(solution)/shard_map/reduce_scatter | solution.py:214
  1428.7 75.3 %reduce-scatter.33.cloned.1.call-done = f32[256,1024]{1,0:T(8,128)} async-done(((f32[2048,1024]{1,0:T(8,128)}), f32[256,1024]{1,0:T(8,128)}) %reduce-scatter.33.cloned.1.call-update) | async-done | bytes 1048592 | tf_op jit(solution)/shard_map/reduce_scatter | solution.py:215
  1504.0 55.5 %reduce-scatter.21.cloned.1.call-done = f32[256,512]{1,0:T(8,128)} async-done(((f32[2048,512]{1,0:T(8,128)}), f32[256,512]{1,0:T(8,128)}) %reduce-scatter.21.cloned.1.call-update) | async-done | bytes 524304 | tf_op jit(solution)/shard_map/reduce_scatter | solution.py:295
  1559.5 55.3 %reduce-scatter.23.cloned.1.call-done = f32[256,512]{1,0:T(8,128)} async-done(((f32[2048,512]{1,0:T(8,128)}), f32[256,512]{1,0:T(8,128)}) %reduce-scatter.23.cloned.1.call-update) | async-done | bytes 524304 | tf_op jit(solution)/shard_map/reduce_scatter | solution.py:296
  1614.8 75.7 %reduce-scatter.25.cloned.1.call-done = f32[256,1024]{1,0:T(8,128)} async-done(((f32[2048,1024]{1,0:T(8,128)}), f32[256,1024]{1,0:T(8,128)}) %reduce-scatter.25.cloned.1.call-update) | async-done | bytes 1048592 | tf_op jit(solution)/shard_map/reduce_scatter | solution.py:297
  1690.5 75.4 %reduce-scatter.27.cloned.1.call-done = f32[256,1024]{1,0:T(8,128)} async-done(((f32[2048,1024]{1,0:T(8,128)}), f32[256,1024]{1,0:T(8,128)}) %reduce-scatter.27.cloned.1.call-update) | async-done | bytes 1048592 | tf_op jit(solution)/shard_map/reduce_scatter | solution.py:298
  1765.9 75.6 %reduce-scatter.29.cloned.1.call-done = f32[256,1024]{1,0:T(8,128)} async-done(((f32[2048,1024]{1,0:T(8,128)}), f32[256,1024]{1,0:T(8,128)}) %reduce-scatter.29.cloned.1.call-update) | async-done | bytes 1048592 | tf_op jit(solution)/shard_map/reduce_scatter | solution.py:299
  (244 shorter events, 125.0 us)
Async XLA Ops:
  7.2 33.4 %all-gather.17.cloned.1.call-start = ((), (), s32[]{:S(2)}) async-start(), calls=%async_computation.13 | async-start | bytes 2359296 | tf_op jit(solution)/shard_map/all_gather | solution.py:71
  7.9 62.4 %all-gather.19.cloned.1.call-start = ((), (), s32[]{:S(2)}) async-start(), calls=%async_computation.14 | async-start | bytes 2359296 | tf_op jit(solution)/shard_map/all_gather | solution.py:72
  8.7 100.3 %all-gather.21.cloned.1.call-start = ((), (), s32[]{:S(2)}) async-start(), calls=%async_computation.15 | async-start | bytes 4718592 | tf_op jit(solution)/shard_map/all_gather | solution.py:73
  9.4 138.1 %all-gather.23.cloned.1.call-start = ((), (), s32[]{:S(2)}) async-start(), calls=%async_computation.16 | async-start | bytes 4718592 | tf_op jit(solution)/shard_map/all_gather | solution.py:74
  10.0 220.3 %all-gather.15.cloned.1.call-start = ((), (), s32[]{:S(2)}) async-start(), calls=%async_computation.12 | async-start | bytes 5242880 | tf_op jit(solution)/shard_map/all_gather | solution.py:116
  26.2 267.1 %all-gather.25.cloned.1.call-start = ((), (), s32[]{:S(2)}) async-start(), calls=%async_computation.17 | async-start | bytes 4718592 | tf_op jit(solution)/shard_map/all_gather | solution.py:75
  26.8 420.5 %reduce-scatter.13.cloned.1.call-start = ((), (), s32[]{:S(2)}) async-start(), calls=%async_computation.18 | async-start | bytes 10485760 | tf_op jit(solution)/shard_map/reduce_scatter | solution.py:158
  26.9 6.9 copy-start.48
  27.0 229.4 %copy-start.35 = (f32[512,512]{1,0:T(8,128)}, f32[512,512]{1,0:T(8,128)S(1)}, u32[]{:S(2)}) copy-start(f32[512,512]{1,0:T(8,128)S(1)} %maximum_convert_fusion.1) | copy-start | bytes 3145732
  31.8 223.7 %copy-start.9 = (f32[1024,256]{1,0:T(8,128)}, f32[1024,256]{1,0:T(8,128)S(1)}, u32[]{:S(2)}) copy-start(f32[1024,256]{1,0:T(8,128)S(1)} %get-tuple-element.137) | copy-start | bytes 3145732
  31.8 223.7 %copy-start.12 = (f32[1024,256]{1,0:T(8,128)}, f32[1024,256]{1,0:T(8,128)S(1)}, u32[]{:S(2)}) copy-start(f32[1024,256]{1,0:T(8,128)S(1)} %get-tuple-element.138) | copy-start | bytes 3145732
  247.5 7.4 copy-start.17
  303.9 143.4 %copy-start.6 = (bf16[256,2048]{1,0:T(8,128)(2,1)S(1)}, bf16[256,2048]{1,0:T(8,128)(2,1)}, u32[]{:S(2)}) copy-start(bf16[256,2048]{1,0:T(8,128)(2,1)} %param.25) | copy-start | bytes 3145732
  303.9 182.7 %all-gather.29.cloned.1.call-start = ((), (), s32[]{:S(2)}) async-start(), calls=%async_computation.20 | async-start | bytes 4718592 | tf_op jit(solution)/shard_map/all_gather | solution.py:82
  304.7 220.6 %all-gather.31.cloned.1.call-start = ((), (), s32[]{:S(2)}) async-start(), calls=%async_computation.21 | async-start | bytes 4718592 | tf_op jit(solution)/shard_map/all_gather | solution.py:83
  305.4 302.6 %all-gather.27.cloned.1.call-start = ((), (), s32[]{:S(2)}) async-start(), calls=%async_computation.19 | async-start | bytes 5242880 | tf_op jit(solution)/shard_map/all_gather | solution.py:166
  314.5 586.2 %copy-start.39 = (f32[8,1,256]{2,1,0:T(1,128)}, f32[8,1,256]{2,1,0:T(1,128)S(1)}, u32[]{:S(2)}) copy-start(f32[8,1,256]{2,1,0:T(1,128)S(1)} %convert_element_type.130) | copy-start | bytes 24580
  449.2 451.4 %copy-start.44 = (f32[256]{0:T(256)}, f32[256]{0:T(256)S(1)}, u32[]{:S(2)}) copy-start(f32[256]{0:T(256)S(1)} %fusion.64) | copy-start | bytes 3076
  451.8 237.2 %all-gather.35.cloned.1.call-start = ((), (), s32[]{:S(2)}) async-start(), calls=%async_computation.24 | async-start | bytes 5242880 | tf_op jit(solution)/shard_map/all_gather | solution.py:183
  452.5 273.5 %all-gather.33.cloned.1.call-start = ((), (), s32[]{:S(2)}) async-start(), calls=%async_computation.22 | async-start | bytes 4718592 | tf_op jit(solution)/shard_map/all_gather | solution.py:84
  453.1 444.1 %reduce-scatter.17.cloned.1.call-start = ((), (), s32[]{:S(2)}) async-start(), calls=%async_computation.25 | async-start | bytes 10485760 | tf_op jit(solution)/shard_map/reduce_scatter | solution.py:201
  726.0 15.5 copy-start.30
  752.5 148.7 %copy-start.11 = (bf16[256,2048]{1,0:T(8,128)(2,1)S(1)}, bf16[256,2048]{1,0:T(8,128)(2,1)}, u32[]{:S(2)}) copy-start(bf16[256,2048]{1,0:T(8,128)(2,1)} %param.37) | copy-start | bytes 3145732
  752.5 232.1 %all-gather.37.cloned.1.call-start = ((), (), s32[]{:S(2)}) async-start(), calls=%async_computation.26 | async-start | bytes 5242880 | tf_op jit(solution)/shard_map/all_gather | solution.py:218
  903.0 241.5 %reduce-scatter.35.cloned.1.call-start = ((), (), s32[]{:S(2)}) async-start(), calls=%async_computation.35 | async-start | bytes 9437184 | tf_op jit(solution)/shard_map/reduce_scatter | solution.py:216
  914.1 290.4 %reduce-scatter.19.cloned.1.call-start = ((), (), s32[]{:S(2)}) async-start(), calls=%async_computation.27 | async-start | bytes 10485760 | tf_op jit(solution)/shard_map/reduce_scatter | solution.py:280
  1004.3 4.7 copy-start.2
  1011.3 5.0 copy-start.18
  1016.2 4.4 copy-start.19
  1029.8 5.7 copy-start.15
  1031.4 6.2 copy-start.10
  1061.1 291.2 %reduce-scatter.15.cloned.1.call-start = ((), (), s32[]{:S(2)}) async-start(), calls=%async_computation.23 | async-start | bytes 10485760 | tf_op jit(solution)/shard_map/reduce_scatter | solution.py:177
  1071.9 356.8 %reduce-scatter.31.cloned.1.call-start = ((), (), s32[]{:S(2)}) async-start(), calls=%async_computation.33 | async-start | bytes 9437184 | tf_op jit(solution)/shard_map/reduce_scatter | solution.py:214
  1090.9 413.1 %reduce-scatter.33.cloned.1.call-start = ((), (), s32[]{:S(2)}) async-start(), calls=%async_computation.34 | async-start | bytes 9437184 | tf_op jit(solution)/shard_map/reduce_scatter | solution.py:215
  1091.7 467.8 %reduce-scatter.21.cloned.1.call-start = ((), (), s32[]{:S(2)}) async-start(), calls=%async_computation.28 | async-start | bytes 4718592 | tf_op jit(solution)/shard_map/reduce_scatter | solution.py:295
  1119.9 494.8 %reduce-scatter.23.cloned.1.call-start = ((), (), s32[]{:S(2)}) async-start(), calls=%async_computation.29 | async-start | bytes 4718592 | tf_op jit(solution)/shard_map/reduce_scatter | solution.py:296
  1120.7 569.9 %reduce-scatter.25.cloned.1.call-start = ((), (), s32[]{:S(2)}) async-start(), calls=%async_computation.30 | async-start | bytes 9437184 | tf_op jit(solution)/shard_map/reduce_scatter | solution.py:297
  1131.8 634.1 %reduce-scatter.27.cloned.1.call-start = ((), (), s32[]{:S(2)}) async-start(), calls=%async_computation.31 | async-start | bytes 9437184 | tf_op jit(solution)/shard_map/reduce_scatter | solution.py:298
  1132.5 709.0 %reduce-scatter.29.cloned.1.call-start = ((), (), s32[]{:S(2)}) async-start(), calls=%async_computation.32 | async-start | bytes 9437184 | tf_op jit(solution)/shard_map/reduce_scatter | solution.py:299
  1142.6 62.0 %copy-start.7 = (bf16[256,2048]{1,0:T(8,128)(2,1)S(1)}, bf16[256,2048]{1,0:T(8,128)(2,1)}, u32[]{:S(2)}) copy-start(bf16[256,2048]{1,0:T(8,128)(2,1)} %param.25) | copy-start | bytes 3145732
  1142.6 62.0 %copy-start.42 = (f32[8,1,256]{2,1,0:T(1,128)S(1)}, f32[8,1,256]{2,1,0:T(1,128)}, u32[]{:S(2)}) copy-start(f32[8,1,256]{2,1,0:T(1,128)} %copy-done.41) | copy-start | bytes 24580
  1142.6 62.0 %copy-start.47 = (f32[256]{0:T(256)S(1)}, f32[256]{0:T(256)}, u32[]{:S(2)}) copy-start(f32[256]{0:T(256)} %copy-done.46) | copy-start | bytes 3076
  1142.6 64.3 %copy-start.43 = (f32[2048]{0:T(1024)S(1)}, f32[2048]{0:T(1024)}, u32[]{:S(2)}) copy-start(f32[2048]{0:T(1024)} %get-tuple-element.100) | copy-start | bytes 24580
  1142.6 101.2 %copy-start.52 = (f32[256]{0:T(256)S(1)}, f32[256]{0:T(256)}, u32[]{:S(2)}) copy-start(f32[256]{0:T(256)} %copy-done.51) | copy-start | bytes 3076
  1142.6 209.7 %copy-start.5 = (f32[256,2048]{1,0:T(8,128)S(1)}, f32[256,2048]{1,0:T(8,128)}, u32[]{:S(2)}) copy-start(f32[256,2048]{1,0:T(8,128)} %copy-done.3) | copy-start | bytes 6291460
  1142.6 209.7 %copy-start.40 = (f32[8,1,256]{2,1,0:T(1,128)S(1)}, f32[8,1,256]{2,1,0:T(1,128)}, u32[]{:S(2)}) copy-start(f32[8,1,256]{2,1,0:T(1,128)} %copy-done.39) | copy-start | bytes 24580
  1142.6 209.7 %copy-start.45 = (f32[256]{0:T(256)S(1)}, f32[256]{0:T(256)}, u32[]{:S(2)}) copy-start(f32[256]{0:T(256)} %copy-done.44) | copy-start | bytes 3076
  1142.6 209.7 %copy-start.50 = (f32[256]{0:T(256)S(1)}, f32[256]{0:T(256)}, u32[]{:S(2)}) copy-start(f32[256]{0:T(256)} %copy-done.49) | copy-start | bytes 3076
  (35 other events, 77.2 us)
Sparse Core Ops, SparseCore 0:
  9.9 30.5 all-gather.16
  42.4 27.8 all-gather.18
  72.2 36.7 all-gather.20
  110.7 36.7 all-gather.22
  149.5 80.7 all-gather.14
  232.0 35.2 all-gather.24
  304.1 143.1 reduce-scatter.12
  449.2 37.4 all-gather.28
  488.5 36.7 all-gather.30
  527.3 80.7 all-gather.26
  609.6 79.2 all-gather.34
  690.7 35.2 all-gather.32
  752.7 144.4 reduce-scatter.16
  903.1 81.4 all-gather.36
  987.9 69.7 reduce-scatter.34
  1061.3 143.2 reduce-scatter.18
  1206.9 145.4 reduce-scatter.14
  1356.6 72.0 reduce-scatter.30
  1432.7 71.2 reduce-scatter.32
  1508.2 51.2 reduce-scatter.20
  1563.5 51.2 reduce-scatter.22
  1619.2 71.2 reduce-scatter.24
  1694.6 71.2 reduce-scatter.26
  1770.2 71.2 reduce-scatter.28
where the time goes:
time: 1860 us; the launch traced here: 1850 us
  waiting for transfers between devices  1430 us (77%)
  matrix products  181 us (10%)
  local copies, waits for them, and re-layouts  116 us (6%)
  blocking collectives  56 us (3%)
  other arithmetic  48.3 us (3%)
    reduce_scatter x1, waiting for transfers between devices, shards(): lax.psum_scatter(lax.dot_general(part_rows, w_pair, CONTRACT_COLUMNS, pre...  145 us
    reduce_scatter x1, waiting for transfers between devices, shards(): lax.psum_scatter(lax.dot_general(part_rows, out_full, CONTRACT_COLUMNS, p...  133 us
    reduce_scatter x1, waiting for transfers between devices, shards(): lax.psum_scatter(lax.dot_general(part_rows, down_full, CONTRACT_COLUMNS,...  109 us
    all_gather x1, waiting for transfers between devices, shards(): lax.all_gather(normalize(residual, gain_two.astype(jnp.float32)).astype(j...  78.1 us
    all_gather x1, waiting for transfers between devices, shards(): lax.all_gather(normalize(inputs, gain_one.astype(jnp.float32)).astype(jnp...  78 us
    reduce_scatter x1, waiting for transfers between devices, shards(): lax.psum_scatter(grad_value, 'dp', scatter_dimension=0, tiled=True)  75.7 us
    reduce_scatter x1, waiting for transfers between devices, shards(): lax.psum_scatter(grad_out, 'dp', scatter_dimension=0, tiled=True)  75.6 us
    reduce_scatter x1, waiting for transfers between devices, shards(): lax.psum_scatter(grad_gate, 'dp', scatter_dimension=0, tiled=True)  75.4 us
  transfers between devices with their start and end apart: 24, of which 22 were waited for; matrix products, arithmetic and copies ran while one was open for 16% of the time, Pallas kernels for 0%

commit v1 on v0

v1 whole, which is shorter than its diff:
```python
import functools
import jax
import jax.numpy as jnp
from jax import lax
from jax.experimental import pallas as pl
from jax.experimental.pallas import tpu as pltpu
from jax.sharding import PartitionSpec as P

AXIS = "tensor"


def line_body(n, chunks, rs, ag, middle, n_in, n_out, *refs):
    ins, outs, scratch = refs[:n_in], refs[n_in : n_in + n_out], list(refs[n_in + n_out :])
    me = lax.axis_index(AXIS)
    last = n - 1
    lag = last if rs else 0
    if rs:
        part, ins = ins[0], ins[1:]
        up_buf, dn_buf, total, up_send, up_recv, dn_send, dn_recv = scratch[:7]
        scratch = scratch[7:]
        rows = up_buf.shape[1]
    if ag:
        full, outs = outs[0], outs[1:]
        own, ag_recv, ag_up, ag_dn, ag_here = scratch[:5]
        rows = own.shape[0]
    size = rows // chunks

    def cut(c, base=0):
        return pl.ds(pl.multiple_of(base + c * size, size), size)

    def send(src, dst, send_sem, recv_sem, to):
        return pltpu.make_async_remote_copy(
            src_ref=src,
            dst_ref=dst,
            send_sem=send_sem,
            recv_sem=recv_sem,
            device_id={AXIS: to},
            device_id_type=pl.DeviceIdType.MESH,
        )

    barrier = pltpu.get_barrier_semaphore()

    @pl.when(me > 0)
    def _():
        pl.semaphore_signal(barrier, inc=1, device_id={AXIS: me - 1}, device_id_type=pl.DeviceIdType.MESH)

    @pl.when(me < last)
    def _():
        pl.semaphore_signal(barrier, inc=1, device_id={AXIS: me + 1}, device_id_type=pl.DeviceIdType.MESH)

    pl.semaphore_wait(barrier, jnp.where((me > 0) & (me < last), 2, 1))

    def sum_copy(up, d, c):
        buf, s, r, to = (up_buf, up_send, up_recv, me + 1) if up else (dn_buf, dn_send, dn_recv, me - 1)
        ref = buf.at[d, cut(c)]
        return send(ref, ref, s.at[d, c], r.at[d, c], to)

    def sum_step(up, d, c):
        buf = up_buf if up else dn_buf
        first = 0 if up else last
        mine = part[cut(c, d * rows)]

        @pl.when(me == first)
        def _():
            buf[d, cut(c)] = mine

        @pl.when(me != first)
        def _():
            sum_copy(up, d, c).wait_recv()
            buf[d, cut(c)] = (buf[d, cut(c)].astype(jnp.float32) + mine.astype(jnp.float32)).astype(buf.dtype)

        sum_copy(up, d, c).start()

    def gather_copy(up, j, c, from_own=False):
        ref = full.at[cut(c, j * rows)]
        src = own.at[cut(c)] if from_own else ref
        return send(src, ref, (ag_up if up else ag_dn).at[j, c], ag_recv.at[j, c], me + 1 if up else me - 1)

    def here_copy(c):
        return pltpu.make_async_copy(own.at[cut(c)], full.at[cut(c, me * rows)], ag_here.at[c])

    def step(s, _):
        if rs:
            for up in (True, False):
                c = s - me if up else s - (last - me)
                for d in range(last, 0, -1) if up else range(last):

                    @pl.when((c >= 0) & (c < chunks) & ((me < d) if up else (me > d)))
                    def _(up=up, c=c, d=d):
                        sum_step(up, d, c)

        c_own = s - lag

        @pl.when((c_own >= 0) & (c_own < chunks))
        def _():
            c = c_own
            if rs:
                total[...] = part[cut(c, me * rows)].astype(jnp.float32)

                @pl.when(me > 0)
                def _():
                    sum_copy(True, me, c).wait_recv()
                    total[...] += up_buf[me, cut(c)].astype(jnp.float32)

                @pl.when(me < last)
                def _():
                    sum_copy(False, me, c).wait_recv()
                    total[...] += dn_buf[me, cut(c)].astype(jnp.float32)

                result = middle(cut(c), total[...], ins, outs)
            else:
                result = middle(cut(c), None, ins, outs)
            if ag:
                own[cut(c)] = result.astype(own.dtype)
                here_copy(c).start()

                @pl.when(me < last)
                def _():
                    gather_copy(True, me, c, True).start()

                @pl.when(me > 0)
                def _():
                    gather_copy(False, me, c, True).start()

        if ag:
            for t in range(1, last):
                c = s - lag - t
                for up in (True, False):
                    j = me - t if up else me + t

                    @pl.when((c >= 0) & (c < chunks) & (((j >= 0) & (me < last)) if up else ((j <= last) & (me > 0))))
                    def _(up=up, c=c, j=j):
                        gather_copy(up, j, c).wait_recv()
                        gather_copy(up, j, c).start()

        return 0

    lax.fori_loop(0, chunks + lag + (last - 1 if ag else 0), step, 0)

    def drain(c, _):
        if rs:
            for d in range(n):

                @pl.when(me < d)
                def _(d=d):
                    sum_copy(True, d, c).wait_send()

                @pl.when(me > d)
                def _(d=d):
                    sum_copy(False, d, c).wait_send()

        if ag:
            here_copy(c).wait()
            for j in range(n):

                @pl.when(((me == last) & (j < me)) | ((me == 0) & (j > me)))
                def _(j=j):
                    gather_copy(True, j, c).wait_recv()

                @pl.when((me < last) & (j <= me))
                def _(j=j):
                    gather_copy(True, j, c).wait_send()

                @pl.when((me > 0) & (j >= me))
                def _(j=j):
                    gather_copy(False, j, c).wait_send()

        return 0

    lax.fori_loop(0, chunks, drain, 0)


def line_pass(name, part, extras, extra_outs, middle, ag, chunks, collective_id, rows, width):
    n = lax.axis_size(AXIS)
    rs = part is not None
    size = rows // chunks
    vmem = pl.BlockSpec(memory_space=pltpu.VMEM)
    scratch = []
    sems = pltpu.SemaphoreType.DMA((n, chunks))
    if rs:
        scratch += [
            pltpu.VMEM((n, rows, width), jnp.bfloat16),
            pltpu.VMEM((n, rows, width), jnp.bfloat16),
            pltpu.VMEM((size, width), jnp.float32),
            sems, sems, sems, sems,
        ]
    if ag:
        scratch += [pltpu.VMEM((rows, width), jnp.bfloat16), sems, sems, sems, pltpu.SemaphoreType.DMA((chunks,))]
    operands = ([part] if rs else []) + list(extras)
    shapes = ([jax.ShapeDtypeStruct((n * rows, width), jnp.bfloat16)] if ag else []) + [
        jax.ShapeDtypeStruct((rows, width), kind) for kind in extra_outs
    ]
    specs = ([pl.BlockSpec(memory_space=pl.ANY)] if ag else []) + [vmem] * len(extra_outs)
    moved = rows * width * 2 * (n - 1)
    return pl.pallas_call(
        functools.partial(line_body, n, chunks, rs, ag, middle, len(operands), len(shapes)),
        out_shape=shapes,
        in_specs=[vmem] * len(operands),
        out_specs=specs,
        scratch_shapes=scratch,
        compiler_params=pltpu.CompilerParams(
            collective_id=collective_id, has_side_effects=True, vmem_limit_bytes=48 * 1024 * 1024
        ),
        cost_estimate=pl.CostEstimate(
            flops=0, bytes_accessed=moved * 40, transcendentals=0, remote_bytes_transferred=moved
        ),
        name=name,
    )(*operands)


HEADS = 8
KD = 256
VD = 512
BLOCK = 512


EPS_NORM = 1e-06
EPS_GROUP = 1.0
CONTRACT_ROWS = (((0,), (0,)), ((), ()))
CONTRACT_COLUMNS = (((1,), (1,)), ((), ()))


def inverse_rms(rows):
    return lax.rsqrt(jnp.mean(rows * rows, axis=-1, keepdims=True) + EPS_NORM)


def norm_pull(unit, inverse, d_unit):
    return inverse * (d_unit - unit * jnp.mean(d_unit * unit, axis=-1, keepdims=True))


def rotary_tables(length, channel_count):
    positions = jnp.arange(length).astype(jnp.float32)[:, None]
    frequency = 10000.0 ** (
        -jnp.arange(channel_count // 2).astype(jnp.float32) * (2.0 / channel_count)
    )
    angles = positions * frequency[None, :]
    angles = jnp.concatenate([angles, angles], axis=1)
    return (jnp.cos(angles), jnp.sin(angles))


def rotate(values, cosine_table, sine_table):
    half_width = values.shape[-1] // 2
    turned = jnp.concatenate([-values[..., half_width:], values[..., :half_width]], axis=-1)
    return values * cosine_table[:, None, :] + turned * sine_table[:, None, :]


def gated_norm(heads_out, gate_pre):
    average = jnp.mean(heads_out, axis=-1, keepdims=True)
    centred = heads_out - average
    variance = jnp.mean(centred * centred, axis=-1, keepdims=True)
    normed = centred * lax.rsqrt(variance + EPS_GROUP)
    return jax.nn.silu(gate_pre) * normed.reshape(gate_pre.shape)


def decay_mask(seg_rows, seg_columns, start_row, logdecay):
    row_ids = start_row + jnp.arange(seg_rows.shape[0])
    col_ids = jnp.arange(seg_columns.shape[0])
    distance = row_ids[:, None] - col_ids[None, :]
    allowed = (distance >= 0) & (seg_rows[:, None] == seg_columns[None, :])
    spans_float = jnp.maximum(distance, 0).astype(jnp.float32)
    return jnp.where(allowed[None], jnp.exp(logdecay[:, None, None] * spans_float[None]), 0.0)


def block_terms(queries, keys_rot, start_row, logdecay, segments):
    end_row = start_row + BLOCK
    decay = decay_mask(segments[start_row:end_row], segments[:end_row], start_row, logdecay)
    scores = jnp.einsum(
        "bhk,mhk->hbm",
        queries[start_row:end_row],
        keys_rot[:end_row],
        preferred_element_type=jnp.float32,
    )
    return (decay, (scores * decay).astype(jnp.bfloat16))


def residual_step(cut, summed, ins, outs):
    residual = ins[0][cut].astype(jnp.float32) + summed
    outs[0][cut] = residual
    return residual * inverse_rms(residual)


def d_residual_step(cut, summed, ins, outs):
    residual = ins[0][cut]
    inverse = inverse_rms(residual)
    d_residual = ins[1][cut].astype(jnp.float32) + norm_pull(residual * inverse, inverse, summed)
    outs[0][cut] = d_residual
    return d_residual


def tokens_step(cut, summed, ins, outs):
    inputs = ins[0][cut].astype(jnp.float32)
    inverse = inverse_rms(inputs)
    grad = ins[1][cut] + norm_pull(inputs * inverse, inverse, summed)
    outs[0][cut] = grad.astype(outs[0].dtype)


def shards(
    tokens,
    segment_ids,
    attn_gain,
    w_query,
    w_key,
    w_value,
    w_gate,
    w_out,
    mlp_gain,
    w_mlp_gate,
    w_mlp_up,
    w_down,
    cotangent,
):
    tensor_parts = lax.axis_size("tensor")
    local_rows, width = tokens.shape
    length = local_rows * tensor_parts
    heads_dev = HEADS // tensor_parts
    key_cols = heads_dev * KD
    value_cols = heads_dev * VD
    hidden_cols = w_mlp_gate.shape[1]
    segments = segment_ids[0]
    gain_one = attn_gain.astype(jnp.float32)[:, None]
    gain_two = mlp_gain.astype(jnp.float32)[:, None]

    def gather(own):
        return lax.all_gather(own, "dp", axis=0, tiled=True)

    def scaled(gain, weight):
        return (weight.astype(jnp.float32) * gain).astype(jnp.bfloat16)

    def scatter(grad):
        return lax.psum_scatter(grad.astype(jnp.bfloat16), "dp", scatter_dimension=0, tiled=True).astype(jnp.float32)

    w_in_own = jnp.concatenate([scaled(gain_one, w) for w in (w_query, w_key, w_value, w_gate)], axis=1)
    w_pair_own = jnp.concatenate([scaled(gain_two, w) for w in (w_mlp_gate, w_mlp_up)], axis=1)
    w_in = gather(w_in_own)
    rest = gather(jnp.concatenate([w_out, w_pair_own, w_down], axis=1))
    out_full = rest[:, :value_cols]
    w_pair = rest[:, value_cols : value_cols + 2 * hidden_cols]
    down_full = rest[:, value_cols + 2 * hidden_cols :]

    inputs = tokens.astype(jnp.float32)
    unit_own = (inputs * inverse_rms(inputs)).astype(jnp.bfloat16)
    (unit_one,) = line_pass(
        "gather_one", None, [unit_own], [], lambda cut, _, ins, outs: ins[0][cut], True, 4, 0, local_rows, width
    )
    d_branch_two = lax.all_gather(cotangent, "tensor", axis=0, tiled=True)
    projected = jnp.dot(unit_one, w_in, preferred_element_type=jnp.float32)
    query_pre = projected[:, :key_cols].reshape(length, heads_dev, KD)
    key_pre = projected[:, key_cols : 2 * key_cols].reshape(length, heads_dev, KD)
    values = (
        projected[:, 2 * key_cols : 2 * key_cols + value_cols]
        .reshape(length, heads_dev, VD)
        .astype(jnp.bfloat16)
    )
    gate_pre = projected[:, 2 * key_cols + value_cols :]
    cosine_table, sine_table = rotary_tables(length, KD)

    def turn_query(query_part):
        return rotate(query_part, cosine_table, sine_table)

    def turn_key(key_part):
        return rotate(key_part, cosine_table, sine_table) * KD ** (-0.5)

    queries = turn_query(query_pre).astype(jnp.bfloat16)
    keys_rot = turn_key(key_pre).astype(jnp.bfloat16)
    head_ids = lax.axis_index("tensor") * heads_dev + jnp.arange(heads_dev)
    logdecay = jnp.log(1.0 - 2.0 ** (-5.0 - head_ids.astype(jnp.float32)))
    pieces = []
    for block_index in range(length // BLOCK):
        start_row = block_index * BLOCK
        decay, weights = block_terms(queries, keys_rot, start_row, logdecay, segments)
        pieces.append(
            jnp.einsum(
                "hbm,mhv->bhv",
                weights,
                values[: start_row + BLOCK],
                preferred_element_type=jnp.float32,
            )
        )
    heads_out = jnp.concatenate(pieces, axis=0)
    mixed = gated_norm(heads_out, gate_pre).astype(jnp.bfloat16)

    part_out = lax.dot_general(
        mixed, out_full, CONTRACT_COLUMNS, preferred_element_type=jnp.float32
    ).astype(jnp.bfloat16)
    unit_two, residual = line_pass(
        "residual", part_out, [tokens], [jnp.float32], residual_step, True, 16, 1, local_rows, width
    )
    both_hidden = jnp.dot(unit_two, w_pair, preferred_element_type=jnp.float32)
    hidden_gate = both_hidden[:, :hidden_cols]
    hidden_up = both_hidden[:, hidden_cols:]
    hidden = (jax.nn.gelu(hidden_gate, approximate=True) * hidden_up).astype(jnp.bfloat16)
    part_down = lax.dot_general(
        hidden, down_full, CONTRACT_COLUMNS, preferred_element_type=jnp.float32
    ).astype(jnp.bfloat16)
    result = residual + lax.psum_scatter(part_down, "tensor", scatter_dimension=0, tiled=True).astype(jnp.float32)

    grad_down = lax.dot_general(
        d_branch_two, hidden, CONTRACT_ROWS, preferred_element_type=jnp.float32
    )
    d_hidden = jnp.dot(d_branch_two, down_full, preferred_element_type=jnp.float32)
    _, gelu_pull = jax.vjp(
        lambda gate_part, up_part: jax.nn.gelu(gate_part, approximate=True) * up_part,
        hidden_gate,
        hidden_up,
    )
    d_gate_hidden, d_up_hidden = gelu_pull(d_hidden)
    d_pair = jnp.concatenate([d_gate_hidden, d_up_hidden], axis=1).astype(jnp.bfloat16)
    grad_pair = lax.dot_general(
        unit_two, d_pair, CONTRACT_ROWS, preferred_element_type=jnp.float32
    )
    part_pair = lax.dot_general(
        d_pair, w_pair, CONTRACT_COLUMNS, preferred_element_type=jnp.float32
    ).astype(jnp.bfloat16)
    d_branch_one, d_residual = line_pass(
        "d_residual", part_pair, [residual, cotangent], [jnp.float32], d_residual_step, True, 16, 2, local_rows, width
    )
    down_grad = scatter(grad_down)
    pair_grad = scatter(grad_pair)

    grad_out = lax.dot_general(
        d_branch_one, mixed, CONTRACT_ROWS, preferred_element_type=jnp.float32
    )
    out_grad = scatter(grad_out)
    d_mixed = jnp.dot(d_branch_one, out_full, preferred_element_type=jnp.float32)
    _, gated_pull = jax.vjp(gated_norm, heads_out, gate_pre)
    d_heads_full, d_gate_pre = gated_pull(d_mixed)
    d_heads = d_heads_full.astype(jnp.bfloat16)
    d_query_parts = []
    d_keys = jnp.zeros((length, heads_dev, KD), jnp.float32)
    d_values = jnp.zeros((length, heads_dev, VD), jnp.float32)
    for block_index in range(length // BLOCK):
        start_row = block_index * BLOCK
        end_row = start_row + BLOCK
        decay, weights = block_terms(queries, keys_rot, start_row, logdecay, segments)
        d_probs = jnp.einsum(
            "bhv,mhv->hbm",
            d_heads[start_row:end_row],
            values[:end_row],
            preferred_element_type=jnp.float32,
        )
        d_scores = (d_probs * decay).astype(jnp.bfloat16)
        d_values = d_values.at[:end_row].add(
            jnp.einsum(
                "hbm,bhv->mhv",
                weights,
                d_heads[start_row:end_row],
                preferred_element_type=jnp.float32,
            )
        )
        d_query_parts.append(
            jnp.einsum(
                "hbm,mhk->bhk", d_scores, keys_rot[:end_row], preferred_element_type=jnp.float32
            )
        )
        d_keys = d_keys.at[:end_row].add(
            jnp.einsum(
                "hbm,bhk->mhk",
                d_scores,
                queries[start_row:end_row],
                preferred_element_type=jnp.float32,
            )
        )
    _, query_pull = jax.vjp(turn_query, query_pre)
    _, key_pull = jax.vjp(turn_key, key_pre)
    (d_query_pre,) = query_pull(jnp.concatenate(d_query_parts, axis=0))
    (d_key_pre,) = key_pull(d_keys)
    d_in = jnp.concatenate(
        [
            d_query_pre.reshape(length, key_cols),
            d_key_pre.reshape(length, key_cols),
            d_values.reshape(length, value_cols),
            d_gate_pre,
        ],
        axis=1,
    ).astype(jnp.bfloat16)
    grad_in = lax.dot_general(unit_one, d_in, CONTRACT_ROWS, preferred_element_type=jnp.float32)
    in_grad = scatter(grad_in)
    part_in = lax.dot_general(
        d_in, w_in, CONTRACT_COLUMNS, preferred_element_type=jnp.float32
    ).astype(jnp.bfloat16)
    (tokens_grad,) = line_pass(
        "tokens_grad", part_in, [tokens, d_residual], [jnp.bfloat16], tokens_step, False, 8, 3, local_rows, width
    )

    def gain_terms(weights, grads):
        return jnp.sum(weights.astype(jnp.float32) * grads, axis=1)

    gain_sums = lax.psum((gain_terms(w_in_own, in_grad), gain_terms(w_pair_own, pair_grad)), "tensor")
    in_grad = in_grad * gain_one
    pair_grad = pair_grad * gain_two
    return (
        result.astype(jnp.bfloat16),
        tokens_grad,
        gain_sums[0] / gain_one[:, 0],
        in_grad[:, :key_cols],
        in_grad[:, key_cols : 2 * key_cols],
        in_grad[:, 2 * key_cols : 2 * key_cols + value_cols],
        in_grad[:, 2 * key_cols + value_cols :],
        out_grad,
        gain_sums[1] / gain_two[:, 0],
        pair_grad[:, :hidden_cols],
        pair_grad[:, hidden_cols:],
        down_grad,
    )


def solution(mesh):
    return jax.shard_map(
        shards,
        mesh=mesh,
        in_specs=(
            P(("dp", "tensor"), None),
            P("dp", None),
            P("dp"),
            P("dp", "tensor"),
            P("dp", "tensor"),
            P("dp", "tensor"),
            P("dp", "tensor"),
            P("dp", "tensor"),
            P("dp"),
            P("dp", "tensor"),
            P("dp", "tensor"),
            P("dp", "tensor"),
            P(("dp", "tensor"), None),
        ),
        out_specs=(
            P(("dp", "tensor"), None),
            P(("dp", "tensor"), None),
            P("dp"),
            P("dp", "tensor"),
            P("dp", "tensor"),
            P("dp", "tensor"),
            P("dp", "tensor"),
            P("dp", "tensor"),
            P("dp"),
            P("dp", "tensor"),
            P("dp", "tensor"),
            P("dp", "tensor"),
        ),
        check_vma=False,
    )
```

time: 1860 us -> 873 us (0.47)
  waiting for transfers between devices: 1430 us -> 96.8 us
  Pallas kernels: 0 us -> 441 us
  blocking collectives: 56 us -> 11.6 us
  local copies, waits for them, and re-layouts: 116 us -> 72.8 us
    reduce_scatter x12 -> x5, waiting for transfers between devices: 927 us -> 87.5 us  [the longest x4 87.5 us: scatter(): lax.psum_scatter(grad.astype(jnp.bfloat16), 'dp', scatter_dimension=0, ti...]
    pallas_call x0 -> x4, Pallas kernels: none -> 441 us  [line_pass(): pl.pallas_call(functools.partial(line_body, n, chunks, rs, ag, middle, le...]
    all_gather x11 -> x2, waiting for transfers between devices: 428 us -> 8.49 us  [gather(): return lax.all_gather(own, 'dp', axis=0, tiled=True)]
    all_gather x1, waiting for transfers between devices: 66.5 us -> 0.01 us  [shards(): d_branch_two = lax.all_gather(cotangent, 'tensor', axis=0, tiled=True)]
    unnamed x1 -> x0, blocking collectives: 24 us -> none
    slice x3, local copies, waits for them, and re-layouts: 25.5 us -> 3.95 us  [the longest x1 1.45 us: shards(): pair_grad[:, hidden_cols:]]
    all_gather x2 -> x0, blocking collectives: 19.3 us -> none  [the longest x1 10.3 us: fetch_attention(): lax.all_gather(attn_gain, 'dp', axis=0, tiled=True)]
    unnamed x128 -> x138, local copies, waits for them, and re-layouts: 37.7 us -> 23 us
  transfers between devices with their start and end apart: 24 -> 8, of which waited for: 22 -> 2; matrix products, arithmetic and copies ran while one was open for 16% -> 29% of each run, Pallas kernels for 0% -> 51%
where the time goes in v1:
time: 873 us; the launch traced here: 869 us
  Pallas kernels  441 us (51%)
  matrix products  183 us (21%)
  waiting for transfers between devices  96.8 us (11%)
  local copies, waits for them, and re-layouts  72.8 us (8%)
  other arithmetic  47.7 us (5%)
  between operations  15.2 us (2%)
  blocking collectives  11.6 us (1%)
    pallas_call x4, Pallas kernels, line_pass(): pl.pallas_call(functools.partial(line_body, n, chunks, rs, ag, middle, le...  441 us
    reduce_scatter x4, waiting for transfers between devices, scatter(): lax.psum_scatter(grad.astype(jnp.bfloat16), 'dp', scatter_dimension=0, ti...  87.5 us
    unnamed x138, local copies, waits for them, and re-layouts  23 us
    dot_general x1, matrix products, shards(): lax.dot_general(d_in, w_in, CONTRACT_COLUMNS, preferred_element_type=jnp....  20.4 us
    dot_general x1, matrix products, shards(): lax.dot_general(unit_one, d_in, CONTRACT_ROWS, preferred_element_type=jnp...  19.6 us
    dot_general x1, matrix products, shards(): projected = jnp.dot(unit_one, w_in, preferred_element_type=jnp.float32)  18.5 us
  transfers between devices with their start and end apart: 8, of which 2 were waited for; matrix products, arithmetic and copies ran while one was open for 29% of the time, Pallas kernels for 51%

profile of v1, /device:TPU:0, one launch (start us, length us, event | category | flops | bytes accessed | tf_op | source)
XLA Modules:
  0.0 868.8 jit_solution(5206489683802902944)
XLA Ops:
  19.7 72.9 %gather_one.1 = bf16[1024,2048]{1,0:T(8,128)(2,1)S(1)} custom-call(bf16[256,2048]{1,0:T(8,128)(2,1)S(1)} %fusion.29.refs_0_), custom_call_target="tpu_custom_call" | custom-call | bytes 125829120 | tf_op jit(solution)/shard_map/gather_one/pallas_call | solution.py:195
  92.6 2.1 copy-done.1
  94.9 4.6 broadcast_multiply_fusion.2
  100.9 18.5 %fusion.79 = (bf16[1024,3072]{1,0:T(8,128)(2,1)}, f32[1024,3072]{1,0:T(8,128)S(1)}) fusion(bf16[1024,2048]{1,0:T(8,128)(2,1)} %copy-done.1, bf16[2048,3072]{1,0:T(8,128)(2,1)} %all-gather.4.cloned.1.call-done), kind=kOutput, calls=%fused_computation.159 | convolution fusion | flops 12888047616 | bytes 35651584 | tf_op jit(solution)/shard_map/dot_general | solution.py:346
  120.6 3.4 copy-done.20
  124.8 2.1 slice.210
  126.9 3.5 slice.219
  132.1 2.0 copy.68
  134.2 3.5 multiply_convert_fusion.3
  137.7 2.9 fusion.31
  140.5 3.1 copy.69
  143.7 2.1 fusion.41
  146.6 2.6 mul.401
  149.2 5.5 copy.71
  154.7 2.6 sub.112
  157.2 5.5 copy.70
  162.8 7.9 multiply_convert_fusion.2
  170.7 8.5 all-gather.6.cloned.1.call-done
  179.2 9.5 %convolution_convert_fusion.5.refs_0_ = bf16[1024,2048]{1,0:T(8,128)(2,1)} fusion(bf16[1024,1024]{1,0:T(8,128)(2,1)} %multiply_convert_fusion.2, bf16[2048,4096]{1,0:T(8,128)(2,1)} %all-gather.6.cloned.1.call-done), kind=kOutput, calls=%fused_computation.48 | convolution fusion | flops 4297064448 | bytes 10485760 | tf_op jit(solution)/shard_map/dot_general | solution.py:382
  188.7 178.7 %residual.1 = (bf16[1024,2048]{1,0:T(8,128)(2,1)}, f32[256,2048]{1,0:T(8,128)S(1)}) custom-call(bf16[1024,2048]{1,0:T(8,128)(2,1)} %convolution_convert_fusion.5.refs_0_, bf16[256,2048]{1,0:T(8,128)(2,1)S(1)} %copy-done), custom_call_target="tpu_custom_call" | custom-call | bytes 125829120 | tf_op jit(solution)/shard_map/residual/pallas_call | solution.py:195
  367.4 14.5 %fusion.2 = f32[1024,2048]{1,0:T(8,128)} fusion(bf16[1024,2048]{1,0:T(8,128)(2,1)} %get-tuple-element.81, bf16[2048,4096]{1,0:T(8,128)(2,1)} %all-gather.6.cloned.1.call-done), kind=kOutput, calls=%fused_computation.4 | convolution fusion | flops 8589934592 | bytes 20971520 | tf_op jit(solution)/shard_map/dot_general | solution.py:388
  381.8 13.8 %fusion.10 = (bf16[1024,1024]{1,0:T(8,128)(2,1)}, bf16[1024,1024]{1,0:T(8,128)(2,1)}, bf16[1024,1024]{1,0:T(8,128)(2,1)S(1)}) fusion(f32[1024,2048]{1,0:T(8,128)} %fusion.2, bf16[1024,2048]{1,0:T(8,128)(2,1)} %all-gather.8.cloned.1.call-done, bf16[2048,4096]{1,0:T(8,128)(2,1)} %all-gather.6.cloned.1.call-done), kind=kOutput, calls=%fused_computation.17 | convolution fusion | flops 4322230272 | bytes 23068672 | tf_op jit(solution)/shard_map/dot_general | solution.py:400
  397.0 6.3 convert_bitcast_fusion
  403.3 14.7 %fusion.18.refs_0_ = bf16[1024,2048]{1,0:T(8,128)(2,1)} fusion(bf16[2048,4096]{1,0:T(8,128)(2,1)} %all-gather.6.cloned.1.call-done, bf16[1024,1024]{1,0:T(8,128)(2,1)} %get-tuple-element.101, bf16[1024,1024]{1,0:T(8,128)(2,1)} %get-tuple-element.100), kind=kOutput, calls=%fused_computation.45 | convolution fusion | flops 8600420352 | bytes 16777216 | tf_op jit(solution)/shard_map/dot_general | solution.py:411
  418.1 112.2 %d_residual.1 = (bf16[1024,2048]{1,0:T(8,128)(2,1)}, f32[256,2048]{1,0:T(8,128)S(1)}) custom-call(bf16[1024,2048]{1,0:T(8,128)(2,1)} %fusion.18.refs_0_, f32[256,2048]{1,0:T(8,128)S(1)} %get-tuple-element.80.refs_1_, bf16[256,2048]{1,0:T(8,128)(2,1)S(1)} %copy-done.2), custom_call_target="tpu_custom_call" | custom-call | bytes 125829120 | tf_op jit(solution)/shard_map/d_residual/pallas_call | solution.py:195
  531.8 8.4 convolution_convert_fusion.3
  540.2 9.4 %convolution_convert_fusion.4 = bf16[1024,2048]{1,0:T(8,128)(2,1)} fusion(bf16[1024,1024]{1,0:T(8,128)(2,1)} %copy-done.67, bf16[2048,4096]{1,0:T(8,128)(2,1)} %all-gather.6.cloned.1.call-done), kind=kOutput, calls=%fused_computation.47 | convolution fusion | flops 4297064448 | bytes 10485760 | tf_op jit(solution)/shard_map/dot_general | solution.py:392
  549.7 2.6 copy.52
  552.4 2.6 copy.53
  555.0 14.4 %convolution_convert_fusion.1 = bf16[2048,2048]{1,0:T(8,128)(2,1)} fusion(bf16[1024,2048]{1,0:T(8,128)(2,1)} %get-tuple-element.81, bf16[1024,1024]{1,0:T(8,128)(2,1)} %get-tuple-element.101, bf16[1024,1024]{1,0:T(8,128)(2,1)} %get-tuple-element.100), kind=kOutput, calls=%fused_computation.1 | convolution fusion | flops 8602517504 | bytes 16777216 | tf_op jit(solution)/shard_map/dot_general | solution.py:408
  569.5 13.4 %fusion.59 = (f32[1024,1024]{1,0:T(8,128)}, bf16[1024,1024]{1,0:T(8,128)(2,1)}) fusion(f32[1024,3072]{1,0:T(8,128)} %copy-done.20, f32[1024,1024]{1,0:T(8,128)} %copy.71, f32[1024,1024]{1,0:T(8,128)} %copy.70, f32[512,1024]{1,0:T(8,128)} %copy.69, f32[512,1024]{1,0:T(8,128)} %copy.68, bf16[1024,2048]{1,0:T(8,128)(2,1)} %get-tuple-element.82, ...), kind=kOutput, calls=%fused_computation.127 | convolution fusion | flops 4311744512 | bytes 31457280 | tf_op jit(solution)/shard_map/dot_general | solution.py:424
  582.9 5.3 copy.74
  588.2 4.8 multiply_reduce_fusion
  601.2 2.1 multiply_convert_fusion
  607.4 2.4 copy.72
  611.8 2.6 convolution_bitcast_fusion.1
  618.6 2.6 fusion.15
  621.2 3.9 copy.73
  625.1 19.6 %convolution_convert_fusion = bf16[2048,3072]{1,0:T(8,128)(2,1)} fusion(bf16[1024,2048]{1,0:T(8,128)(2,1)} %copy-done.1, bf16[1024,1024]{1,0:T(8,128)(2,1)} %get-tuple-element.99, bf16[1024,1024]{1,0:T(8,128)(2,1)} %copy.73, bf16[1024,512]{1,0:T(8,128)(2,1)} %copy.72, bf16[1024,512]{1,0:T(8,128)(2,1)} %bitcast.117), kind=kOutput, calls=%fused_computation | convolution fusion | flops 12916359168 | bytes 23068672 | tf_op jit(solution)/shard_map/dot_general | solution.py:476
  644.8 20.4 %convolution_convert_fusion.2.refs_0_ = bf16[1024,2048]{1,0:T(8,128)(2,1)} fusion(bf16[2048,3072]{1,0:T(8,128)(2,1)} %all-gather.4.cloned.1.call-done, bf16[1024,1024]{1,0:T(8,128)(2,1)} %get-tuple-element.99, bf16[1024,1024]{1,0:T(8,128)(2,1)} %copy.73, bf16[1024,512]{1,0:T(8,128)(2,1)} %copy.72, bf16[1024,512]{1,0:T(8,128)(2,1)} %bitcast.118), kind=kOutput, calls=%fused_computation.44 | convolution fusion | flops 12912164864 | bytes 23068672 | tf_op jit(solution)/shard_map/dot_general | solution.py:478
  666.8 77.6 %tokens_grad.1 = bf16[256,2048]{1,0:T(8,128)(2,1)S(1)} custom-call(bf16[1024,2048]{1,0:T(8,128)(2,1)} %convolution_convert_fusion.2.refs_0_, bf16[256,2048]{1,0:T(8,128)(2,1)S(1)} %copy-done, f32[256,2048]{1,0:T(8,128)S(1)} %copy-done.6), custom_call_target="tpu_custom_call" | custom-call | bytes 125829120 | tf_op jit(solution)/shard_map/tokens_grad/pallas_call | solution.py:195
  745.4 2.2 copy.57
  747.6 2.1 convert_element_type.216
  749.7 2.5 add_convert_fusion.3
  752.3 2.1 convert_multiply_fusion.2
  755.8 87.4 %reduce-scatter.8.cloned.1.call-done = bf16[256,3072]{1,0:T(8,128)(2,1)} async-done(((bf16[2048,3072]{1,0:T(8,128)(2,1)}), bf16[256,3072]{1,0:T(8,128)(2,1)}) %reduce-scatter.8.cloned.1.call-update) | async-done | bytes 1572880 | tf_op jit(solution)/shard_map/reduce_scatter | solution.py:330
  843.3 2.1 convert_multiply_fusion
  848.0 11.6 %all-reduce.6 = (f32[256]{0:T(256)S(1)}, f32[256]{0:T(256)S(1)}) all-reduce(f32[256]{0:T(256)S(1)} %get-tuple-element.122, f32[256]{0:T(256)S(1)} %get-tuple-element.124), channel_id=1, replica_groups=mesh['dp'=8,'tensor'=4] {'tensor'}, use_global_device_ids=true, to_apply=%region_8.9 | all-reduce | flops 512 | bytes 4096 | tf_op jit(solution)/shard_map/psum | solution.py:488
  (207 shorter events, 48.5 us)
Async XLA Ops:
  7.2 5.3 copy-start.60
  7.2 5.3 copy-start.49
  7.2 5.3 copy-start.48
  7.2 93.7 %all-gather.4.cloned.1.call-start = ((), (), s32[]{:S(2)}) async-start(), calls=%async_computation.5 | async-start | bytes 14155776 | tf_op jit(solution)/shard_map/all_gather | solution.py:324
  9.2 4.5 copy-start.50
  9.2 4.5 copy-start.51
  12.4 166.8 %all-gather.6.cloned.1.call-start = ((), (), s32[]{:S(2)}) async-start(), calls=%async_computation.6 | async-start | bytes 18874368 | tf_op jit(solution)/shard_map/all_gather | solution.py:324
  13.7 3.4 copy-start
  13.7 3.8 copy-start.54
  15.3 366.6 %all-gather.8.cloned.1.call-start = ((), (), s32[]{:S(2)}) async-start(), calls=%async_computation.8 | async-start | bytes 5242880 | tf_op jit(solution)/shard_map/all_gather | solution.py:345
  16.0 729.4 %reduce-scatter.14.cloned.1.call-start = ((), (), s32[]{:S(2)}) async-start(), calls=%async_computation.12 | async-start | bytes 4718592 | tf_op jit(solution)/shard_map/reduce_scatter | solution.py:330
  17.2 117.0 %copy-start.63 = (f32[2]{0:T(128)}, f32[2]{0:T(128)S(1)}, u32[]{:S(2)}) copy-start(f32[2]{0:T(128)S(1)} %subtract_log_fusion) | copy-start | bytes 28
  17.7 112.7 %copy-start.52 = (pred[512,512]{1,0:T(8,128)(4,1)}, pred[512,512]{1,0:T(8,128)(4,1)S(1)}, u32[]{:S(2)}) copy-start(pred[512,512]{1,0:T(8,128)(4,1)S(1)} %fusion.52) | copy-start | bytes 786436
  99.5 24.5 %copy-start.13 = (f32[1024,256]{1,0:T(8,128)}, f32[1024,256]{1,0:T(8,128)S(1)}, u32[]{:S(2)}) copy-start(f32[1024,256]{1,0:T(8,128)S(1)} %get-tuple-element.127) | copy-start | bytes 3145732
  99.5 24.5 %copy-start.15 = (f32[1024,256]{1,0:T(8,128)}, f32[1024,256]{1,0:T(8,128)S(1)}, u32[]{:S(2)}) copy-start(f32[1024,256]{1,0:T(8,128)S(1)} %get-tuple-element.128) | copy-start | bytes 3145732
  119.4 4.5 copy-start.20
  124.7 6.4 copy-start.19
  124.8 6.4 copy-start.29
  124.8 5.6 copy-start.45
  126.8 4.3 copy-start.32
  132.1 13.6 %copy-start.7 = (f32[2,512,512]{2,1,0:T(8,128)}, f32[2,512,512]{2,1,0:T(8,128)S(1)}, u32[]{:S(2)}) copy-start(f32[2,512,512]{2,1,0:T(8,128)S(1)} %fusion.46) | copy-start | bytes 6291460
  134.2 3.5 copy-start.43
  137.6 2.9 copy-start.65
  157.2 5.5 copy-start.17
  381.8 15.1 %copy-start.62 = (bf16[1024,2048]{1,0:T(8,128)(2,1)S(1)}, bf16[1024,2048]{1,0:T(8,128)(2,1)}, u32[]{:S(2)}) copy-start(bf16[1024,2048]{1,0:T(8,128)(2,1)} %all-gather.8.cloned.1.call-done) | copy-start | bytes 12582916
  403.3 344.3 %reduce-scatter.10.cloned.1.call-start = ((), (), s32[]{:S(2)}) async-start(), calls=%async_computation.10 | async-start | bytes 4718592 | tf_op jit(solution)/shard_map/reduce_scatter | solution.py:330
  403.3 14.8 %copy-start.2 = (bf16[256,2048]{1,0:T(8,128)(2,1)S(1)}, bf16[256,2048]{1,0:T(8,128)(2,1)}, u32[]{:S(2)}) copy-start(bf16[256,2048]{1,0:T(8,128)(2,1)} %refs_2_.1) | copy-start | bytes 3145732
  418.1 113.7 %copy-start.41 = (bf16[1024,1024]{1,0:T(8,128)(2,1)S(1)}, bf16[1024,1024]{1,0:T(8,128)(2,1)}, u32[]{:S(2)}) copy-start(bf16[1024,1024]{1,0:T(8,128)(2,1)} %multiply_convert_fusion.2) | copy-start | bytes 6291460
  540.2 209.5 %reduce-scatter.6.cloned.1.call-start = ((), (), s32[]{:S(2)}) async-start(), calls=%async_computation.7 | async-start | bytes 5242880 | tf_op jit(solution)/shard_map/reduce_scatter | solution.py:395
  549.7 202.6 %reduce-scatter.12.cloned.1.call-start = ((), (), s32[]{:S(2)}) async-start(), calls=%async_computation.11 | async-start | bytes 9437184 | tf_op jit(solution)/shard_map/reduce_scatter | solution.py:330
  569.4 273.9 %reduce-scatter.8.cloned.1.call-start = ((), (), s32[]{:S(2)}) async-start(), calls=%async_computation.9 | async-start | bytes 14155776 | tf_op jit(solution)/shard_map/reduce_scatter | solution.py:330
  588.2 4.8 copy-start.8
  588.2 4.8 copy-start.10
  588.2 6.1 copy-start.11
  597.0 2.7 copy-start.42
  597.0 4.1 copy-start.44
  597.0 4.2 copy-start.47
  598.9 4.4 copy-start.31
  609.9 4.5 copy-start.14
  745.4 6.9 copy-start.58
  752.2 91.1 %copy-start.24 = (bf16[256,1024]{1,0:T(8,128)(2,1)S(1)}, bf16[256,1024]{1,0:T(8,128)(2,1)}, u32[]{:S(2)}) copy-start(bf16[256,1024]{1,0:T(8,128)(2,1)} %copy-done.23) | copy-start | bytes 1572868
  752.2 91.1 %copy-start.26 = (bf16[256,1024]{1,0:T(8,128)(2,1)S(1)}, bf16[256,1024]{1,0:T(8,128)(2,1)}, u32[]{:S(2)}) copy-start(bf16[256,1024]{1,0:T(8,128)(2,1)} %copy-done.25) | copy-start | bytes 1572868
  752.2 91.1 %copy-start.38 = (bf16[256,512]{1,0:T(8,128)(2,1)S(1)}, bf16[256,512]{1,0:T(8,128)(2,1)}, u32[]{:S(2)}) copy-start(bf16[256,512]{1,0:T(8,128)(2,1)} %copy-done.37) | copy-start | bytes 786436
  752.2 91.1 %copy-start.40 = (bf16[256,512]{1,0:T(8,128)(2,1)S(1)}, bf16[256,512]{1,0:T(8,128)(2,1)}, u32[]{:S(2)}) copy-start(bf16[256,512]{1,0:T(8,128)(2,1)} %copy-done.39) | copy-start | bytes 786436
  752.2 91.1 %copy-start.56 = (f32[256]{0:T(256)S(1)}, f32[256]{0:T(256)}, u32[]{:S(2)}) copy-start(f32[256]{0:T(256)} %copy-done.55) | copy-start | bytes 3076
  845.5 14.2 %copy-start.59 = (bf16[256]{0:T(256)(128)(2,1)S(1)}, bf16[256]{0:T(256)(128)(2,1)}, u32[]{:S(2)}) copy-start(bf16[256]{0:T(256)(128)(2,1)} %param.27) | copy-start | bytes 1540
  845.5 14.7 %copy-start.61 = (bf16[256]{0:T(256)(128)(2,1)S(1)}, bf16[256]{0:T(256)(128)(2,1)}, u32[]{:S(2)}) copy-start(bf16[256]{0:T(256)(128)(2,1)} %param.33) | copy-start | bytes 1540
  845.5 15.3 %copy-start.4 = (bf16[256,2048]{1,0:T(8,128)(2,1)S(1)}, bf16[256,2048]{1,0:T(8,128)(2,1)}, u32[]{:S(2)}) copy-start(bf16[256,2048]{1,0:T(8,128)(2,1)} %copy-done.3) | copy-start | bytes 3145732
  (28 other events, 44.7 us)
Sparse Core Ops, SparseCore 0:
  12.5 74.8 all-gather.3
  89.3 89.8 all-gather.5
  180.8 139.7 all-gather.7
  403.4 51.0 reduce-scatter.13
  540.3 51.2 reduce-scatter.9
  593.7 76.7 reduce-scatter.5
  674.3 72.9 reduce-scatter.11
  750.9 92.3 reduce-scatter.7

commit v2 on v1

v2 whole, which is shorter than its diff:
```python
import functools
import jax
import jax.numpy as jnp
import numpy as np
from jax import lax
from jax.experimental import pallas as pl
from jax.experimental.pallas import tpu as pltpu
from jax.sharding import PartitionSpec as P

AXIS = "tensor"


def line_body(n, chunks, rs, ag, middle, n_in, n_out, *refs):
    ins, outs, scratch = refs[:n_in], refs[n_in : n_in + n_out], list(refs[n_in + n_out :])
    me = lax.axis_index(AXIS)
    last = n - 1
    lag = last if rs else 0
    if rs:
        part, ins = ins[0], ins[1:]
        up_buf, dn_buf, total, up_send, up_recv, dn_send, dn_recv = scratch[:7]
        scratch = scratch[7:]
        rows = up_buf.shape[1]
    if ag:
        full, outs = outs[0], outs[1:]
        own, ag_recv, ag_up, ag_dn, ag_here = scratch[:5]
        rows = own.shape[0]
    size = rows // chunks

    def cut(c, base=0):
        return pl.ds(pl.multiple_of(base + c * size, size), size)

    def send(src, dst, send_sem, recv_sem, to):
        return pltpu.make_async_remote_copy(
            src_ref=src,
            dst_ref=dst,
            send_sem=send_sem,
            recv_sem=recv_sem,
            device_id={AXIS: to},
            device_id_type=pl.DeviceIdType.MESH,
        )

    barrier = pltpu.get_barrier_semaphore()

    @pl.when(me > 0)
    def _():
        pl.semaphore_signal(barrier, inc=1, device_id={AXIS: me - 1}, device_id_type=pl.DeviceIdType.MESH)

    @pl.when(me < last)
    def _():
        pl.semaphore_signal(barrier, inc=1, device_id={AXIS: me + 1}, device_id_type=pl.DeviceIdType.MESH)

    pl.semaphore_wait(barrier, jnp.where((me > 0) & (me < last), 2, 1))

    def sum_copy(up, d, c):
        buf, s, r, to = (up_buf, up_send, up_recv, me + 1) if up else (dn_buf, dn_send, dn_recv, me - 1)
        ref = buf.at[d, cut(c)]
        return send(ref, ref, s.at[d, c], r.at[d, c], to)

    def sum_step(up, d, c):
        buf = up_buf if up else dn_buf
        first = 0 if up else last
        mine = part[cut(c, d * rows)]

        @pl.when(me == first)
        def _():
            buf[d, cut(c)] = mine

        @pl.when(me != first)
        def _():
            sum_copy(up, d, c).wait_recv()
            buf[d, cut(c)] = (buf[d, cut(c)].astype(jnp.float32) + mine.astype(jnp.float32)).astype(buf.dtype)

        sum_copy(up, d, c).start()

    def gather_copy(up, j, c, from_own=False):
        ref = full.at[cut(c, j * rows)]
        src = own.at[cut(c)] if from_own else ref
        return send(src, ref, (ag_up if up else ag_dn).at[j, c], ag_recv.at[j, c], me + 1 if up else me - 1)

    def here_copy(c):
        return pltpu.make_async_copy(own.at[cut(c)], full.at[cut(c, me * rows)], ag_here.at[c])

    def step(s, _):
        if rs:
            for up in (True, False):
                c = s - me if up else s - (last - me)
                for d in range(last, 0, -1) if up else range(last):

                    @pl.when((c >= 0) & (c < chunks) & ((me < d) if up else (me > d)))
                    def _(up=up, c=c, d=d):
                        sum_step(up, d, c)

        c_own = s - lag

        @pl.when((c_own >= 0) & (c_own < chunks))
        def _():
            c = c_own
            if rs:
                total[...] = part[cut(c, me * rows)].astype(jnp.float32)

                @pl.when(me > 0)
                def _():
                    sum_copy(True, me, c).wait_recv()
                    total[...] += up_buf[me, cut(c)].astype(jnp.float32)

                @pl.when(me < last)
                def _():
                    sum_copy(False, me, c).wait_recv()
                    total[...] += dn_buf[me, cut(c)].astype(jnp.float32)

                result = middle(cut(c), total[...], ins, outs)
            else:
                result = middle(cut(c), None, ins, outs)
            if ag:
                own[cut(c)] = result.astype(own.dtype)
                here_copy(c).start()

                @pl.when(me < last)
                def _():
                    gather_copy(True, me, c, True).start()

                @pl.when(me > 0)
                def _():
                    gather_copy(False, me, c, True).start()

        if ag:
            for t in range(1, last):
                c = s - lag - t
                for up in (True, False):
                    j = me - t if up else me + t

                    @pl.when((c >= 0) & (c < chunks) & (((j >= 0) & (me < last)) if up else ((j <= last) & (me > 0))))
                    def _(up=up, c=c, j=j):
                        gather_copy(up, j, c).wait_recv()
                        gather_copy(up, j, c).start()

        return 0

    lax.fori_loop(0, chunks + lag + (last - 1 if ag else 0), step, 0)

    def drain(c, _):
        if rs:
            for d in range(n):

                @pl.when(me < d)
                def _(d=d):
                    sum_copy(True, d, c).wait_send()

                @pl.when(me > d)
                def _(d=d):
                    sum_copy(False, d, c).wait_send()

        if ag:
            here_copy(c).wait()
            for j in range(n):

                @pl.when(((me == last) & (j < me)) | ((me == 0) & (j > me)))
                def _(j=j):
                    gather_copy(True, j, c).wait_recv()

                @pl.when((me < last) & (j <= me))
                def _(j=j):
                    gather_copy(True, j, c).wait_send()

                @pl.when((me > 0) & (j >= me))
                def _(j=j):
                    gather_copy(False, j, c).wait_send()

        return 0

    lax.fori_loop(0, chunks, drain, 0)


def line_pass(name, part, extras, extra_outs, middle, ag, chunks, collective_id, rows, width):
    n = lax.axis_size(AXIS)
    rs = part is not None
    size = rows // chunks
    vmem = pl.BlockSpec(memory_space=pltpu.VMEM)
    scratch = []
    sems = pltpu.SemaphoreType.DMA((n, chunks))
    if rs:
        scratch += [
            pltpu.VMEM((n, rows, width), jnp.bfloat16),
            pltpu.VMEM((n, rows, width), jnp.bfloat16),
            pltpu.VMEM((size, width), jnp.float32),
            sems, sems, sems, sems,
        ]
    if ag:
        scratch += [pltpu.VMEM((rows, width), jnp.bfloat16), sems, sems, sems, pltpu.SemaphoreType.DMA((chunks,))]
    operands = ([part] if rs else []) + list(extras)
    shapes = ([jax.ShapeDtypeStruct((n * rows, width), jnp.bfloat16)] if ag else []) + [
        jax.ShapeDtypeStruct((rows, width), kind) for kind in extra_outs
    ]
    specs = ([pl.BlockSpec(memory_space=pl.ANY)] if ag else []) + [vmem] * len(extra_outs)
    moved = rows * width * 2 * (n - 1)
    return pl.pallas_call(
        functools.partial(line_body, n, chunks, rs, ag, middle, len(operands), len(shapes)),
        out_shape=shapes,
        in_specs=[vmem] * len(operands),
        out_specs=specs,
        scratch_shapes=scratch,
        compiler_params=pltpu.CompilerParams(
            collective_id=collective_id, has_side_effects=True, vmem_limit_bytes=48 * 1024 * 1024
        ),
        cost_estimate=pl.CostEstimate(
            flops=0, bytes_accessed=moved * 40, transcendentals=0, remote_bytes_transferred=moved
        ),
        name=name,
    )(*operands)


HEADS = 8
KD = 256
VD = 512
ROWS = 256


EPS_NORM = 1e-06
EPS_GROUP = 1.0
CONTRACT_ROWS = (((0,), (0,)), ((), ()))
CONTRACT_COLUMNS = (((1,), (1,)), ((), ()))


def rotary_tables(length):
    positions = np.arange(length).astype(np.float32)[:, None]
    frequency = np.float32(10000.0) ** (-np.arange(KD // 2).astype(np.float32) * np.float32(2.0 / KD))
    angles = (positions * frequency[None, :]).astype(np.float32).astype(np.float64)
    return np.cos(angles).astype(np.float32), np.sin(angles).astype(np.float32)


def turn(rows, cosine, sine):
    low, high = rows[:, : KD // 2], rows[:, KD // 2 :]
    return jnp.concatenate([low * cosine - high * sine, high * cosine + low * sine], axis=1)


def dot(left, right, dims=(((1,), (0,)), ((), ()))):
    return lax.dot_general(left, right, dims, preferred_element_type=jnp.float32)


def head_decay(decay_ref, log_ref, head, reach):
    ahead = lax.broadcasted_iota(jnp.int32, decay_ref.shape, 0) - lax.broadcasted_iota(jnp.int32, decay_ref.shape, 1)
    distance = ahead + reach
    value = jnp.exp(log_ref[head] * jnp.maximum(distance, 0).astype(jnp.float32))
    decay_ref[...] = jnp.where(distance >= 0, value, 0.0)


def normed_heads(heads_out):
    centred = heads_out - jnp.mean(heads_out, axis=-1, keepdims=True)
    inverse = lax.rsqrt(jnp.mean(centred * centred, axis=-1, keepdims=True) + EPS_GROUP)
    return centred * inverse, inverse


def retention_body(block, reach, log_ref, proj, cosine, sine, seg_rows, seg_line, kept, mixed, keys, vals, decay):
    head, row = pl.program_id(0), pl.program_id(1)
    here = pl.ds(pl.multiple_of(reach + row * block, block), block)
    window = pl.ds(pl.multiple_of(row * block, block), reach + block)

    @pl.when(row == 0)
    def _():
        head_decay(decay, log_ref, head, reach)
        keys[:reach] = jnp.zeros((reach, KD), keys.dtype)
        vals[:reach] = jnp.zeros((reach, VD), vals.dtype)

    query = turn(proj[:, :KD], cosine[...], sine[...]).astype(jnp.bfloat16)
    key = (turn(proj[:, KD : 2 * KD], cosine[...], sine[...]) * KD ** (-0.5)).astype(jnp.bfloat16)
    value = proj[:, 2 * KD : 2 * KD + VD].astype(jnp.bfloat16)
    keys[here] = key
    vals[here] = value
    kept[:, :KD] = query
    kept[:, KD : 2 * KD] = key
    kept[:, 2 * KD :] = value
    weight = jnp.where(seg_rows[...] == seg_line[:, window], decay[...], 0.0)
    probs = (dot(query, keys[window], CONTRACT_COLUMNS) * weight).astype(jnp.bfloat16)
    normed, _ = normed_heads(dot(probs, vals[window]))
    mixed[...] = (jax.nn.silu(proj[:, 2 * KD + VD :]) * normed).astype(jnp.bfloat16)


def retention_pull_body(
    block, reach, log_ref, kept, gate, d_mixed, cosine, sine, seg_rows, seg_line, d_in, keys, vals, d_keys, d_vals, decay
):
    head, row = pl.program_id(0), pl.num_programs(1) - 1 - pl.program_id(1)
    mine = pl.ds(pl.multiple_of(row * block, block), block)
    here = pl.ds(pl.multiple_of(reach + row * block, block), block)
    window = pl.ds(pl.multiple_of(row * block, block), reach + block)

    @pl.when(pl.program_id(1) == 0)
    def _():
        head_decay(decay, log_ref, head, reach)
        keys[:reach] = jnp.zeros((reach, KD), keys.dtype)
        vals[:reach] = jnp.zeros((reach, VD), vals.dtype)
        keys[reach:] = kept[:, KD : 2 * KD]
        vals[reach:] = kept[:, 2 * KD :]
        d_keys[...] = jnp.zeros_like(d_keys)
        d_vals[...] = jnp.zeros_like(d_vals)

    query = kept[mine, :KD]
    weight = jnp.where(seg_rows[...] == seg_line[:, window], decay[...], 0.0)
    probs = (dot(query, keys[window], CONTRACT_COLUMNS) * weight).astype(jnp.bfloat16)
    normed, inverse = normed_heads(dot(probs, vals[window]))
    gate_pre, upstream = gate[...], d_mixed[...]
    opened = jax.nn.sigmoid(gate_pre)
    silu = gate_pre * opened
    d_in[:, 2 * KD + VD :] = (upstream * normed * (opened + silu * (1.0 - opened))).astype(jnp.bfloat16)
    e = upstream * silu
    d_heads = e - jnp.mean(e, axis=-1, keepdims=True) - normed * jnp.mean(e * normed, axis=-1, keepdims=True)
    d_heads = (d_heads * inverse).astype(jnp.bfloat16)
    d_scores = (dot(d_heads, vals[window], CONTRACT_COLUMNS) * weight).astype(jnp.bfloat16)
    d_vals[window] += dot(probs, d_heads, CONTRACT_ROWS)
    d_keys[window] += dot(d_scores, query, CONTRACT_ROWS)
    d_query = dot(d_scores, keys[window])
    d_in[:, :KD] = turn(d_query, cosine[...], -sine[...]).astype(jnp.bfloat16)
    d_in[:, KD : 2 * KD] = (turn(d_keys[here], cosine[...], -sine[...]) * KD ** (-0.5)).astype(jnp.bfloat16)
    d_in[:, 2 * KD : 2 * KD + VD] = d_vals[here].astype(jnp.bfloat16)


def retention_inputs(segments, heads):
    length = segments.shape[0]
    block = min(ROWS, length // 2)
    reach = length // 2
    head_ids = lax.axis_index("tensor") * heads + jnp.arange(heads)
    log_decay = jnp.log(1.0 - 2.0 ** (-5.0 - head_ids.astype(jnp.float32)))
    seg_line = jnp.concatenate([jnp.full((reach,), -1, jnp.int32), segments])[None, :]
    return block, reach, log_decay, segments[:, None], seg_line


def retention(projected, segments, heads):
    length = projected.shape[0]
    block, reach, log_decay, seg_rows, seg_line = retention_inputs(segments, heads)
    cosine, sine = rotary_tables(length)
    per_head = projected.shape[1] // heads
    table = pl.BlockSpec((block, KD // 2), lambda h, r: (r, 0))
    return pl.pallas_call(
        functools.partial(retention_body, block, reach),
        grid=(heads, length // block),
        in_specs=[
            pl.BlockSpec(memory_space=pltpu.SMEM),
            pl.BlockSpec((block, per_head), lambda h, r: (r, h)),
            table,
            table,
            pl.BlockSpec((block, 1), lambda h, r: (r, 0)),
            pl.BlockSpec(seg_line.shape, lambda h, r: (0, 0)),
        ],
        out_specs=[
            pl.BlockSpec((block, 2 * KD + VD), lambda h, r: (r, h)),
            pl.BlockSpec((block, VD), lambda h, r: (r, h)),
        ],
        out_shape=[
            jax.ShapeDtypeStruct((length, heads * (2 * KD + VD)), jnp.bfloat16),
            jax.ShapeDtypeStruct((length, heads * VD), jnp.bfloat16),
        ],
        scratch_shapes=[
            pltpu.VMEM((reach + length, KD), jnp.bfloat16),
            pltpu.VMEM((reach + length, VD), jnp.bfloat16),
            pltpu.VMEM((block, reach + block), jnp.float32),
        ],
        compiler_params=pltpu.CompilerParams(vmem_limit_bytes=48 * 1024 * 1024),
        cost_estimate=pl.CostEstimate(
            flops=heads * length * (reach + block) * (KD + VD) * 2, bytes_accessed=projected.size * 6, transcendentals=0
        ),
        name="retention",
    )(log_decay, projected, cosine, sine, seg_rows, seg_line)


def retention_pull(kept, projected, d_mixed, segments, heads):
    length = kept.shape[0]
    block, reach, log_decay, seg_rows, seg_line = retention_inputs(segments, heads)
    cosine, sine = rotary_tables(length)
    per_head = projected.shape[1] // heads
    last = length // block - 1
    gate_block = per_head // VD
    table = pl.BlockSpec((block, KD // 2), lambda h, r: (last - r, 0))
    return pl.pallas_call(
        functools.partial(retention_pull_body, block, reach),
        grid=(heads, last + 1),
        in_specs=[
            pl.BlockSpec(memory_space=pltpu.SMEM),
            pl.BlockSpec((length, 2 * KD + VD), lambda h, r: (0, h)),
            pl.BlockSpec((block, VD), lambda h, r: (last - r, gate_block * h + gate_block - 1)),
            pl.BlockSpec((block, VD), lambda h, r: (last - r, h)),
            table,
            table,
            pl.BlockSpec((block, 1), lambda h, r: (last - r, 0)),
            pl.BlockSpec(seg_line.shape, lambda h, r: (0, 0)),
        ],
        out_specs=pl.BlockSpec((block, per_head), lambda h, r: (last - r, h)),
        out_shape=jax.ShapeDtypeStruct(projected.shape, jnp.bfloat16),
        scratch_shapes=[
            pltpu.VMEM((reach + length, KD), jnp.bfloat16),
            pltpu.VMEM((reach + length, VD), jnp.bfloat16),
            pltpu.VMEM((reach + length, KD), jnp.float32),
            pltpu.VMEM((reach + length, VD), jnp.float32),
            pltpu.VMEM((block, reach + block), jnp.float32),
        ],
        compiler_params=pltpu.CompilerParams(vmem_limit_bytes=48 * 1024 * 1024),
        cost_estimate=pl.CostEstimate(
            flops=heads * length * (reach + block) * (3 * KD + 3 * VD) * 2, bytes_accessed=projected.size * 8, transcendentals=0
        ),
        name="retention_pull",
    )(log_decay, kept, projected, d_mixed, cosine, sine, seg_rows, seg_line)


def inverse_rms(rows):
    return lax.rsqrt(jnp.mean(rows * rows, axis=-1, keepdims=True) + EPS_NORM)


def norm_pull(unit, inverse, d_unit):
    return inverse * (d_unit - unit * jnp.mean(d_unit * unit, axis=-1, keepdims=True))


def residual_step(cut, summed, ins, outs):
    residual = ins[0][cut].astype(jnp.float32) + summed
    outs[0][cut] = residual
    return residual * inverse_rms(residual)


def d_residual_step(cut, summed, ins, outs):
    residual = ins[0][cut]
    inverse = inverse_rms(residual)
    d_residual = ins[1][cut].astype(jnp.float32) + norm_pull(residual * inverse, inverse, summed)
    outs[0][cut] = d_residual
    return d_residual


def tokens_step(cut, summed, ins, outs):
    inputs = ins[0][cut].astype(jnp.float32)
    inverse = inverse_rms(inputs)
    grad = ins[1][cut] + norm_pull(inputs * inverse, inverse, summed)
    outs[0][cut] = grad.astype(outs[0].dtype)


def hops(up):
    n = lax.axis_size(AXIS)
    return [(i, i + 1) if up else (i + 1, i) for i in range(n - 1)]


def steps_of(part, parts):
    n = lax.axis_size(AXIS)
    return range((n - 1) * part // parts, (n - 1) * (part + 1) // parts)


def gather_start(own):
    n, me = lax.axis_size(AXIS), lax.axis_index(AXIS)
    rows = own.shape[0]
    full = jnp.zeros(((n + 1) * rows,) + own.shape[1:], own.dtype)
    return own, own, lax.dynamic_update_slice_in_dim(full, own, me * rows, 0)


def gather_steps(state, steps):
    n, me = lax.axis_size(AXIS), lax.axis_index(AXIS)
    up, down, full = state
    rows = up.shape[0]
    for t in steps:
        up, down = lax.ppermute(up, AXIS, hops(True)), lax.ppermute(down, AXIS, hops(False))
        for arrived, j in ((up, me - t - 1), (down, me + t + 1)):
            full = lax.dynamic_update_slice_in_dim(full, arrived, jnp.where((j >= 0) & (j < n), j, n) * rows, 0)
    return up, down, full


def scatter_rows(part, j):
    n = lax.axis_size(AXIS)
    rows = part.shape[0] // n
    return lax.dynamic_slice_in_dim(part, jnp.clip(j, 0, n - 1) * rows, rows, 0).astype(jnp.float32)


def scatter_steps(state, part, steps):
    n, me = lax.axis_size(AXIS), lax.axis_index(AXIS)
    for t in steps:
        mine = scatter_rows(part, me + n - 1 - t), scatter_rows(part, me - n + 1 + t)
        if t:
            mine = [rows + sums.astype(jnp.float32) for rows, sums in zip(mine, state)]
        state = tuple(
            lax.ppermute(sums.astype(part.dtype), AXIS, hops(way)) for sums, way in zip(mine, (True, False))
        )
    return state


def shards(tokens,
    segment_ids,
    attn_gain,
    w_query,
    w_key,
    w_value,
    w_gate,
    w_out,
    mlp_gain,
    w_mlp_gate,
    w_mlp_up,
    w_down,
    cotangent,
):
    local_rows, width = tokens.shape
    heads = HEADS // lax.axis_size(AXIS)
    hidden_cols = w_mlp_gate.shape[1]
    segments = segment_ids[0]
    gain_one = attn_gain.astype(jnp.float32)[:, None]
    gain_two = mlp_gain.astype(jnp.float32)[:, None]
    after = lax.optimization_barrier

    def gather(own):
        return lax.all_gather(own, "dp", axis=0, tiled=True)

    def scaled(gain, weight):
        return (weight.astype(jnp.float32) * gain).astype(jnp.bfloat16)

    def scatter(grad):
        return lax.psum_scatter(grad, "dp", scatter_dimension=0, tiled=True)

    def by_head(query, key, value, gate):
        parts = []
        for head in range(heads):
            for array, columns in ((query, KD), (key, KD), (value, VD), (gate, VD)):
                parts.append(array[:, head * columns : (head + 1) * columns])
        return jnp.concatenate(parts, axis=1)

    def from_heads(array):
        found, at = ([], [], [], []), 0
        for _ in range(heads):
            for where, columns in zip(found, (KD, KD, VD, VD)):
                where.append(array[:, at : at + columns])
                at += columns
        return [jnp.concatenate(parts, axis=1) for parts in found]

    w_in_own = by_head(*[scaled(gain_one, w) for w in (w_query, w_key, w_value, w_gate)])
    w_pair_own = jnp.concatenate([scaled(gain_two, w) for w in (w_mlp_gate, w_mlp_up)], axis=1)
    mlp_own = jnp.concatenate([w_pair_own, w_down], axis=1)
    inputs = tokens.astype(jnp.float32)
    unit_own = (inputs * inverse_rms(inputs)).astype(jnp.bfloat16)
    w_in = gather(w_in_own)
    (unit_one,) = line_pass(
        "gather_one", None, [unit_own], [], lambda cut, _, ins, outs: ins[0][cut], True, 4, 0, local_rows, width
    )
    w_in, unit_one, w_out, cot_own = after((w_in, unit_one, w_out, cotangent))
    out_full = gather(w_out)
    cot = gather_steps(gather_start(cot_own), steps_of(0, 3))
    projected = dot(unit_one, w_in)
    projected, *cot = after((projected, *cot))
    cot = gather_steps(cot, steps_of(1, 3))
    kept, mixed = retention(projected, segments, heads)
    part_out = dot(mixed, out_full, CONTRACT_COLUMNS).astype(jnp.bfloat16)
    part_out, mlp_own, *cot = after((part_out, mlp_own, *cot))
    mlp_full = gather(mlp_own)
    unit_two, residual = line_pass(
        "residual", part_out, [tokens], [jnp.float32], residual_step, True, 16, 1, local_rows, width
    )
    unit_two, mlp_full, *cot = after((unit_two, mlp_full, *cot))
    w_pair, down_full = mlp_full[:, : 2 * hidden_cols], mlp_full[:, 2 * hidden_cols :]

    cot = gather_steps(cot, steps_of(2, 3))
    both_hidden = dot(unit_two, w_pair)
    hidden_gate, hidden_up = both_hidden[:, :hidden_cols], both_hidden[:, hidden_cols:]
    hidden = (jax.nn.gelu(hidden_gate, approximate=True) * hidden_up).astype(jnp.bfloat16)
    part_down = dot(hidden, down_full, CONTRACT_COLUMNS).astype(jnp.bfloat16)
    part_down, cot_full = after((part_down, cot[2]))
    cot_full = cot_full[: unit_two.shape[0]]

    sums = scatter_steps(None, part_down, steps_of(0, 3))
    grad_down = dot(cot_full, hidden, CONTRACT_ROWS).astype(jnp.bfloat16)
    d_hidden = dot(cot_full, down_full)
    _, gelu_pull = jax.vjp(
        lambda gate_part, up_part: jax.nn.gelu(gate_part, approximate=True) * up_part,
        hidden_gate,
        hidden_up,
    )
    d_pair = jnp.concatenate(gelu_pull(d_hidden), axis=1).astype(jnp.bfloat16)
    d_pair, grad_down, *sums = after((d_pair, grad_down, *sums))
    sums = scatter_steps(sums, part_down, steps_of(1, 3))
    grad_pair = dot(unit_two, d_pair, CONTRACT_ROWS).astype(jnp.bfloat16)
    part_pair = dot(d_pair, w_pair, CONTRACT_COLUMNS).astype(jnp.bfloat16)
    part_pair, grad_pair, grad_down, *sums = after((part_pair, grad_pair, grad_down, *sums))
    pair_grad = scatter(grad_pair)
    d_branch_one, d_residual = line_pass(
        "d_residual", part_pair, [residual, cotangent], [jnp.float32], d_residual_step, True, 16, 2, local_rows, width
    )
    d_branch_one, d_residual, pair_grad, grad_down, *sums = after((d_branch_one, d_residual, pair_grad, grad_down, *sums))

    down_grad = scatter(grad_down)
    sums = scatter_steps(sums, part_down, steps_of(2, 3))
    grad_out = dot(d_branch_one, mixed, CONTRACT_ROWS).astype(jnp.bfloat16)
    out_grad = scatter(grad_out)
    d_mixed = dot(d_branch_one, out_full)
    d_in = retention_pull(kept, projected, d_mixed, segments, heads)
    grad_in = dot(unit_one, d_in, CONTRACT_ROWS).astype(jnp.bfloat16)
    result = residual + sum(sums_in.astype(jnp.float32) for sums_in in sums) + scatter_rows(part_down, lax.axis_index(AXIS))
    result = result.astype(jnp.bfloat16)
    d_in, grad_in, result = after((d_in, grad_in, result))
    in_grad = scatter(grad_in)
    part_in = dot(d_in, w_in, CONTRACT_COLUMNS).astype(jnp.bfloat16)
    (tokens_grad,) = line_pass(
        "tokens_grad", part_in, [tokens, d_residual], [jnp.bfloat16], tokens_step, False, 8, 3, local_rows, width
    )

    def gain_terms(weights, grads):
        return jnp.sum(weights.astype(jnp.float32) * grads.astype(jnp.float32), axis=1)

    gain_sums = lax.psum((gain_terms(w_in_own, in_grad), gain_terms(w_pair_own, pair_grad)), AXIS)
    in_grads = [grad.astype(jnp.float32) * gain_one for grad in from_heads(in_grad)]
    pair_grad = pair_grad.astype(jnp.float32) * gain_two
    return (
        result,
        tokens_grad,
        gain_sums[0] / gain_one[:, 0],
        *in_grads,
        out_grad.astype(jnp.float32),
        gain_sums[1] / gain_two[:, 0],
        pair_grad[:, :hidden_cols],
        pair_grad[:, hidden_cols:],
        down_grad.astype(jnp.float32),
    )


def solution(mesh):
    return jax.shard_map(
        shards,
        mesh=mesh,
        in_specs=(
            P(("dp", "tensor"), None),
            P("dp", None),
            P("dp"),
            P("dp", "tensor"),
            P("dp", "tensor"),
            P("dp", "tensor"),
            P("dp", "tensor"),
            P("dp", "tensor"),
            P("dp"),
            P("dp", "tensor"),
            P("dp", "tensor"),
            P("dp", "tensor"),
            P(("dp", "tensor"), None),
        ),
        out_specs=(
            P(("dp", "tensor"), None),
            P(("dp", "tensor"), None),
            P("dp"),
            P("dp", "tensor"),
            P("dp", "tensor"),
            P("dp", "tensor"),
            P("dp", "tensor"),
            P("dp", "tensor"),
            P("dp"),
            P("dp", "tensor"),
            P("dp", "tensor"),
            P("dp", "tensor"),
        ),
        check_vma=False,
    )
```

time: 873 us -> 732 us (0.84)
  waiting for transfers between devices: 96.8 us -> 48.3 us
  Pallas kernels: 441 us -> 395 us
  local copies, waits for them, and re-layouts: 72.8 us -> 30.6 us
  starting transfers between devices: 0.33 us -> 33.7 us
  matrix products: 183 us -> 150 us
  other arithmetic: 47.7 us -> 38.9 us
    pallas_call x4, Pallas kernels: 441 us -> 365 us  [line_pass(): pl.pallas_call(functools.partial(line_body, n, chunks, rs, ag, middle, le...]
    reduce_scatter x5 -> x4, waiting for transfers between devices: 87.5 us -> 36.7 us  [scatter(): return lax.psum_scatter(grad, 'dp', scatter_dimension=0, tiled=True)]
    ppermute x0 -> x12, starting transfers between devices: none -> 33.4 us  [the longest x6 19.4 us: scatter_steps(): lax.ppermute(sums.astype(part.dtype), AXIS, hops(way))]
    dot_general x24 -> x12, matrix products: 183 us -> 150 us  [dot(): lax.dot_general(left, right, dims, preferred_element_type=jnp.float32)]
    pallas_call x0 -> x2, Pallas kernels: none -> 29.8 us  [the longest x1 18.5 us: retention_pull(): pl.pallas_call(functools.partial(retention_pull_body, block, reach), grid...]
    mul x4 -> x0, local copies, waits for them, and re-layouts: 13.4 us -> none  [the longest x2 8.08 us: gated_norm(): normed = centred * lax.rsqrt(variance + EPS_GROUP)]
    reshape x6 -> x0, local copies, waits for them, and re-layouts: 13.1 us -> none  [the longest x1 5.34 us: gated_norm(): return jax.nn.silu(gate_pre) * normed.reshape(gate_pre.shape)]
    dynamic_update_slice x0 -> x7, local copies, waits for them, and re-layouts: none -> 11.8 us  [the longest x6 10.8 us: gather_steps(): lax.dynamic_update_slice_in_dim(full, arrived, jnp.where((j >= 0) & (j <...]
  transfers between devices with their start and end apart: 8 -> 19, of which waited for: 2 -> 5; matrix products, arithmetic and copies ran while one was open for 29% -> 23% of each run, Pallas kernels for 51% -> 55%
where the time goes in v2:
time: 732 us; the launch traced here: 723 us
  Pallas kernels  395 us (54%)
  matrix products  150 us (20%)
  waiting for transfers between devices  48.3 us (7%)
  other arithmetic  38.9 us (5%)
  starting transfers between devices  33.7 us (5%)
  local copies, waits for them, and re-layouts  30.6 us (4%)
  between operations  15 us (2%)
  blocking collectives  11.7 us (2%)
    pallas_call x4, Pallas kernels, line_pass(): pl.pallas_call(functools.partial(line_body, n, chunks, rs, ag, middle, le...  365 us
    dot_general x12, matrix products, dot(): lax.dot_general(left, right, dims, preferred_element_type=jnp.float32)  150 us
    reduce_scatter x4, waiting for transfers between devices, scatter(): return lax.psum_scatter(grad, 'dp', scatter_dimension=0, tiled=True)  36.7 us
    ppermute x6, starting transfers between devices, scatter_steps(): lax.ppermute(sums.astype(part.dtype), AXIS, hops(way))  19.4 us
    pallas_call x1, Pallas kernels, retention_pull(): pl.pallas_call(functools.partial(retention_pull_body, block, reach), grid...  18.5 us
  transfers between devices with their start and end apart: 19, of which 5 were waited for; matrix products, arithmetic and copies ran while one was open for 23% of the time, Pallas kernels for 55%

profile of v2, /device:TPU:0, one launch (start us, length us, event | category | flops | bytes accessed | tf_op | source)
XLA Modules:
  0.0 722.6 jit_solution(1938181014701503687)
XLA Ops:
  12.6 73.0 %gather_one.1 = bf16[1024,2048]{1,0:T(8,128)(2,1)S(1)} custom-call(bf16[256,2048]{1,0:T(8,128)(2,1)S(1)} %fusion.20.refs_0_), custom_call_target="tpu_custom_call" | custom-call | bytes 125829120 | tf_op jit(solution)/shard_map/gather_one/pallas_call | solution.py:196
  85.6 1.9 copy-done.5
  88.9 5.5 collective-permute-start
  94.5 19.5 %fusion.25.proj.gate = f32[1024,3072]{1,0:T(8,128)} fusion(bf16[1024,2048]{1,0:T(8,128)(2,1)} %copy-done.5, bf16[2048,3072]{1,0:T(8,128)(2,1)} %all-gather.4.cloned.1.call-done), kind=kOutput, calls=%fused_computation.78 | convolution fusion | flops 12884901888 | bytes 29360128 | tf_op jit(solution)/shard_map/dot_general | solution.py:237
  114.0 3.0 broadcast_in_dim.4
  118.0 2.3 constant_dynamic-update-slice_fusion.5
  122.4 2.9 collective-permute-start.2
  129.3 2.3 pad_maximum_fusion.1
  131.6 11.2 %retention.1 = (bf16[1024,2048]{1,0:T(8,128)(2,1)}, bf16[1024,1024]{1,0:T(8,128)(2,1)S(1)}) custom-call(f32[2]{0:T(128)S(1)} %subtract_log_fusion.log_ref, f32[1024,3072]{1,0:T(8,128)} %fusion.25.proj.gate, f32[1024,128]{1,0:T(8,128)S(1)} %copy-done.10, f32[1024,128]{1,0:T(8,128)S(1)} %copy-done.8, s32[1024,1]{1,0:T(8,128)S(1)} %copy.31.seg_rows, ...), custom_call_target="tpu_custom_call" | custom-call | flops 2415919104 | bytes 18874368 | tf_op jit(solution)/shard_map/retention/pallas_call | solution.py:332
  144.1 2.3 collective-permute-done.2
  146.4 2.5 constant_dynamic-update-slice_fusion.3
  148.9 2.9 collective-permute-done.3
  151.8 2.3 constant_dynamic-update-slice_fusion.2
  154.2 8.3 %convolution_convert_fusion.6.refs_0_ = bf16[1024,2048]{1,0:T(8,128)(2,1)} fusion(bf16[1024,1024]{1,0:T(8,128)(2,1)S(1)} %copy-done.15, bf16[2048,1024]{1,0:T(8,128)(2,1)} %all-gather.6.cloned.1.call-done), kind=kOutput, calls=%fused_computation.24 | convolution fusion | flops 4297064448 | bytes 10485760 | tf_op jit(solution)/shard_map/dot_general | solution.py:237
  162.6 112.0 %residual.1 = (bf16[1024,2048]{1,0:T(8,128)(2,1)}, f32[256,2048]{1,0:T(8,128)S(1)}) custom-call(bf16[1024,2048]{1,0:T(8,128)(2,1)} %convolution_convert_fusion.6.refs_0_, bf16[256,2048]{1,0:T(8,128)(2,1)S(1)} %copy-done), custom_call_target="tpu_custom_call" | custom-call | bytes 125829120 | tf_op jit(solution)/shard_map/residual/pallas_call | solution.py:196
  274.6 1.6 collective-permute-start.4
  276.3 1.5 collective-permute-start.5
  277.8 12.5 %fusion.2 = f32[1024,2048]{1,0:T(8,128)S(1)} fusion(bf16[1024,2048]{1,0:T(8,128)(2,1)} %get-tuple-element.72, bf16[2048,3072]{1,0:T(8,128)(2,1)} %all-gather.8.cloned.1.call-done), kind=kOutput, calls=%fused_computation.4 | convolution fusion | flops 8589934592 | bytes 20971520 | tf_op jit(solution)/shard_map/dot_general | solution.py:237
  290.3 1.5 multiply_convert_fusion.1
  291.8 7.0 convolution_convert_fusion.5
  301.3 10.2 %fusion.10 = (bf16[1024,1024]{1,0:T(8,128)(2,1)S(1)}, bf16[1024,1024]{1,0:T(8,128)(2,1)S(1)}) fusion(f32[1024,2048]{1,0:T(8,128)S(1)} %fusion.2, bf16[2048,3072]{1,0:T(8,128)(2,1)} %all-gather.8.cloned.1.call-done, bf16[1280,2048]{1,0:T(8,128)(2,1)} %constant_dynamic-update-slice_fusion), kind=kOutput, calls=%fused_computation.14 | convolution fusion | flops 4320133120 | bytes 20971520 | tf_op jit(solution)/shard_map/dot_general | solution.py:237
  311.6 1.6 constant_dynamic-slice_fusion
  314.4 6.4 collective-permute-start.6
  320.9 2.4 pad_maximum_fusion
  323.3 8.3 %convolution_convert_fusion.4 = bf16[2048,1024]{1,0:T(8,128)(2,1)} fusion(bf16[1024,1024]{1,0:T(8,128)(2,1)S(1)} %multiply_convert_fusion.1, bf16[1280,2048]{1,0:T(8,128)(2,1)} %constant_dynamic-update-slice_fusion), kind=kOutput, calls=%fused_computation.22 | convolution fusion | flops 4297064448 | bytes 10485760 | tf_op jit(solution)/shard_map/dot_general | solution.py:237
  331.6 5.0 collective-permute-done.7
  337.8 4.4 add_convert_fusion.3
  343.5 6.1 collective-permute-start.8
  349.6 13.4 %convolution_convert_fusion.1 = bf16[2048,2048]{1,0:T(8,128)(2,1)} fusion(bf16[1024,2048]{1,0:T(8,128)(2,1)} %get-tuple-element.72, bf16[1024,2048]{1,0:T(8,128)(2,1)S(1)} %copy-done.22), kind=kOutput, calls=%fused_computation.1 | convolution fusion | flops 8594128896 | bytes 16777216 | tf_op jit(solution)/shard_map/dot_general | solution.py:237
  363.1 14.0 %fusion.11.refs_0_ = bf16[1024,2048]{1,0:T(8,128)(2,1)} fusion(bf16[1024,2048]{1,0:T(8,128)(2,1)} %pad_maximum_fusion, bf16[2048,3072]{1,0:T(8,128)(2,1)} %all-gather.8.cloned.1.call-done), kind=kOutput, calls=%fused_computation.20 | convolution fusion | flops 8592031744 | bytes 16777216 | tf_op jit(solution)/shard_map/dot_general | solution.py:237
  378.3 111.6 %d_residual.1 = (bf16[1024,2048]{1,0:T(8,128)(2,1)}, f32[256,2048]{1,0:T(8,128)S(1)}) custom-call(bf16[1024,2048]{1,0:T(8,128)(2,1)} %fusion.11.refs_0_, f32[256,2048]{1,0:T(8,128)S(1)} %get-tuple-element.84.refs_1_, bf16[256,2048]{1,0:T(8,128)(2,1)S(1)} %copy-done.4), custom_call_target="tpu_custom_call" | custom-call | bytes 125829120 | tf_op jit(solution)/shard_map/d_residual/pallas_call | solution.py:196
  491.4 9.4 %convolution_convert_fusion.3 = bf16[2048,1024]{1,0:T(8,128)(2,1)} fusion(bf16[1024,2048]{1,0:T(8,128)(2,1)} %get-tuple-element.91, bf16[1024,1024]{1,0:T(8,128)(2,1)} %copy-done.14), kind=kOutput, calls=%fused_computation.21 | convolution fusion | flops 4297064448 | bytes 10485760 | tf_op jit(solution)/shard_map/dot_general | solution.py:237
  500.9 5.0 add_convert_fusion.2
  505.9 2.6 collective-permute-start.10
  508.4 1.7 collective-permute-start.11
  510.2 8.2 %fusion.26.d_mixed = f32[1024,1024]{1,0:T(8,128)} fusion(bf16[1024,2048]{1,0:T(8,128)(2,1)} %get-tuple-element.91, bf16[2048,1024]{1,0:T(8,128)(2,1)S(1)} %copy-done.33), kind=kOutput, calls=%fused_computation.79 | convolution fusion | flops 4294967296 | bytes 12582912 | tf_op jit(solution)/shard_map/dot_general | solution.py:237
  518.4 18.5 %retention_pull.1 = bf16[1024,3072]{1,0:T(8,128)(2,1)} custom-call(f32[2]{0:T(128)S(1)} %subtract_log_fusion.log_ref, bf16[1024,2048]{1,0:T(8,128)(2,1)S(1)} %copy-done.7, f32[1024,3072]{1,0:T(8,128)} %fusion.25.proj.gate, f32[1024,1024]{1,0:T(8,128)} %fusion.26.d_mixed, f32[1024,128]{1,0:T(8,128)S(1)} %copy-done.11, f32[1024,128]{1,0:T(8,128)S(1)} %copy-done.9, ...), custom_call_target="tpu_custom_call" | custom-call | flops 7247757312 | bytes 25165824 | tf_op jit(solution)/shard_map/retention_pull/pallas_call | solution.py:372
  537.0 18.5 %convolution_convert_fusion = bf16[2048,3072]{1,0:T(8,128)(2,1)} fusion(bf16[1024,2048]{1,0:T(8,128)(2,1)S(1)} %copy-done.6, bf16[1024,3072]{1,0:T(8,128)(2,1)} %retention_pull.1), kind=kOutput, calls=%fused_computation | convolution fusion | flops 12891193344 | bytes 23068672 | tf_op jit(solution)/shard_map/dot_general | solution.py:237
  555.5 3.8 add_convert_fusion
  560.8 1.8 convert_multiply_fusion
  562.7 20.2 %convolution_convert_fusion.2.refs_0_ = bf16[1024,2048]{1,0:T(8,128)(2,1)} fusion(bf16[1024,3072]{1,0:T(8,128)(2,1)} %retention_pull.1, bf16[2048,3072]{1,0:T(8,128)(2,1)} %all-gather.4.cloned.1.call-done), kind=kOutput, calls=%fused_computation.19 | convolution fusion | flops 12886999040 | bytes 23068672 | tf_op jit(solution)/shard_map/dot_general | solution.py:237
  582.8 68.5 %tokens_grad.1 = bf16[256,2048]{1,0:T(8,128)(2,1)S(1)} custom-call(bf16[1024,2048]{1,0:T(8,128)(2,1)} %convolution_convert_fusion.2.refs_0_, bf16[256,2048]{1,0:T(8,128)(2,1)S(1)} %copy-done, f32[256,2048]{1,0:T(8,128)S(1)} %copy-done.13), custom_call_target="tpu_custom_call" | custom-call | bytes 125829120 | tf_op jit(solution)/shard_map/tokens_grad/pallas_call | solution.py:196
  651.4 2.1 convert_element_type.214
  653.6 2.1 convert_element_type.211
  655.7 36.7 %reduce-scatter.7.cloned.1.call-done = bf16[256,3072]{1,0:T(8,128)(2,1)} async-done(((bf16[2048,3072]{1,0:T(8,128)(2,1)}), bf16[256,3072]{1,0:T(8,128)(2,1)}) %reduce-scatter.7.cloned.1.call-update) | async-done | bytes 1572880 | tf_op jit(solution)/shard_map/reduce_scatter | solution.py:506
  692.4 2.4 multiply_reduce_fusion
  694.7 11.7 %all-reduce.1 = (f32[256]{0:T(256)S(1)}, f32[256]{0:T(256)S(1)}) all-reduce(f32[256]{0:T(256)S(1)} %multiply_reduce_fusion, f32[256]{0:T(256)S(1)} %get-tuple-element.121), channel_id=1, replica_groups=mesh['dp'=8,'tensor'=4] {'tensor'}, use_global_device_ids=true, to_apply=%region_4.5 | all-reduce | flops 512 | bytes 4096 | tf_op jit(solution)/shard_map/psum | solution.py:595
  710.5 4.0 convert_multiply_fusion.4
  (129 shorter events, 30.8 us)
Async XLA Ops:
  7.2 4.9 copy-start
  7.2 80.4 %all-gather.4.cloned.1.call-start = ((), (), s32[]{:S(2)}) async-start(), calls=%async_computation.4 | async-start | bytes 14155776 | tf_op jit(solution)/shard_map/all_gather | solution.py:500
  8.0 2.8 copy-start.26
  12.0 142.2 %all-gather.6.cloned.1.call-start = ((), (), s32[]{:S(2)}) async-start(), calls=%async_computation.5 | async-start | bytes 4718592 | tf_op jit(solution)/shard_map/all_gather | solution.py:500
  12.3 75.3 %copy-start.3 = (bf16[256,2048]{1,0:T(8,128)(2,1)S(1)}, bf16[256,2048]{1,0:T(8,128)(2,1)}, u32[]{:S(2)}) copy-start(bf16[256,2048]{1,0:T(8,128)(2,1)} %refs_2_.1) | copy-start | bytes 3145732
  85.6 2.0 copy-start.5
  87.6 187.1 %all-gather.8.cloned.1.call-start = ((), (), s32[]{:S(2)}) async-start(), calls=%async_computation.6 | async-start | bytes 14155776 | tf_op jit(solution)/shard_map/all_gather | solution.py:500
  87.6 32.7 %collective-permute-start.1 = (bf16[256,2048]{1,0:T(8,128)(2,1)S(1)}, bf16[256,2048]{1,0:T(8,128)(2,1)S(1)}, u32[]{:S(2)}, u32[]{:S(2)}) collective-permute-start(bf16[256,2048]{1,0:T(8,128)(2,1)S(1)} %copy-done.3), channel_id=1, source_target_pairs={{1,0},{2,1},{3,2},{5,4},{6,5},{7,6},{9,8},{10,9},{11,10},{13,12},{... | collective-permute-start | bytes 3145736 | tf_op jit(solution)/shard_map/ppermute | solution.py:453
  88.9 29.1 %collective-permute-start = (bf16[256,2048]{1,0:T(8,128)(2,1)S(1)}, bf16[256,2048]{1,0:T(8,128)(2,1)}, u32[]{:S(2)}, u32[]{:S(2)}) collective-permute-start(bf16[256,2048]{1,0:T(8,128)(2,1)S(1)} %copy-done.3), channel_id=1, source_target_pairs={{0,1},{1,2},{2,3},{4,5},{5,6},{6,7},{8,9},{9,10},{10,11},{12,13},{... | collective-permute-start | bytes 3145736 | tf_op jit(solution)/shard_map/ppermute | solution.py:453
  117.0 8.3 %copy-start.31 = (bf16[256]{0:T(256)(128)(2,1)S(1)}, bf16[256]{0:T(256)(128)(2,1)}, u32[]{:S(2)}) copy-start(bf16[256]{0:T(256)(128)(2,1)} %param.25) | copy-start | bytes 1540
  117.0 8.3 %copy-start.25 = (s32[1,1024]{1,0:T(1,128)S(1)}, s32[1,1024]{1,0:T(1,128)}, u32[]{:S(2)}) copy-start(s32[1,1024]{1,0:T(1,128)} %param.18) | copy-start | bytes 12292
  120.4 11.2 %copy-start.8 = (f32[1024,128]{1,0:T(8,128)S(1)}, f32[1024,128]{1,0:T(8,128)}, u32[]{:S(2)}) copy-start(f32[1024,128]{1,0:T(8,128)} %constant.75.clone.sine) | copy-start | bytes 1572868
  120.4 11.2 %copy-start.10 = (f32[1024,128]{1,0:T(8,128)S(1)}, f32[1024,128]{1,0:T(8,128)}, u32[]{:S(2)}) copy-start(f32[1024,128]{1,0:T(8,128)} %constant.74.clone.cosine) | copy-start | bytes 1572868
  122.4 24.0 %collective-permute-start.2 = (bf16[256,2048]{1,0:T(8,128)(2,1)}, bf16[256,2048]{1,0:T(8,128)(2,1)}, u32[]{:S(2)}, u32[]{:S(2)}) collective-permute-start(bf16[256,2048]{1,0:T(8,128)(2,1)} %collective-permute-done), channel_id=1, source_target_pairs={{0,1},{1,2},{2,3},{4,5},{5,6},{6,7},{8,9},{9,10},{10,11},{12,13},{... | collective-permute-start | bytes 3145736 | tf_op jit(solution)/shard_map/ppermute | solution.py:453
  125.3 17.5 %copy-start.28 = (f32[256]{0:T(256)}, f32[256]{0:T(256)S(1)}, u32[]{:S(2)}) copy-start(f32[256]{0:T(256)S(1)} %convert_element_type.177) | copy-start | bytes 3076
  125.6 17.3 %copy-start.1 = (s32[1024,1]{1,0:T(8,128)}, s32[1024,1]{1,0:T(8,128)S(1)}, u32[]{:S(2)}) copy-start(s32[1024,1]{1,0:T(8,128)S(1)} %copy.31.seg_rows) | copy-start | bytes 12292
  125.6 26.2 %collective-permute-start.3 = (bf16[256,2048]{1,0:T(8,128)(2,1)}, bf16[256,2048]{1,0:T(8,128)(2,1)}, u32[]{:S(2)}, u32[]{:S(2)}) collective-permute-start(bf16[256,2048]{1,0:T(8,128)(2,1)} %copy-done.23), channel_id=1, source_target_pairs={{1,0},{2,1},{3,2},{5,4},{6,5},{7,6},{9,8},{10,9},{11,10},{13,12},{... | collective-permute-start | bytes 3145736 | tf_op jit(solution)/shard_map/ppermute | solution.py:453
  142.8 1.3 copy-start.14
  146.4 7.7 %copy-start.15 = (bf16[1024,1024]{1,0:T(8,128)(2,1)S(1)}, bf16[1024,1024]{1,0:T(8,128)(2,1)}, u32[]{:S(2)}) copy-start(bf16[1024,1024]{1,0:T(8,128)(2,1)} %copy-done.14) | copy-start | bytes 6291460
  162.5 328.8 %reduce-scatter.5.cloned.1.call-start = ((), (), s32[]{:S(2)}) async-start(), calls=%async_computation.7 | async-start | bytes 9437184 | tf_op jit(solution)/shard_map/reduce_scatter | solution.py:506
  274.6 24.1 %collective-permute-start.4 = (bf16[256,2048]{1,0:T(8,128)(2,1)}, bf16[256,2048]{1,0:T(8,128)(2,1)S(1)}, u32[]{:S(2)}, u32[]{:S(2)}) collective-permute-start(bf16[256,2048]{1,0:T(8,128)(2,1)} %collective-permute-done.2), channel_id=1, source_target_pairs={{0,1},{1,2},{2,3},{4,5},{5,6},{6,7},{8,9},{9,10},{10,11},{12,13},{... | collective-permute-start | bytes 3145736 | tf_op jit(solution)/shard_map/ppermute | solution.py:453
  276.3 23.7 %collective-permute-start.5 = (bf16[256,2048]{1,0:T(8,128)(2,1)}, bf16[256,2048]{1,0:T(8,128)(2,1)S(1)}, u32[]{:S(2)}, u32[]{:S(2)}) collective-permute-start(bf16[256,2048]{1,0:T(8,128)(2,1)} %collective-permute-done.3), channel_id=1, source_target_pairs={{1,0},{2,1},{3,2},{5,4},{6,5},{7,6},{9,8},{10,9},{11,10},{13,12},{... | collective-permute-start | bytes 3145736 | tf_op jit(solution)/shard_map/ppermute | solution.py:453
  298.7 12.8 %copy-start.16 = (bf16[1024,2048]{1,0:T(8,128)(2,1)}, bf16[1024,2048]{1,0:T(8,128)(2,1)S(1)}, u32[]{:S(2)}) copy-start(bf16[1024,2048]{1,0:T(8,128)(2,1)S(1)} %convolution_convert_fusion.5) | copy-start | bytes 12582916
  313.1 23.5 %collective-permute-start.7 = (bf16[256,2048]{1,0:T(8,128)(2,1)}, bf16[256,2048]{1,0:T(8,128)(2,1)}, u32[]{:S(2)}, u32[]{:S(2)}) collective-permute-start(bf16[256,2048]{1,0:T(8,128)(2,1)} %get-tuple-element.108), channel_id=1, source_target_pairs={{1,0},{2,1},{3,2},{5,4},{6,5},{7,6},{9,8},{10,9},{11,10},{13,12},{... | collective-permute-start | bytes 3145736 | tf_op jit(solution)/shard_map/ppermute | solution.py:472
  314.4 23.4 %collective-permute-start.6 = (bf16[256,2048]{1,0:T(8,128)(2,1)}, bf16[256,2048]{1,0:T(8,128)(2,1)}, u32[]{:S(2)}, u32[]{:S(2)}) collective-permute-start(bf16[256,2048]{1,0:T(8,128)(2,1)} %get-tuple-element.109), channel_id=1, source_target_pairs={{0,1},{1,2},{2,3},{4,5},{5,6},{6,7},{8,9},{9,10},{10,11},{12,13},{... | collective-permute-start | bytes 3145736 | tf_op jit(solution)/shard_map/ppermute | solution.py:472
  331.6 18.0 %copy-start.22 = (bf16[1024,2048]{1,0:T(8,128)(2,1)S(1)}, bf16[1024,2048]{1,0:T(8,128)(2,1)}, u32[]{:S(2)}) copy-start(bf16[1024,2048]{1,0:T(8,128)(2,1)} %pad_maximum_fusion) | copy-start | bytes 12582916
  342.2 34.8 %collective-permute-start.9 = (bf16[256,2048]{1,0:T(8,128)(2,1)}, bf16[256,2048]{1,0:T(8,128)(2,1)}, u32[]{:S(2)}, u32[]{:S(2)}) collective-permute-start(bf16[256,2048]{1,0:T(8,128)(2,1)} %get-tuple-element.106), channel_id=1, source_target_pairs={{1,0},{2,1},{3,2},{5,4},{6,5},{7,6},{9,8},{10,9},{11,10},{13,12},{... | collective-permute-start | bytes 3145736 | tf_op jit(solution)/shard_map/ppermute | solution.py:472
  343.5 33.5 %collective-permute-start.8 = (bf16[256,2048]{1,0:T(8,128)(2,1)}, bf16[256,2048]{1,0:T(8,128)(2,1)}, u32[]{:S(2)}, u32[]{:S(2)}) collective-permute-start(bf16[256,2048]{1,0:T(8,128)(2,1)} %get-tuple-element.107), channel_id=1, source_target_pairs={{0,1},{1,2},{2,3},{4,5},{5,6},{6,7},{8,9},{9,10},{10,11},{12,13},{... | collective-permute-start | bytes 3145736 | tf_op jit(solution)/shard_map/ppermute | solution.py:472
  377.1 274.4 %reduce-scatter.11.cloned.1.call-start = ((), (), s32[]{:S(2)}) async-start(), calls=%async_computation.10 | async-start | bytes 4718592 | tf_op jit(solution)/shard_map/reduce_scatter | solution.py:506
  377.1 1.2 copy-start.4
  490.0 1.4 copy-start.12
  491.3 162.2 %reduce-scatter.9.cloned.1.call-start = ((), (), s32[]{:S(2)}) async-start(), calls=%async_computation.9 | async-start | bytes 4718592 | tf_op jit(solution)/shard_map/reduce_scatter | solution.py:506
  500.8 191.5 %reduce-scatter.7.cloned.1.call-start = ((), (), s32[]{:S(2)}) async-start(), calls=%async_computation.8 | async-start | bytes 14155776 | tf_op jit(solution)/shard_map/reduce_scatter | solution.py:506
  500.9 9.3 %copy-start.33 = (bf16[2048,1024]{1,0:T(8,128)(2,1)S(1)}, bf16[2048,1024]{1,0:T(8,128)(2,1)}, u32[]{:S(2)}) copy-start(bf16[2048,1024]{1,0:T(8,128)(2,1)} %all-gather.6.cloned.1.call-done) | copy-start | bytes 12582916
  505.9 49.6 %collective-permute-start.10 = (bf16[256,2048]{1,0:T(8,128)(2,1)}, bf16[256,2048]{1,0:T(8,128)(2,1)}, u32[]{:S(2)}, u32[]{:S(2)}) collective-permute-start(bf16[256,2048]{1,0:T(8,128)(2,1)} %get-tuple-element.104), channel_id=1, source_target_pairs={{0,1},{1,2},{2,3},{4,5},{5,6},{6,7},{8,9},{9,10},{10,11},{12,13},{... | collective-permute-start | bytes 3145736 | tf_op jit(solution)/shard_map/ppermute | solution.py:472
  508.4 10.0 %copy-start.2 = (s32[1024,1]{1,0:T(8,128)S(1)}, s32[1024,1]{1,0:T(8,128)}, u32[]{:S(2)}) copy-start(s32[1024,1]{1,0:T(8,128)} %copy-done.1) | copy-start | bytes 12292
  508.4 10.0 %copy-start.7 = (bf16[1024,2048]{1,0:T(8,128)(2,1)S(1)}, bf16[1024,2048]{1,0:T(8,128)(2,1)}, u32[]{:S(2)}) copy-start(bf16[1024,2048]{1,0:T(8,128)(2,1)} %get-tuple-element.60.kept) | copy-start | bytes 12582916
  508.4 10.0 %copy-start.9 = (f32[1024,128]{1,0:T(8,128)S(1)}, f32[1024,128]{1,0:T(8,128)}, u32[]{:S(2)}) copy-start(f32[1024,128]{1,0:T(8,128)} %constant.75.clone.sine) | copy-start | bytes 1572868
  508.4 10.0 %copy-start.11 = (f32[1024,128]{1,0:T(8,128)S(1)}, f32[1024,128]{1,0:T(8,128)}, u32[]{:S(2)}) copy-start(f32[1024,128]{1,0:T(8,128)} %constant.74.clone.cosine) | copy-start | bytes 1572868
  508.4 47.1 %collective-permute-start.11 = (bf16[256,2048]{1,0:T(8,128)(2,1)}, bf16[256,2048]{1,0:T(8,128)(2,1)}, u32[]{:S(2)}, u32[]{:S(2)}) collective-permute-start(bf16[256,2048]{1,0:T(8,128)(2,1)} %get-tuple-element.105), channel_id=1, source_target_pairs={{1,0},{2,1},{3,2},{5,4},{6,5},{7,6},{9,8},{10,9},{11,10},{13,12},{... | collective-permute-start | bytes 3145736 | tf_op jit(solution)/shard_map/ppermute | solution.py:472
  518.4 18.6 %copy-start.6 = (bf16[1024,2048]{1,0:T(8,128)(2,1)S(1)}, bf16[1024,2048]{1,0:T(8,128)(2,1)}, u32[]{:S(2)}) copy-start(bf16[1024,2048]{1,0:T(8,128)(2,1)} %copy-done.5) | copy-start | bytes 12582916
  559.3 1.2 copy-start.21
  559.3 1.5 copy-start.24
  559.3 1.5 copy-start.29
  562.7 20.2 %copy-start.13 = (f32[256,2048]{1,0:T(8,128)S(1)}, f32[256,2048]{1,0:T(8,128)}, u32[]{:S(2)}) copy-start(f32[256,2048]{1,0:T(8,128)} %copy-done.12) | copy-start | bytes 6291460
  651.4 55.1 %copy-start.30 = (bf16[256]{0:T(256)(128)(2,1)S(1)}, bf16[256]{0:T(256)(128)(2,1)}, u32[]{:S(2)}) copy-start(bf16[256]{0:T(256)(128)(2,1)} %param.19) | copy-start | bytes 1540
  651.4 55.0 %copy-start.32 = (bf16[256]{0:T(256)(128)(2,1)S(1)}, bf16[256]{0:T(256)(128)(2,1)}, u32[]{:S(2)}) copy-start(bf16[256]{0:T(256)(128)(2,1)} %param.25) | copy-start | bytes 1540
  651.4 56.8 %copy-start.27 = (f32[256]{0:T(256)S(1)}, f32[256]{0:T(256)}, u32[]{:S(2)}) copy-start(f32[256]{0:T(256)} %copy-done.26) | copy-start | bytes 3076
  (5 other events, 4.9 us)
Sparse Core Ops, SparseCore 0:
  12.1 74.8 all-gather.3
  88.9 36.7 all-gather.5
  162.6 70.2 all-gather.7
  377.2 71.0 reduce-scatter.4
  491.5 49.9 reduce-scatter.10
  544.7 51.3 reduce-scatter.8
  599.9 92.4 reduce-scatter.6

commit v3 on v2

--- a/solution.py
+++ b/solution.py
@@ -8,18 +8,52 @@
 from jax.sharding import PartitionSpec as P
 
 AXIS = "tensor"
-
-
-def line_body(n, chunks, rs, ag, middle, n_in, n_out, *refs):
+TALL = 256
+COLUMNS = 1024
+
+
+def line_body(n, chunks, rs, ag, rolled, middle, square, n_in, n_out, *refs):
     ins, outs, scratch = refs[:n_in], refs[n_in : n_in + n_out], list(refs[n_in + n_out :])
     me = lax.axis_index(AXIS)
     last = n - 1
     lag = last if rs else 0
+    greet, also, finish, steps = lambda barrier: 0, lambda s: None, lambda: None, 0
     if rs:
-        part, ins = ins[0], ins[1:]
-        up_buf, dn_buf, total, up_send, up_recv, dn_send, dn_recv = scratch[:7]
-        scratch = scratch[7:]
-        rows = up_buf.shape[1]
+        here, load_sems, left_sems, right_sems = scratch[:n_in], *scratch[n_in : n_in + 3]
+        scratch = scratch[n_in + 3 :]
+        outside, (left, right) = ins, here[:2]
+        groups = left.shape[0] // TALL
+        rows, tall, wide = left.shape[0] // n, left.shape[0] // n // groups, min(COLUMNS, right.shape[0])
+
+        def left_copy(g, j):
+            at = pl.ds(j * rows + g * tall, tall)
+            return pltpu.make_async_copy(outside[0].at[at], left.at[at], left_sems.at[g, j])
+
+        def right_copy(q):
+            at = pl.ds(pl.multiple_of(q * wide, wide), wide)
+            return pltpu.make_async_copy(outside[1].at[at, pl.ds(0, right.shape[1])], right.at[at], right_sems.at[q])
+
+        def later_copies():
+            return [left_copy(g, j) for g in range(1, groups) for j in range(n)] + [
+                pltpu.make_async_copy(outside[i], here[i], load_sems.at[i]) for i in range(2, n_in)
+            ]
+
+        for j in range(n):
+            left_copy(0, j).start()
+        for q in range(right.shape[0] // wide):
+            right_copy(q).start()
+        for copy in later_copies():
+            copy.start()
+        ins = here
+    if square is not None:
+        counts = square[1:]
+        square_refs = ins[n_in - counts[0] :], outs[n_out - counts[1] :], scratch[len(scratch) - counts[2] :]
+        ins, outs, scratch = ins[: n_in - counts[0]], outs[: n_out - counts[1]], scratch[: len(scratch) - counts[2]]
+        greet, also, finish, steps = square[0](ins[0], *square_refs)
+    if rs:
+        ins = ins[2:]
+        part, up_buf, dn_buf, total, up_send, up_recv, dn_send, dn_recv = scratch[:8]
+        scratch = scratch[8:]
     if ag:
         full, outs = outs[0], outs[1:]
         own, ag_recv, ag_up, ag_dn, ag_here = scratch[:5]
@@ -28,6 +62,27 @@
 
     def cut(c, base=0):
         return pl.ds(pl.multiple_of(base + c * size, size), size)
+
+    def slot(j, device, turned):
+        return lax.rem(j - device + n, n) if turned else j
+
+    def product(g):
+        block = jnp.concatenate([left[pl.ds(pl.multiple_of(j * rows + g * tall, tall), tall)] for j in range(n)], axis=0)
+
+        def tile(q, _):
+            @pl.when(g == 0)
+            def _():
+                right_copy(q).wait()
+
+            columns = pl.ds(pl.multiple_of(q * wide, wide), wide)
+            found = lax.dot_general(block, right[columns], (((1,), (1,)), ((), ())), preferred_element_type=jnp.float32)
+            for j in range(n):
+                part[pl.ds(pl.multiple_of(j * rows + g * tall, tall), tall), columns] = found[
+                    j * tall : (j + 1) * tall
+                ].astype(part.dtype)
+            return 0
+
+        lax.fori_loop(0, right.shape[0] // wide, tile, 0)
 
     def send(src, dst, send_sem, recv_sem, to):
         return pltpu.make_async_remote_copy(
@@ -49,36 +104,38 @@
     def _():
         pl.semaphore_signal(barrier, inc=1, device_id={AXIS: me + 1}, device_id_type=pl.DeviceIdType.MESH)
 
-    pl.semaphore_wait(barrier, jnp.where((me > 0) & (me < last), 2, 1))
+    others = greet(barrier)
+    pl.semaphore_wait(barrier, jnp.where((me > 0) & (me < last), 2, 1) + others)
 
     def sum_copy(up, d, c):
         buf, s, r, to = (up_buf, up_send, up_recv, me + 1) if up else (dn_buf, dn_send, dn_recv, me - 1)
-        ref = buf.at[d, cut(c)]
+        ref = buf.at[d - up, cut(c)]
         return send(ref, ref, s.at[d, c], r.at[d, c], to)
 
     def sum_step(up, d, c):
         buf = up_buf if up else dn_buf
         first = 0 if up else last
-        mine = part[cut(c, d * rows)]
+        mine = part[cut(c, slot(d, me, rolled[0]) * rows)]
 
         @pl.when(me == first)
         def _():
-            buf[d, cut(c)] = mine
+            buf[d - up, cut(c)] = mine
 
         @pl.when(me != first)
         def _():
             sum_copy(up, d, c).wait_recv()
-            buf[d, cut(c)] = (buf[d, cut(c)].astype(jnp.float32) + mine.astype(jnp.float32)).astype(buf.dtype)
+            buf[d - up, cut(c)] = (buf[d - up, cut(c)].astype(jnp.float32) + mine.astype(jnp.float32)).astype(buf.dtype)
 
         sum_copy(up, d, c).start()
 
     def gather_copy(up, j, c, from_own=False):
-        ref = full.at[cut(c, j * rows)]
-        src = own.at[cut(c)] if from_own else ref
-        return send(src, ref, (ag_up if up else ag_dn).at[j, c], ag_recv.at[j, c], me + 1 if up else me - 1)
+        to = me + 1 if up else me - 1
+        src = own.at[cut(c)] if from_own else full.at[cut(c, slot(j, me, rolled[1]) * rows)]
+        dst = full.at[cut(c, slot(j, to, rolled[1]) * rows)]
+        return send(src, dst, (ag_up if up else ag_dn).at[j, c], ag_recv.at[j, c], to)
 
     def here_copy(c):
-        return pltpu.make_async_copy(own.at[cut(c)], full.at[cut(c, me * rows)], ag_here.at[c])
+        return pltpu.make_async_copy(own.at[cut(c)], full.at[cut(c, slot(me, me, rolled[1]) * rows)], ag_here.at[c])
 
     def step(s, _):
         if rs:
@@ -90,18 +147,30 @@
                     def _(up=up, c=c, d=d):
                         sum_step(up, d, c)
 
+            @pl.when(s == 0)
+            def _():
+                for copy in later_copies():
+                    copy.wait()
+
+            per_group = chunks // groups
+
+            @pl.when((lax.rem(s, per_group) == 0) & (s + per_group < chunks))
+            def _():
+                product(s // per_group + 1)
+
+        also(s)
         c_own = s - lag
 
         @pl.when((c_own >= 0) & (c_own < chunks))
         def _():
             c = c_own
             if rs:
-                total[...] = part[cut(c, me * rows)].astype(jnp.float32)
+                total[...] = part[cut(c, slot(me, me, rolled[0]) * rows)].astype(jnp.float32)
 
                 @pl.when(me > 0)
                 def _():
                     sum_copy(True, me, c).wait_recv()
-                    total[...] += up_buf[me, cut(c)].astype(jnp.float32)
+                    total[...] += up_buf[me - 1, cut(c)].astype(jnp.float32)
 
                 @pl.when(me < last)
                 def _():
@@ -136,7 +205,12 @@
 
         return 0
 
-    lax.fori_loop(0, chunks + lag + (last - 1 if ag else 0), step, 0)
+    if rs:
+        for j in range(n):
+            left_copy(0, j).wait()
+        product(0)
+    lax.fori_loop(0, max(chunks + lag + (last - 1 if ag else 0), steps), step, 0)
+    finish()
 
     def drain(c, _):
         if rs:
@@ -171,42 +245,270 @@
     lax.fori_loop(0, chunks, drain, 0)
 
 
-def line_pass(name, part, extras, extra_outs, middle, ag, chunks, collective_id, rows, width):
+def line_pass(name, summed, extras, extra_outs, middle, ag, chunks, collective_id, rows, width, rolled=(False, False), square=None, square_ins=(), square_outs=(), square_scratch=()):
     n = lax.axis_size(AXIS)
-    rs = part is not None
+    rs = summed is not None
     size = rows // chunks
     vmem = pl.BlockSpec(memory_space=pltpu.VMEM)
+    operands = (list(summed) if rs else []) + list(extras) + list(square_ins)
     scratch = []
     sems = pltpu.SemaphoreType.DMA((n, chunks))
     if rs:
+        depth = summed[0].shape[1]
+        shapes = [(n * rows, depth), (width, depth)] + [operand.shape for operand in operands[2:]]
+        scratch += [pltpu.VMEM(shape, operand.dtype) for shape, operand in zip(shapes, operands)]
         scratch += [
-            pltpu.VMEM((n, rows, width), jnp.bfloat16),
-            pltpu.VMEM((n, rows, width), jnp.bfloat16),
+            pltpu.SemaphoreType.DMA((len(operands),)),
+            pltpu.SemaphoreType.DMA((n * rows // TALL, n)),
+            pltpu.SemaphoreType.DMA((width // min(COLUMNS, width),)),
+            pltpu.VMEM((n * rows, width), jnp.bfloat16),
+            pltpu.VMEM((n - 1, rows, width), jnp.bfloat16),
+            pltpu.VMEM((n - 1, rows, width), jnp.bfloat16),
             pltpu.VMEM((size, width), jnp.float32),
             sems, sems, sems, sems,
         ]
     if ag:
         scratch += [pltpu.VMEM((rows, width), jnp.bfloat16), sems, sems, sems, pltpu.SemaphoreType.DMA((chunks,))]
-    operands = ([part] if rs else []) + list(extras)
     shapes = ([jax.ShapeDtypeStruct((n * rows, width), jnp.bfloat16)] if ag else []) + [
         jax.ShapeDtypeStruct((rows, width), kind) for kind in extra_outs
-    ]
-    specs = ([pl.BlockSpec(memory_space=pl.ANY)] if ag else []) + [vmem] * len(extra_outs)
+    ] + list(square_outs)
+    specs = ([pl.BlockSpec(memory_space=pl.ANY)] if ag else []) + [vmem] * (len(extra_outs) + len(square_outs))
+    if square is not None:
+        square = (square, len(square_ins), len(square_outs), len(square_scratch))
     moved = rows * width * 2 * (n - 1)
     return pl.pallas_call(
-        functools.partial(line_body, n, chunks, rs, ag, middle, len(operands), len(shapes)),
+        functools.partial(line_body, n, chunks, rs, ag, rolled, middle, square, len(operands), len(shapes)),
         out_shape=shapes,
-        in_specs=[vmem] * len(operands),
+        in_specs=[pl.BlockSpec(memory_space=pl.ANY) if rs else vmem] * len(operands),
         out_specs=specs,
-        scratch_shapes=scratch,
+        scratch_shapes=scratch + list(square_scratch),
         compiler_params=pltpu.CompilerParams(
-            collective_id=collective_id, has_side_effects=True, vmem_limit_bytes=48 * 1024 * 1024
+            collective_id=collective_id, has_side_effects=True, vmem_limit_bytes=(62 if square else 52 if rs else 16) * 1024 * 1024
         ),
         cost_estimate=pl.CostEstimate(
             flops=0, bytes_accessed=moved * 40, transcendentals=0, remote_bytes_transferred=moved
         ),
         name=name,
     )(*operands)
+
+
+def flipped(index, bit):
+    return index + (1 << bit) - 2 * (1 << bit) * lax.rem(index // (1 << bit), 2)
+
+
+def square_parts(heads, left, ins, outs, scratch):
+    turned, gain, weights = ins
+    gain_sum, grads = outs[0], outs[1:]
+    sums, sums_in, sums_send, sums_recv, sent, own, *rest = scratch
+    line = lax.axis_index(AXIS)
+    line_bits = lax.axis_size(AXIS).bit_length() - 1
+    size = lax.axis_size("dp")
+    bits = size.bit_length() - 1
+    arrived, (first_send, first_recv), sems = rest[:bits], rest[bits : bits + 2], rest[bits + 2 :]
+    me = lax.axis_index("dp")
+    rows, wide = own.shape[2:]
+    half = wide // 2
+    pairs = arrived[0].shape[0]
+    orders = list(range(bits - 1)), list(range(bits - 1))[::-1]
+
+    def greet(barrier):
+        for bit in range(bits):
+            pl.semaphore_signal(barrier, inc=1, device_id={"dp": flipped(me, bit)}, device_id_type=pl.DeviceIdType.MESH)
+        for bit in range(line_bits):
+            pl.semaphore_signal(barrier, inc=1, device_id={AXIS: flipped(line, bit)}, device_id_type=pl.DeviceIdType.MESH)
+        return bits + line_bits
+
+    def sums_copy(bit):
+        return pltpu.make_async_remote_copy(
+            src_ref=sums.at[bit],
+            dst_ref=sums_in.at[bit],
+            send_sem=sums_send.at[bit],
+            recv_sem=sums_recv.at[bit],
+            device_id={AXIS: flipped(line, bit)},
+            device_id_type=pl.DeviceIdType.MESH,
+        )
+
+    def send(src, dst, send_sem, recv_sem, bit):
+        return pltpu.make_async_remote_copy(
+            src_ref=src,
+            dst_ref=dst,
+            send_sem=send_sem,
+            recv_sem=recv_sem,
+            device_id={"dp": flipped(me, bit)},
+            device_id_type=pl.DeviceIdType.MESH,
+        )
+
+    def first_copy(p, u):
+        return send(sent.at[lax.rem(p, 2), u], arrived[0].at[p, u], first_send.at[p, u], first_recv.at[p, u], 0)
+
+    def kept(side, stage):
+        done = orders[side][: stage - 1]
+        return [u for u in range(size // 2) if all(not u >> bit & 1 for bit in done)]
+
+    def later_copies(p, side, stage):
+        bit = orders[side][stage - 1]
+        stay = kept(side, stage + 1)
+        columns = pl.ds(side * half, half)
+        send_sem, recv_sem = sems[2 * (stage - 1)], sems[2 * (stage - 1) + 1]
+        return [
+            send(
+                arrived[0].at[p, u | 1 << bit, :, columns],
+                arrived[stage].at[p, rank, :, columns],
+                send_sem.at[p, side, rank],
+                recv_sem.at[p, side, rank],
+                bit + 1,
+            )
+            for rank, u in enumerate(stay)
+        ]
+
+    def multiply(p, u, odd):
+        owner = me
+        for bit in range(bits):
+            set_bit = odd if bit == 0 else lax.rem(u // (1 << (bit - 1)), 2)
+            owner = owner + set_bit * (1 << bit) * (1 - 2 * lax.rem(me // (1 << bit), 2))
+        block = turned[pl.ds(pl.multiple_of(owner * rows, rows), rows)]
+        columns = left[:, pl.ds(pl.multiple_of(p * wide, wide), wide)]
+        return jnp.dot(block, columns, preferred_element_type=jnp.float32).astype(own.dtype)
+
+    def also(s):
+        @pl.when(s < pairs)
+        def _():
+            p = s
+
+            @pl.when(p >= 2)
+            def _():
+                for u in range(size // 2):
+                    first_copy(p - 2, u).wait_send()
+
+            def to_send(u, _):
+                sent[lax.rem(p, 2), u] = multiply(p, u, 1)
+                first_copy(p, u).start()
+                return 0
+
+            def to_keep(u, _):
+                own[lax.rem(p, 2), u] = multiply(p, u, 0)
+                return 0
+
+            lax.fori_loop(0, size // 2, to_send, 0)
+            lax.fori_loop(0, size // 2, to_keep, 0)
+
+        for stage in range(1, bits + 1):
+
+            @pl.when((s >= stage) & (s < pairs + stage))
+            def _(stage=stage):
+                p = s - stage
+                if stage == 1:
+                    for u in range(size // 2):
+                        first_copy(p, u).wait_recv()
+                        summed = arrived[0][p, u].astype(jnp.float32) + own[lax.rem(p, 2), u].astype(jnp.float32)
+                        arrived[0][p, u] = summed.astype(own.dtype)
+                for side in range(2):
+                    columns = pl.ds(side * half, half)
+                    if stage > 1:
+                        for copy in later_copies(p, side, stage - 1):
+                            copy.wait_recv()
+                        for rank, u in enumerate(kept(side, stage)):
+                            summed = arrived[0][p, u, :, columns].astype(jnp.float32) + arrived[stage - 1][
+                                p, rank, :, columns
+                            ].astype(jnp.float32)
+                            if stage < bits:
+                                arrived[0][p, u, :, columns] = summed.astype(own.dtype)
+                            else:
+                                result(p, side, summed)
+                    if stage < bits:
+                        for copy in later_copies(p, side, stage):
+                            copy.start()
+
+        for bit in range(line_bits + 1):
+
+            @pl.when(s == pairs + bits + bit)
+            def _(bit=bit):
+                if bit:
+                    sums_copy(bit - 1).wait()
+                    sums[bit] = sums[bit - 1] + sums_in[bit - 1]
+                if bit < line_bits:
+                    sums_copy(bit).start()
+                else:
+                    gain_sum[...] = sums[bit]
+
+    def result(p, side, summed):
+        at = pl.ds(pl.multiple_of(p * wide + side * half, half), half)
+        terms = jnp.sum(summed * weights[:, at].astype(jnp.float32), axis=1, keepdims=True)
+        terms = jnp.broadcast_to(terms, sums.shape[1:])
+        if side:
+            sums[0] += terms
+        else:
+
+            @pl.when(p == 0)
+            def _():
+                sums[0] = terms
+
+            @pl.when(p > 0)
+            def _():
+                sums[0] += terms
+
+        summed = summed * gain[...]
+        for found in range(pairs):
+            head, kind = found // (pairs // heads), found % (pairs // heads)
+            where = grads[side] if kind == 0 else grads[1 + kind]
+            start = head * half if kind == 0 else head * wide + side * half
+
+            @pl.when(p == found)
+            def _(where=where, start=start):
+                where[:, start : start + half] = summed
+
+    def finish():
+        for p in range(max(pairs - 2, 0), pairs):
+            for u in range(size // 2):
+                first_copy(p, u).wait_send()
+
+        def drain(p, _):
+            for side in range(2):
+                for stage in range(1, bits):
+                    for copy in later_copies(p, side, stage):
+                        copy.wait_send()
+            return 0
+
+        lax.fori_loop(0, pairs, drain, 0)
+
+    return greet, also, finish, pairs + bits + line_bits + 1
+
+
+def square_shapes(rows, heads, columns):
+    size = lax.axis_size("dp")
+    bits = size.bit_length() - 1
+    wide = 2 * KD
+    pairs = columns // wide
+    sums = [pltpu.VMEM((pairs, size >> (stage + 1), rows, wide), jnp.bfloat16) for stage in range(bits)]
+    sems = [pltpu.SemaphoreType.DMA((pairs, size // 2))] * 2
+    for stage in range(1, bits):
+        sems += [pltpu.SemaphoreType.DMA((pairs, 2, size >> (stage + 1)))] * 2
+    outs = [jax.ShapeDtypeStruct((rows, 128), jnp.float32)]
+    line_bits = lax.axis_size(AXIS).bit_length() - 1
+    line_sems = pltpu.SemaphoreType.DMA((max(line_bits, 1),))
+    line_scratch = [
+        pltpu.VMEM((line_bits + 1, rows, 128), jnp.float32),
+        pltpu.VMEM((max(line_bits, 1), rows, 128), jnp.float32),
+        line_sems,
+        line_sems,
+    ]
+    outs += [jax.ShapeDtypeStruct((rows, heads * cols), jnp.float32) for cols in (KD, KD, VD, VD)]
+    return outs, line_scratch + [pltpu.VMEM((2, size // 2, rows, wide), jnp.bfloat16)] * 2 + sums + sems
+
+
+def turn_parts(blocks, left, ins, outs, scratch):
+    (rows_in,), (turned,) = ins, outs
+    columns = rows_in.shape[1] // blocks
+
+    def also(s):
+        for block in range(blocks):
+
+            @pl.when(s == block)
+            def _(block=block):
+                at = pl.ds(block * columns, columns)
+                turned[at] = rows_in[:, at].T
+
+    return lambda barrier: 0, also, lambda: None, blocks
 
 
 HEADS = 8
@@ -276,7 +578,7 @@
 
 
 def retention_pull_body(
-    block, reach, log_ref, kept, gate, d_mixed, cosine, sine, seg_rows, seg_line, d_in, keys, vals, d_keys, d_vals, decay
+    block, reach, log_ref, kept, gate, d_branch, w_out, cosine, sine, seg_rows, seg_line, d_in, keys, vals, d_keys, d_vals, decay
 ):
     head, row = pl.program_id(0), pl.num_programs(1) - 1 - pl.program_id(1)
     mine = pl.ds(pl.multiple_of(row * block, block), block)
@@ -297,7 +599,7 @@
     weight = jnp.where(seg_rows[...] == seg_line[:, window], decay[...], 0.0)
     probs = (dot(query, keys[window], CONTRACT_COLUMNS) * weight).astype(jnp.bfloat16)
     normed, inverse = normed_heads(dot(probs, vals[window]))
-    gate_pre, upstream = gate[...], d_mixed[...]
+    gate_pre, upstream = gate[...], dot(d_branch[...], w_out[...])
     opened = jax.nn.sigmoid(gate_pre)
     silu = gate_pre * opened
     d_in[:, 2 * KD + VD :] = (upstream * normed * (opened + silu * (1.0 - opened))).astype(jnp.bfloat16)
@@ -361,7 +663,7 @@
     )(log_decay, projected, cosine, sine, seg_rows, seg_line)
 
 
-def retention_pull(kept, projected, d_mixed, segments, heads):
+def retention_pull(kept, projected, d_branch, w_out, segments, heads):
     length = kept.shape[0]
     block, reach, log_decay, seg_rows, seg_line = retention_inputs(segments, heads)
     cosine, sine = rotary_tables(length)
@@ -376,7 +678,8 @@
             pl.BlockSpec(memory_space=pltpu.SMEM),
             pl.BlockSpec((length, 2 * KD + VD), lambda h, r: (0, h)),
             pl.BlockSpec((block, VD), lambda h, r: (last - r, gate_block * h + gate_block - 1)),
-            pl.BlockSpec((block, VD), lambda h, r: (last - r, h)),
+            pl.BlockSpec((block, d_branch.shape[1]), lambda h, r: (last - r, 0)),
+            pl.BlockSpec((w_out.shape[0], VD), lambda h, r: (0, h)),
             table,
             table,
             pl.BlockSpec((block, 1), lambda h, r: (last - r, 0)),
@@ -396,7 +699,7 @@
             flops=heads * length * (reach + block) * (3 * KD + 3 * VD) * 2, bytes_accessed=projected.size * 8, transcendentals=0
         ),
         name="retention_pull",
-    )(log_decay, kept, projected, d_mixed, cosine, sine, seg_rows, seg_line)
+    )(log_decay, kept, projected, d_branch, w_out, cosine, sine, seg_rows, seg_line)
 
 
 def inverse_rms(rows):
@@ -405,6 +708,11 @@
 
 def norm_pull(unit, inverse, d_unit):
     return inverse * (d_unit - unit * jnp.mean(d_unit * unit, axis=-1, keepdims=True))
+
+
+def unit_step(cut, summed, ins, outs):
+    inputs = ins[0][cut].astype(jnp.float32)
+    return inputs * inverse_rms(inputs)
 
 
 def residual_step(cut, summed, ins, outs):
@@ -433,45 +741,62 @@
     return [(i, i + 1) if up else (i + 1, i) for i in range(n - 1)]
 
 
+def joined_body(parts, plain, *refs):
+    *arrays, gain, out = refs
+    at = 0
+    for array, index, columns in parts:
+        found = arrays[array][:, index * columns : (index + 1) * columns]
+        if array < len(arrays) - plain:
+            found = (found.astype(jnp.float32) * gain[...]).astype(out.dtype)
+        out[:, at : at + columns] = found
+        at += columns
+
+
+def joined(name, arrays, gain, parts, plain=0):
+    columns = sum(part[2] for part in parts)
+    return pl.pallas_call(
+        functools.partial(joined_body, parts, plain),
+        out_shape=jax.ShapeDtypeStruct((gain.shape[0], columns), arrays[0].dtype),
+        compiler_params=pltpu.CompilerParams(vmem_limit_bytes=16 * 1024 * 1024),
+        name=name,
+    )(*arrays, gain)
+
+
 def steps_of(part, parts):
     n = lax.axis_size(AXIS)
     return range((n - 1) * part // parts, (n - 1) * (part + 1) // parts)
 
 
-def gather_start(own):
+def gather_steps(state, steps):
+    for _ in steps:
+        up, down = state[-2:]
+        state = [*state, lax.ppermute(up, AXIS, hops(True)), lax.ppermute(down, AXIS, hops(False))]
+    return state
+
+
+def gather_end(state):
     n, me = lax.axis_size(AXIS), lax.axis_index(AXIS)
-    rows = own.shape[0]
-    full = jnp.zeros(((n + 1) * rows,) + own.shape[1:], own.dtype)
-    return own, own, lax.dynamic_update_slice_in_dim(full, own, me * rows, 0)
-
-
-def gather_steps(state, steps):
-    n, me = lax.axis_size(AXIS), lax.axis_index(AXIS)
-    up, down, full = state
-    rows = up.shape[0]
-    for t in steps:
-        up, down = lax.ppermute(up, AXIS, hops(True)), lax.ppermute(down, AXIS, hops(False))
-        for arrived, j in ((up, me - t - 1), (down, me + t + 1)):
-            full = lax.dynamic_update_slice_in_dim(full, arrived, jnp.where((j >= 0) & (j < n), j, n) * rows, 0)
-    return up, down, full
-
-
-def scatter_rows(part, j):
+    ups, downs = state[::2], state[1::2]
+    return jnp.concatenate([ups[0]] + [jnp.where(me + k < n, downs[k], ups[n - k]) for k in range(1, n)], axis=0)
+
+
+def scatter_steps(state, part, steps):
     n = lax.axis_size(AXIS)
     rows = part.shape[0] // n
-    return lax.dynamic_slice_in_dim(part, jnp.clip(j, 0, n - 1) * rows, rows, 0).astype(jnp.float32)
-
-
-def scatter_steps(state, part, steps):
-    n, me = lax.axis_size(AXIS), lax.axis_index(AXIS)
     for t in steps:
-        mine = scatter_rows(part, me + n - 1 - t), scatter_rows(part, me - n + 1 + t)
+        mine = [part[k * rows : (k + 1) * rows].astype(jnp.float32) for k in (n - 1 - t, 1 + t)]
         if t:
-            mine = [rows + sums.astype(jnp.float32) for rows, sums in zip(mine, state)]
-        state = tuple(
-            lax.ppermute(sums.astype(part.dtype), AXIS, hops(way)) for sums, way in zip(mine, (True, False))
-        )
+            mine = [own + sums.astype(jnp.float32) for own, sums in zip(mine, state)]
+        state = [lax.ppermute(sums.astype(part.dtype), AXIS, hops(way)) for sums, way in zip(mine, (True, False))]
     return state
+
+
+def line_sum(value):
+    n, step = lax.axis_size(AXIS), 1
+    while step < n:
+        value = value + lax.ppermute(value, AXIS, [(i, i ^ step) for i in range(n)])
+        step *= 2
+    return value
 
 
 def shards(tokens,
@@ -499,48 +824,43 @@
     def gather(own):
         return lax.all_gather(own, "dp", axis=0, tiled=True)
 
-    def scaled(gain, weight):
-        return (weight.astype(jnp.float32) * gain).astype(jnp.bfloat16)
-
     def scatter(grad):
         return lax.psum_scatter(grad, "dp", scatter_dimension=0, tiled=True)
 
-    def by_head(query, key, value, gate):
-        parts = []
-        for head in range(heads):
-            for array, columns in ((query, KD), (key, KD), (value, VD), (gate, VD)):
-                parts.append(array[:, head * columns : (head + 1) * columns])
-        return jnp.concatenate(parts, axis=1)
-
-    def from_heads(array):
-        found, at = ([], [], [], []), 0
-        for _ in range(heads):
-            for where, columns in zip(found, (KD, KD, VD, VD)):
-                where.append(array[:, at : at + columns])
-                at += columns
-        return [jnp.concatenate(parts, axis=1) for parts in found]
-
-    w_in_own = by_head(*[scaled(gain_one, w) for w in (w_query, w_key, w_value, w_gate)])
-    w_pair_own = jnp.concatenate([scaled(gain_two, w) for w in (w_mlp_gate, w_mlp_up)], axis=1)
-    mlp_own = jnp.concatenate([w_pair_own, w_down], axis=1)
-    inputs = tokens.astype(jnp.float32)
-    unit_own = (inputs * inverse_rms(inputs)).astype(jnp.bfloat16)
+    def gain_terms(weights, grads):
+        return jnp.sum(weights.astype(jnp.float32) * grads.astype(jnp.float32), axis=1)
+
+    in_parts = [(array, head, columns) for head in range(heads) for array, columns in enumerate((KD, KD, VD, VD))]
+    w_in_own = joined("join_in", [w_query, w_key, w_value, w_gate], gain_one, in_parts)
+    mlp_own = joined("join_mlp", [w_mlp_gate, w_mlp_up, w_down], gain_two, [(i, 0, hidden_cols) for i in range(3)], 1)
     w_in = gather(w_in_own)
     (unit_one,) = line_pass(
-        "gather_one", None, [unit_own], [], lambda cut, _, ins, outs: ins[0][cut], True, 4, 0, local_rows, width
+        "gather_one", None, [tokens], [], unit_step, True, 4, 0, local_rows, width
     )
-    w_in, unit_one, w_out, cot_own = after((w_in, unit_one, w_out, cotangent))
+    w_in, unit_one, w_out, cot_own, mlp_own = after((w_in, unit_one, w_out, cotangent, mlp_own))
     out_full = gather(w_out)
-    cot = gather_steps(gather_start(cot_own), steps_of(0, 3))
+    cot = gather_steps([cot_own, cot_own], steps_of(0, 3))
     projected = dot(unit_one, w_in)
     projected, *cot = after((projected, *cot))
     cot = gather_steps(cot, steps_of(1, 3))
     kept, mixed = retention(projected, segments, heads)
-    part_out = dot(mixed, out_full, CONTRACT_COLUMNS).astype(jnp.bfloat16)
-    part_out, mlp_own, *cot = after((part_out, mlp_own, *cot))
-    mlp_full = gather(mlp_own)
-    unit_two, residual = line_pass(
-        "residual", part_out, [tokens], [jnp.float32], residual_step, True, 16, 1, local_rows, width
+    mixed, out_full, mlp_send, *cot = after((mixed, out_full, mlp_own, *cot))
+    mlp_full = gather(mlp_send)
+    unit_two, residual, unit_turned = line_pass(
+        "residual",
+        (mixed, out_full),
+        [tokens],
+        [jnp.float32],
+        residual_step,
+        True,
+        16,
+        1,
+        local_rows,
+        width,
+        (False, True),
+        square=functools.partial(turn_parts, 8),
+        square_ins=[unit_one],
+        square_outs=[jax.ShapeDtypeStruct(unit_one.shape[::-1], unit_one.dtype)],
     )
     unit_two, mlp_full, *cot = after((unit_two, mlp_full, *cot))
     w_pair, down_full = mlp_full[:, : 2 * hidden_cols], mlp_full[:, 2 * hidden_cols :]
@@ -550,8 +870,8 @@
     hidden_gate, hidden_up = both_hidden[:, :hidden_cols], both_hidden[:, hidden_cols:]
     hidden = (jax.nn.gelu(hidden_gate, approximate=True) * hidden_up).astype(jnp.bfloat16)
     part_down = dot(hidden, down_full, CONTRACT_COLUMNS).astype(jnp.bfloat16)
-    part_down, cot_full = after((part_down, cot[2]))
-    cot_full = cot_full[: unit_two.shape[0]]
+    part_down, *cot = after((part_down, *cot))
+    cot_full = gather_end(cot)
 
     sums = scatter_steps(None, part_down, steps_of(0, 3))
     grad_down = dot(cot_full, hidden, CONTRACT_ROWS).astype(jnp.bfloat16)
@@ -563,48 +883,57 @@
     )
     d_pair = jnp.concatenate(gelu_pull(d_hidden), axis=1).astype(jnp.bfloat16)
     d_pair, grad_down, *sums = after((d_pair, grad_down, *sums))
+    down_grad = scatter(grad_down)
     sums = scatter_steps(sums, part_down, steps_of(1, 3))
     grad_pair = dot(unit_two, d_pair, CONTRACT_ROWS).astype(jnp.bfloat16)
-    part_pair = dot(d_pair, w_pair, CONTRACT_COLUMNS).astype(jnp.bfloat16)
-    part_pair, grad_pair, grad_down, *sums = after((part_pair, grad_pair, grad_down, *sums))
+    d_pair, grad_pair, *sums = after((d_pair, grad_pair, *sums))
     pair_grad = scatter(grad_pair)
     d_branch_one, d_residual = line_pass(
-        "d_residual", part_pair, [residual, cotangent], [jnp.float32], d_residual_step, True, 16, 2, local_rows, width
+        "d_residual", (d_pair, mlp_full), [residual, cotangent], [jnp.float32], d_residual_step, True, 16, 2, local_rows, width, (True, False)
     )
-    d_branch_one, d_residual, pair_grad, grad_down, *sums = after((d_branch_one, d_residual, pair_grad, grad_down, *sums))
-
-    down_grad = scatter(grad_down)
+    d_branch_one, d_residual, pair_grad, down_grad, *sums = after((d_branch_one, d_residual, pair_grad, down_grad, *sums))
+
     sums = scatter_steps(sums, part_down, steps_of(2, 3))
     grad_out = dot(d_branch_one, mixed, CONTRACT_ROWS).astype(jnp.bfloat16)
     out_grad = scatter(grad_out)
-    d_mixed = dot(d_branch_one, out_full)
-    d_in = retention_pull(kept, projected, d_mixed, segments, heads)
-    grad_in = dot(unit_one, d_in, CONTRACT_ROWS).astype(jnp.bfloat16)
-    result = residual + sum(sums_in.astype(jnp.float32) for sums_in in sums) + scatter_rows(part_down, lax.axis_index(AXIS))
+    d_in = retention_pull(kept, projected, d_branch_one, out_full, segments, heads)
+    result = residual + part_down[:local_rows].astype(jnp.float32) + sum(arrived.astype(jnp.float32) for arrived in sums)
     result = result.astype(jnp.bfloat16)
-    d_in, grad_in, result = after((d_in, grad_in, result))
-    in_grad = scatter(grad_in)
-    part_in = dot(d_in, w_in, CONTRACT_COLUMNS).astype(jnp.bfloat16)
-    (tokens_grad,) = line_pass(
-        "tokens_grad", part_in, [tokens, d_residual], [jnp.bfloat16], tokens_step, False, 8, 3, local_rows, width
+    gain_sum_two = line_sum(gain_terms(mlp_own[:, : 2 * hidden_cols], pair_grad)) / gain_two[:, 0]
+    pair_grad = pair_grad.astype(jnp.float32) * gain_two
+    gate_grad, up_grad = pair_grad[:, :hidden_cols], pair_grad[:, hidden_cols:]
+    down_grad = down_grad.astype(jnp.float32)
+    d_in, result, gain_sum_two, gate_grad, up_grad, down_grad = after(
+        (d_in, result, gain_sum_two, gate_grad, up_grad, down_grad)
     )
-
-    def gain_terms(weights, grads):
-        return jnp.sum(weights.astype(jnp.float32) * grads.astype(jnp.float32), axis=1)
-
-    gain_sums = lax.psum((gain_terms(w_in_own, in_grad), gain_terms(w_pair_own, pair_grad)), AXIS)
-    in_grads = [grad.astype(jnp.float32) * gain_one for grad in from_heads(in_grad)]
-    pair_grad = pair_grad.astype(jnp.float32) * gain_two
+    square_outs, square_scratch = square_shapes(gain_one.shape[0], heads, w_in.shape[1])
+    tokens_grad, gain_sum_one, *in_grads = line_pass(
+        "tokens_grad",
+        (d_in, w_in),
+        [tokens, d_residual],
+        [jnp.bfloat16],
+        tokens_step,
+        False,
+        8,
+        3,
+        local_rows,
+        width,
+        square=functools.partial(square_parts, heads),
+        square_ins=[unit_turned, gain_one, w_in_own],
+        square_outs=square_outs,
+        square_scratch=square_scratch,
+    )
+    gain_sum_one = gain_sum_one[:, 0] / gain_one[:, 0]
     return (
         result,
         tokens_grad,
-        gain_sums[0] / gain_one[:, 0],
+        gain_sum_one,
         *in_grads,
         out_grad.astype(jnp.float32),
-        gain_sums[1] / gain_two[:, 0],
-        pair_grad[:, :hidden_cols],
-        pair_grad[:, hidden_cols:],
-        down_grad.astype(jnp.float32),
+        gain_sum_two,
+        gate_grad,
+        up_grad,
+        down_grad,
     )
 
 

time: 732 us -> 651 us (0.89)
  matrix products: 150 us -> 78.6 us
  Pallas kernels: 395 us -> 440 us
  waiting for transfers between devices: 48.3 us -> 14.3 us
  other arithmetic: 38.9 us -> 25.6 us
  blocking collectives: 11.7 us -> 0 us
  starting transfers between devices: 33.7 us -> 42.8 us
    dot_general x12 -> x7, matrix products: 150 us -> 78.6 us  [dot(): lax.dot_general(left, right, dims, preferred_element_type=jnp.float32)]
    pallas_call x4 -> x6, Pallas kernels: 365 us -> 407 us  [the longest x4 404 us: line_pass(): pl.pallas_call(functools.partial(line_body, n, chunks, rs, ag, rolled, mi...]
    reduce_scatter x4 -> x3, waiting for transfers between devices: 36.7 us -> 0.04 us  [scatter(): return lax.psum_scatter(grad, 'dp', scatter_dimension=0, tiled=True)]
    dynamic_update_slice x7 -> x0, local copies, waits for them, and re-layouts: 11.8 us -> none  [the longest x6 10.8 us: gather_steps(): lax.dynamic_update_slice_in_dim(full, arrived, jnp.where((j >= 0) & (j <...]
    psum x1 -> x0, blocking collectives: 11.7 us -> none  [shards(): lax.psum((gain_terms(w_in_own, in_grad), gain_terms(w_pair_own, pair_grad...]
    unnamed x76 -> x75, local copies, waits for them, and re-layouts: 11.6 us -> 21.6 us
  transfers between devices with their start and end apart: 19 -> 20, of which waited for: 5 -> 6; matrix products, arithmetic and copies ran while one was open for 23% -> 15% of each run, Pallas kernels for 55% -> 68%
where the time goes in v3:
time: 651 us; the launch traced here: 643 us
  Pallas kernels  440 us (68%)
  matrix products  78.6 us (12%)
  starting transfers between devices  42.8 us (7%)
  local copies, waits for them, and re-layouts  26.4 us (4%)
  other arithmetic  25.6 us (4%)
  between operations  14.9 us (2%)
  waiting for transfers between devices  14.3 us (2%)
    pallas_call x4, Pallas kernels, line_pass(): pl.pallas_call(functools.partial(line_body, n, chunks, rs, ag, rolled, mi...  404 us
    dot_general x7, matrix products, dot(): lax.dot_general(left, right, dims, preferred_element_type=jnp.float32)  78.6 us
    pallas_call x1, Pallas kernels, retention_pull(): pl.pallas_call(functools.partial(retention_pull_body, block, reach), grid...  22.2 us
    unnamed x75, local copies, waits for them, and re-layouts  21.6 us
    ppermute x6, starting transfers between devices, scatter_steps(): lax.ppermute(sums.astype(part.dtype), AXIS, hops(way))  19.8 us
    ppermute x3, starting transfers between devices, gather_steps(): lax.ppermute(up, AXIS, hops(True))  13.6 us
  transfers between devices with their start and end apart: 20, of which 6 were waited for; matrix products, arithmetic and copies ran while one was open for 15% of the time, Pallas kernels for 68%

profile of v3, /device:TPU:0, one launch (start us, length us, event | category | flops | bytes accessed | tf_op | source)
XLA Modules:
  0.0 642.7 jit_solution(14114011818714796611)
XLA Ops:
  12.1 1.6 join_in.1.refs_6_
  13.9 73.1 %gather_one.1.refs_3_ = bf16[1024,2048]{1,0:T(8,128)(2,1)S(1)} custom-call(bf16[256,2048]{1,0:T(8,128)(2,1)S(1)} %copy-done.1), custom_call_target="tpu_custom_call" | custom-call | bytes 125829120 | tf_op jit(solution)/shard_map/gather_one/pallas_call | solution.py:279
  87.1 2.0 copy-done
  91.2 1.4 join_mlp.1
  92.7 1.4 collective-permute-start.1
  94.2 5.5 collective-permute-start
  99.7 19.2 %fusion.19.proj.gate = f32[1024,3072]{1,0:T(8,128)} fusion(bf16[1024,2048]{1,0:T(8,128)(2,1)} %copy-done, bf16[2048,3072]{1,0:T(8,128)(2,1)} %all-gather.4.cloned.1.call-done.refs_1_), kind=kOutput, calls=%fused_computation.44 | convolution fusion | flops 12884901888 | bytes 29360128 | tf_op jit(solution)/shard_map/dot_general | solution.py:539
  120.1 5.5 collective-permute-start.2
  125.5 1.3 collective-permute-start.3
  127.1 11.3 %retention.1 = (bf16[1024,2048]{1,0:T(8,128)(2,1)}, bf16[1024,1024]{1,0:T(8,128)(2,1)S(1)}) custom-call(f32[2]{0:T(128)S(1)} %subtract_log_fusion.log_ref, f32[1024,3072]{1,0:T(8,128)} %fusion.19.proj.gate, f32[1024,128]{1,0:T(8,128)S(1)} %copy-done.4, f32[1024,128]{1,0:T(8,128)S(1)} %copy-done.3, s32[1024,1]{1,0:T(8,128)S(1)} %copy.33.seg_rows, ...), custom_call_target="tpu_custom_call" | custom-call | flops 2415919104 | bytes 18874368 | tf_op jit(solution)/shard_map/retention/pallas_call | solution.py:634
  138.5 1.5 copy-done.5
  139.9 5.4 collective-permute-done.2
  145.3 5.1 collective-permute-done.3
  150.5 115.1 %residual.1 = (bf16[1024,2048]{1,0:T(8,128)(2,1)}, f32[256,2048]{1,0:T(8,128)}, bf16[2048,1024]{1,0:T(8,128)(2,1)}) custom-call(bf16[1024,1024]{1,0:T(8,128)(2,1)} %copy-done.5, bf16[2048,1024]{1,0:T(8,128)(2,1)} %all-gather.6.cloned.1.call-done.refs_1_.w_out, bf16[256,2048]{1,0:T(8,128)(2,1)} %refs_2_.7, bf16[1024,2048]{1,0:T(8,128)(2,1)} %copy-done), custom_call_target="tpu_custom_call" | custom-call | bytes 125829120 | tf_op jit(solution)/shard_map/residual/pallas_call | solution.py:279
  265.7 2.6 collective-permute-start.4
  268.2 1.6 collective-permute-start.5
  269.8 12.6 %fusion = f32[1024,2048]{1,0:T(8,128)S(1)} fusion(bf16[1024,2048]{1,0:T(8,128)(2,1)} %get-tuple-element.97, bf16[2048,3072]{1,0:T(8,128)(2,1)} %all-gather.8.cloned.1.call-done.refs_1_), kind=kOutput, calls=%fused_computation | convolution fusion | flops 8589934592 | bytes 20971520 | tf_op jit(solution)/shard_map/dot_general | solution.py:539
  282.5 3.3 copy-done.21
  285.8 1.5 multiply_convert_fusion.1
  287.3 4.8 convolution_convert_fusion.3
  292.1 1.6 fusion.17
  293.7 1.3 collective-permute-start.7
  295.0 6.8 %collective-permute-start.6 = (bf16[256,2048]{1,0:T(8,128)(2,1)}, bf16[256,2048]{1,0:T(8,128)(2,1)}, u32[]{:S(2)}, u32[]{:S(2)}) collective-permute-start(bf16[256,2048]{1,0:T(8,128)(2,1)} %get-tuple-element.149), channel_id=1, source_target_pairs={{0,1},{1,2},{2,3},{4,5},{5,6},{6,7},{8,9},{9,10},{10,11},{12,13},{... | collective-permute-start | bytes 3145736 | tf_op jit(solution)/shard_map/ppermute | solution.py:790
  301.8 1.3 broadcast_select_fusion.2
  303.2 3.1 broadcast_select_fusion
  306.2 12.3 %fusion.8 = (bf16[1024,1024]{1,0:T(8,128)(2,1)S(1)}, bf16[1024,1024]{1,0:T(8,128)(2,1)}) fusion(f32[1024,2048]{1,0:T(8,128)} %copy-done.21, bf16[2048,3072]{1,0:T(8,128)(2,1)S(1)} %copy-done.17, bf16[256,2048]{1,0:T(8,128)(2,1)} %get-tuple-element.154, bf16[256,2048]{1,0:T(8,128)(2,1)} %get-tuple-element.155, ...), kind=kOutput, calls=%fused_computation.11 | convolution fusion | flops 4336910336 | bytes 20971520 | tf_op jit(solution)/shard_map/dot_general | solution.py:539
  318.6 4.2 pad_maximum_fusion.1.refs_0_
  322.8 6.3 convolution_convert_fusion.2
  329.2 4.1 fusion.13
  333.3 1.3 collective-permute-start.9
  334.6 5.7 collective-permute-start.8
  340.3 13.9 %convolution_convert_fusion = bf16[2048,2048]{1,0:T(8,128)(2,1)} fusion(bf16[1024,2048]{1,0:T(8,128)(2,1)} %get-tuple-element.97, bf16[1024,2048]{1,0:T(8,128)(2,1)S(1)} %copy-done.16), kind=kOutput, calls=%fused_computation.2 | convolution fusion | flops 8594128896 | bytes 16777216 | tf_op jit(solution)/shard_map/dot_general | solution.py:539
  354.2 1.3 collective-permute-done.9
  356.8 117.2 %d_residual.1 = (bf16[1024,2048]{1,0:T(8,128)(2,1)}, f32[256,2048]{1,0:T(8,128)}) custom-call(bf16[1024,2048]{1,0:T(8,128)(2,1)} %pad_maximum_fusion.1.refs_0_, bf16[2048,3072]{1,0:T(8,128)(2,1)} %all-gather.8.cloned.1.call-done.refs_1_, f32[256,2048]{1,0:T(8,128)} %get-tuple-element.116.refs_2_, bf16[256,2048]{1,0:T(8,128)(2,1)S(1)} %copy-done.8), custom_call_target="tpu_custom_call" | custom-call | bytes 125829120 | tf_op jit(solution)/shard_map/d_residual/pallas_call | solution.py:279
  474.0 9.4 %convolution_convert_fusion.1 = bf16[2048,1024]{1,0:T(8,128)(2,1)} fusion(bf16[1024,2048]{1,0:T(8,128)(2,1)} %get-tuple-element.123.d_branch, bf16[1024,1024]{1,0:T(8,128)(2,1)} %copy-done.5), kind=kOutput, calls=%fused_computation.17 | convolution fusion | flops 4297064448 | bytes 10485760 | tf_op jit(solution)/shard_map/dot_general | solution.py:539
  483.5 1.2 copy-done.26
  484.7 1.9 convert_multiply_fusion
  487.2 2.7 add_convert_fusion.2
  489.9 3.2 collective-permute-start.10
  493.1 1.5 collective-permute-start.11
  494.6 22.2 %retention_pull.1.refs_0_ = bf16[1024,3072]{1,0:T(8,128)(2,1)} custom-call(f32[2]{0:T(128)S(1)} %subtract_log_fusion.log_ref, bf16[1024,2048]{1,0:T(8,128)(2,1)S(1)} %copy-done.2, f32[1024,3072]{1,0:T(8,128)} %fusion.19.proj.gate, bf16[1024,2048]{1,0:T(8,128)(2,1)} %get-tuple-element.123.d_branch, ...), custom_call_target="tpu_custom_call" | custom-call | flops 7247757312 | bytes 25165824 | tf_op jit(solution)/shard_map/retention_pull/pallas_call | solution.py:674
  516.9 4.9 collective-permute-start.13
  521.8 1.6 fusion.18
  525.0 1.7 add_convert_fusion
  526.7 98.1 %tokens_grad.1 = (bf16[256,2048]{1,0:T(8,128)(2,1)}, f32[256,128]{1,0:T(8,128)}, f32[256,512]{1,0:T(8,128)}, f32[256,512]{1,0:T(8,128)}, f32[256,1024]{1,0:T(8,128)}, /*index=5*/f32[256,1024]{1,0:T(8,128)}) custom-call(bf16[1024,3072]{1,0:T(8,128)(2,1)} %retention_pull.1.refs_0_, bf16[2048,3072]{1,0:T(8,128)(2,1)} %all-gather.4.cloned.1.call-done.refs_1_, ...), custom_call_target="tpu_custom_call" | custom-call | bytes 125829120 | tf_op jit(solution)/shard_map/tokens_grad/pallas_call | solution.py:279
  626.6 2.1 convert_element_type.115
  628.7 2.3 copy.44
  631.0 1.9 copy.45
  (112 shorter events, 16.9 us)
Async XLA Ops:
  7.2 6.8 %copy-start.1 = (bf16[256,2048]{1,0:T(8,128)(2,1)S(1)}, bf16[256,2048]{1,0:T(8,128)(2,1)}, u32[]{:S(2)}) copy-start(bf16[256,2048]{1,0:T(8,128)(2,1)} %refs_2_.7) | copy-start | bytes 3145732
  7.2 85.4 %all-gather.4.cloned.1.call-start = ((), (), s32[]{:S(2)}) async-start(), calls=%async_computation.3 | async-start | bytes 14155776 | tf_op jit(solution)/shard_map/all_gather | solution.py:825
  12.1 74.9 %copy-start.6 = (f32[256,1]{1,0:T(8,128)}, f32[256,1]{1,0:T(8,128)S(1)}, u32[]{:S(2)}) copy-start(f32[256,1]{1,0:T(8,128)S(1)} %copy.31.refs_4_.refs_5_) | copy-start | bytes 3076
  12.1 1.7 copy-start.32
  13.7 75.4 %copy-start.11 = (bf16[256,1024]{1,0:T(8,128)(2,1)S(1)}, bf16[256,1024]{1,0:T(8,128)(2,1)}, u32[]{:S(2)}) copy-start(bf16[256,1024]{1,0:T(8,128)(2,1)} %refs_0_.5) | copy-start | bytes 1572868
  13.7 136.7 %all-gather.6.cloned.1.call-start = ((), (), s32[]{:S(2)}) async-start(), calls=%async_computation.4 | async-start | bytes 4718592 | tf_op jit(solution)/shard_map/all_gather | solution.py:825
  13.9 78.8 %copy-start.7 = (bf16[256,2048]{1,0:T(8,128)(2,1)S(1)}, bf16[256,2048]{1,0:T(8,128)(2,1)}, u32[]{:S(2)}) copy-start(bf16[256,2048]{1,0:T(8,128)(2,1)} %refs_3_.3) | copy-start | bytes 3145732
  87.1 2.0 copy-start
  92.6 34.2 %copy-start.31 = (s32[1,1024]{1,0:T(1,128)S(1)}, s32[1,1024]{1,0:T(1,128)}, u32[]{:S(2)}) copy-start(s32[1,1024]{1,0:T(1,128)} %param.18) | copy-start | bytes 12292
  92.7 34.5 %copy-start.3 = (f32[1024,128]{1,0:T(8,128)S(1)}, f32[1024,128]{1,0:T(8,128)}, u32[]{:S(2)}) copy-start(f32[1024,128]{1,0:T(8,128)} %constant.38.clone.sine) | copy-start | bytes 1572868
  92.7 34.5 %copy-start.4 = (f32[1024,128]{1,0:T(8,128)S(1)}, f32[1024,128]{1,0:T(8,128)}, u32[]{:S(2)}) copy-start(f32[1024,128]{1,0:T(8,128)} %constant.37.clone.cosine) | copy-start | bytes 1572868
  92.7 173.0 %all-gather.8.cloned.1.call-start = ((), (), s32[]{:S(2)}) async-start(), calls=%async_computation.5 | async-start | bytes 14155776 | tf_op jit(solution)/shard_map/all_gather | solution.py:825
  92.7 26.3 %collective-permute-start.1 = (bf16[256,2048]{1,0:T(8,128)(2,1)S(1)}, bf16[256,2048]{1,0:T(8,128)(2,1)}, u32[]{:S(2)}, u32[]{:S(2)}) collective-permute-start(bf16[256,2048]{1,0:T(8,128)(2,1)S(1)} %copy-done.7), channel_id=1, source_target_pairs={{1,0},{2,1},{3,2},{5,4},{6,5},{7,6},{9,8},{10,9},{11,10},{13,12},{... | collective-permute-start | bytes 3145736 | tf_op jit(solution)/shard_map/ppermute | solution.py:773
  94.2 25.9 %collective-permute-start = (bf16[256,2048]{1,0:T(8,128)(2,1)S(1)}, bf16[256,2048]{1,0:T(8,128)(2,1)}, u32[]{:S(2)}, u32[]{:S(2)}) collective-permute-start(bf16[256,2048]{1,0:T(8,128)(2,1)S(1)} %copy-done.7), channel_id=1, source_target_pairs={{0,1},{1,2},{2,3},{4,5},{5,6},{6,7},{8,9},{9,10},{10,11},{12,13},{... | collective-permute-start | bytes 3145736 | tf_op jit(solution)/shard_map/ppermute | solution.py:773
  120.1 25.2 %collective-permute-start.2 = (bf16[256,2048]{1,0:T(8,128)(2,1)}, bf16[256,2048]{1,0:T(8,128)(2,1)}, u32[]{:S(2)}, u32[]{:S(2)}) collective-permute-start(bf16[256,2048]{1,0:T(8,128)(2,1)} %collective-permute-done), channel_id=1, source_target_pairs={{0,1},{1,2},{2,3},{4,5},{5,6},{6,7},{8,9},{9,10},{10,11},{12,13},{... | collective-permute-start | bytes 3145736 | tf_op jit(solution)/shard_map/ppermute | solution.py:773
  125.5 24.8 %collective-permute-start.3 = (bf16[256,2048]{1,0:T(8,128)(2,1)}, bf16[256,2048]{1,0:T(8,128)(2,1)}, u32[]{:S(2)}, u32[]{:S(2)}) collective-permute-start(bf16[256,2048]{1,0:T(8,128)(2,1)} %collective-permute-done.1), channel_id=1, source_target_pairs={{1,0},{2,1},{3,2},{5,4},{6,5},{7,6},{9,8},{10,9},{11,10},{13,12},{... | collective-permute-start | bytes 3145736 | tf_op jit(solution)/shard_map/ppermute | solution.py:773
  138.5 1.5 copy-start.5
  150.4 323.6 %reduce-scatter.6.cloned.1.call-start = ((), (), s32[]{:S(2)}) async-start(), calls=%async_computation.7 | async-start | bytes 4718592 | tf_op jit(solution)/shard_map/reduce_scatter | solution.py:828
  265.7 26.4 %collective-permute-start.4 = (bf16[256,2048]{1,0:T(8,128)(2,1)}, bf16[256,2048]{1,0:T(8,128)(2,1)}, u32[]{:S(2)}, u32[]{:S(2)}) collective-permute-start(bf16[256,2048]{1,0:T(8,128)(2,1)} %collective-permute-done.2), channel_id=1, source_target_pairs={{0,1},{1,2},{2,3},{4,5},{5,6},{6,7},{8,9},{9,10},{10,11},{12,13},{... | collective-permute-start | bytes 3145736 | tf_op jit(solution)/shard_map/ppermute | solution.py:773
  268.2 23.9 %collective-permute-start.5 = (bf16[256,2048]{1,0:T(8,128)(2,1)}, bf16[256,2048]{1,0:T(8,128)(2,1)}, u32[]{:S(2)}, u32[]{:S(2)}) collective-permute-start(bf16[256,2048]{1,0:T(8,128)(2,1)} %collective-permute-done.3), channel_id=1, source_target_pairs={{1,0},{2,1},{3,2},{5,4},{6,5},{7,6},{9,8},{10,9},{11,10},{13,12},{... | collective-permute-start | bytes 3145736 | tf_op jit(solution)/shard_map/ppermute | solution.py:773
  269.8 17.4 %copy-start.17 = (bf16[2048,3072]{1,0:T(8,128)(2,1)S(1)}, bf16[2048,3072]{1,0:T(8,128)(2,1)}, u32[]{:S(2)}) copy-start(bf16[2048,3072]{1,0:T(8,128)(2,1)} %all-gather.8.cloned.1.call-done.refs_1_) | copy-start | bytes 37748740
  282.5 3.3 copy-start.21
  287.3 4.8 copy-start.22
  292.1 2.9 copy-start.18
  293.7 35.4 %collective-permute-start.7 = (bf16[256,2048]{1,0:T(8,128)(2,1)}, bf16[256,2048]{1,0:T(8,128)(2,1)}, u32[]{:S(2)}, u32[]{:S(2)}) collective-permute-start(bf16[256,2048]{1,0:T(8,128)(2,1)} %get-tuple-element.148), channel_id=1, source_target_pairs={{1,0},{2,1},{3,2},{5,4},{6,5},{7,6},{9,8},{10,9},{11,10},{13,12},{... | collective-permute-start | bytes 3145736 | tf_op jit(solution)/shard_map/ppermute | solution.py:790
  295.0 11.3 %copy-start.8 = (bf16[256,2048]{1,0:T(8,128)(2,1)S(1)}, bf16[256,2048]{1,0:T(8,128)(2,1)}, u32[]{:S(2)}) copy-start(bf16[256,2048]{1,0:T(8,128)(2,1)} %refs_3_.3) | copy-start | bytes 3145732
  295.0 34.1 %collective-permute-start.6 = (bf16[256,2048]{1,0:T(8,128)(2,1)}, bf16[256,2048]{1,0:T(8,128)(2,1)}, u32[]{:S(2)}, u32[]{:S(2)}) collective-permute-start(bf16[256,2048]{1,0:T(8,128)(2,1)} %get-tuple-element.149), channel_id=1, source_target_pairs={{0,1},{1,2},{2,3},{4,5},{5,6},{6,7},{8,9},{9,10},{10,11},{12,13},{... | collective-permute-start | bytes 3145736 | tf_op jit(solution)/shard_map/ppermute | solution.py:790
  318.6 4.3 copy-start.23
  318.6 4.3 copy-start.27
  318.6 4.3 copy-start.28
  329.2 144.9 %reduce-scatter.4.cloned.1.call-start = ((), (), s32[]{:S(2)}) async-start(), calls=%async_computation.6 | async-start | bytes 9437184 | tf_op jit(solution)/shard_map/reduce_scatter | solution.py:828
  329.2 11.1 %copy-start.16 = (bf16[1024,2048]{1,0:T(8,128)(2,1)S(1)}, bf16[1024,2048]{1,0:T(8,128)(2,1)}, u32[]{:S(2)}) copy-start(bf16[1024,2048]{1,0:T(8,128)(2,1)} %pad_maximum_fusion.1.refs_0_) | copy-start | bytes 12582916
  333.3 22.3 %collective-permute-start.9 = (bf16[256,2048]{1,0:T(8,128)(2,1)}, bf16[256,2048]{1,0:T(8,128)(2,1)}, u32[]{:S(2)}, u32[]{:S(2)}) collective-permute-start(bf16[256,2048]{1,0:T(8,128)(2,1)} %get-tuple-element.146), channel_id=1, source_target_pairs={{1,0},{2,1},{3,2},{5,4},{6,5},{7,6},{9,8},{10,9},{11,10},{13,12},{... | collective-permute-start | bytes 3145736 | tf_op jit(solution)/shard_map/ppermute | solution.py:790
  334.6 22.2 %collective-permute-start.8 = (bf16[256,2048]{1,0:T(8,128)(2,1)}, bf16[256,2048]{1,0:T(8,128)(2,1)}, u32[]{:S(2)}, u32[]{:S(2)}) collective-permute-start(bf16[256,2048]{1,0:T(8,128)(2,1)} %get-tuple-element.147), channel_id=1, source_target_pairs={{0,1},{1,2},{2,3},{4,5},{5,6},{6,7},{8,9},{9,10},{10,11},{12,13},{... | collective-permute-start | bytes 3145736 | tf_op jit(solution)/shard_map/ppermute | solution.py:790
  356.7 269.9 %reduce-scatter.8.cloned.1.call-start = ((), (), s32[]{:S(2)}) async-start(), calls=%async_computation.8 | async-start | bytes 4718592 | tf_op jit(solution)/shard_map/reduce_scatter | solution.py:828
  484.7 2.5 copy-start.19
  486.6 8.0 %copy-start.2 = (bf16[1024,2048]{1,0:T(8,128)(2,1)S(1)}, bf16[1024,2048]{1,0:T(8,128)(2,1)}, u32[]{:S(2)}) copy-start(bf16[1024,2048]{1,0:T(8,128)(2,1)} %get-tuple-element.81.kept) | copy-start | bytes 12582916
  486.6 30.3 %collective-permute-start.12 = (f32[256]{0:T(256)S(1)}, f32[256]{0:T(256)S(1)}, u32[]{:S(2)}, u32[]{:S(2)}) collective-permute-start(f32[256]{0:T(256)S(1)} %get-tuple-element.153), channel_id=1, source_target_pairs={{0,1},{1,0},{2,3},{3,2},{4,5},{5,4},{6,7},{7,6},{8,9},{9,8},{10,11... | collective-permute-start | bytes 3080 | tf_op jit(solution)/shard_map/ppermute | solution.py:797
  489.9 35.1 %collective-permute-start.10 = (bf16[256,2048]{1,0:T(8,128)(2,1)S(1)}, bf16[256,2048]{1,0:T(8,128)(2,1)S(1)}, u32[]{:S(2)}, u32[]{:S(2)}) collective-permute-start(bf16[256,2048]{1,0:T(8,128)(2,1)S(1)} %get-tuple-element.144), channel_id=1, source_target_pairs={{0,1},{1,2},{2,3},{4,5},{5,6},{6,7},{8,9},{9,10},{10,11},{12,13},{... | collective-permute-start | bytes 3145736 | tf_op jit(solution)/shard_map/ppermute | solution.py:790
  493.1 31.9 %collective-permute-start.11 = (bf16[256,2048]{1,0:T(8,128)(2,1)S(1)}, bf16[256,2048]{1,0:T(8,128)(2,1)S(1)}, u32[]{:S(2)}, u32[]{:S(2)}) collective-permute-start(bf16[256,2048]{1,0:T(8,128)(2,1)S(1)} %get-tuple-element.145), channel_id=1, source_target_pairs={{1,0},{2,1},{3,2},{5,4},{6,5},{7,6},{9,8},{10,9},{11,10},{13,12},{... | collective-permute-start | bytes 3145736 | tf_op jit(solution)/shard_map/ppermute | solution.py:790
  516.8 6.5 %copy-start.29 = (bf16[256,1024]{1,0:T(8,128)(2,1)S(1)}, bf16[256,1024]{1,0:T(8,128)(2,1)}, u32[]{:S(2)}) copy-start(bf16[256,1024]{1,0:T(8,128)(2,1)} %reduce-scatter.6.cloned.1.call-done) | copy-start | bytes 1572868
  516.8 7.6 %copy-start.33 = (bf16[256]{0:T(256)(128)(2,1)S(1)}, bf16[256]{0:T(256)(128)(2,1)}, u32[]{:S(2)}) copy-start(bf16[256]{0:T(256)(128)(2,1)} %param.25) | copy-start | bytes 1540
  516.9 8.2 %copy-start.20 = (f32[256,2048]{1,0:T(8,128)S(1)}, f32[256,2048]{1,0:T(8,128)}, u32[]{:S(2)}) copy-start(f32[256,2048]{1,0:T(8,128)} %get-tuple-element.116.refs_2_) | copy-start | bytes 6291460
  516.9 7.5 %collective-permute-start.13 = (f32[256]{0:T(256)S(1)}, f32[256]{0:T(256)S(1)}, u32[]{:S(2)}, u32[]{:S(2)}) collective-permute-start(f32[256]{0:T(256)S(1)} %add.75), channel_id=1, source_target_pairs={{0,2},{1,3},{2,0},{3,1},{4,6},{5,7},{6,4},{7,5},{8,10},{9,11},{10,... | collective-permute-start | bytes 3080 | tf_op jit(solution)/shard_map/ppermute | solution.py:797
  526.7 99.3 %copy-start.34 = (bf16[256]{0:T(256)(128)(2,1)S(1)}, bf16[256]{0:T(256)(128)(2,1)}, u32[]{:S(2)}) copy-start(bf16[256]{0:T(256)(128)(2,1)} %param.19) | copy-start | bytes 1540
  624.8 8.1 %copy-start.30 = (f32[256,512]{1,0:T(8,128)S(1)}, f32[256,512]{1,0:T(8,128)}, u32[]{:S(2)}) copy-start(f32[256,512]{1,0:T(8,128)} %get-tuple-element.172) | copy-start | bytes 1572868
  624.8 8.9 %copy-start.25 = (f32[256,1024]{1,0:T(8,128)S(1)}, f32[256,1024]{1,0:T(8,128)}, u32[]{:S(2)}) copy-start(f32[256,1024]{1,0:T(8,128)} %get-tuple-element.173) | copy-start | bytes 3145732
  624.9 9.8 %copy-start.24 = (f32[256,1024]{1,0:T(8,128)S(1)}, f32[256,1024]{1,0:T(8,128)}, u32[]{:S(2)}) copy-start(f32[256,1024]{1,0:T(8,128)} %get-tuple-element.174) | copy-start | bytes 3145732
  (7 other events, 7.3 us)
Sparse Core Ops, SparseCore 0:
  13.8 74.8 all-gather.3
  92.8 36.8 all-gather.5
  150.5 70.6 all-gather.7
  329.3 52.8 reduce-scatter.5
  385.8 71.2 reduce-scatter.3
  483.6 52.1 reduce-scatter.7

commit v4 on v3

--- a/solution.py
+++ b/solution.py
@@ -1,4 +1,5 @@
 import functools
+import math
 import jax
 import jax.numpy as jnp
 import numpy as np
@@ -10,6 +11,7 @@
 AXIS = "tensor"
 TALL = 256
 COLUMNS = 1024
+VMEM = 62 * 1024 * 1024
 
 
 def line_body(n, chunks, rs, ag, rolled, middle, square, n_in, n_out, *refs):
@@ -124,7 +126,7 @@
         @pl.when(me != first)
         def _():
             sum_copy(up, d, c).wait_recv()
-            buf[d - up, cut(c)] = (buf[d - up, cut(c)].astype(jnp.float32) + mine.astype(jnp.float32)).astype(buf.dtype)
+            buf[d - up, cut(c)] += mine
 
         sum_copy(up, d, c).start()
 
@@ -152,13 +154,14 @@
                 for copy in later_copies():
                     copy.wait()
 
+        also(s)
+        if rs:
             per_group = chunks // groups
 
             @pl.when((lax.rem(s, per_group) == 0) & (s + per_group < chunks))
             def _():
                 product(s // per_group + 1)
 
-        also(s)
         c_own = s - lag
 
         @pl.when((c_own >= 0) & (c_own < chunks))
@@ -283,7 +286,7 @@
         out_specs=specs,
         scratch_shapes=scratch + list(square_scratch),
         compiler_params=pltpu.CompilerParams(
-            collective_id=collective_id, has_side_effects=True, vmem_limit_bytes=(62 if square else 52 if rs else 16) * 1024 * 1024
+            collective_id=collective_id, has_side_effects=True, vmem_limit_bytes=VMEM
         ),
         cost_estimate=pl.CostEstimate(
             flops=0, bytes_accessed=moved * 40, transcendentals=0, remote_bytes_transferred=moved
@@ -297,16 +300,16 @@
 
 
 def square_parts(heads, left, ins, outs, scratch):
-    turned, gain, weights = ins
+    turned, gain, weights, other_terms = ins
     gain_sum, grads = outs[0], outs[1:]
-    sums, sums_in, sums_send, sums_recv, sent, own, *rest = scratch
+    terms_one, sums, sums_in, sums_send, sums_recv, sent, *rest = scratch
     line = lax.axis_index(AXIS)
     line_bits = lax.axis_size(AXIS).bit_length() - 1
     size = lax.axis_size("dp")
     bits = size.bit_length() - 1
-    arrived, (first_send, first_recv), sems = rest[:bits], rest[bits : bits + 2], rest[bits + 2 :]
+    arrived, sems = rest[:bits], rest[bits:]
     me = lax.axis_index("dp")
-    rows, wide = own.shape[2:]
+    rows, wide = sent.shape[-2:]
     half = wide // 2
     pairs = arrived[0].shape[0]
     orders = list(range(bits - 1)), list(range(bits - 1))[::-1]
@@ -338,37 +341,37 @@
             device_id_type=pl.DeviceIdType.MESH,
         )
 
-    def first_copy(p, u):
-        return send(sent.at[lax.rem(p, 2), u], arrived[0].at[p, u], first_send.at[p, u], first_recv.at[p, u], 0)
-
-    def kept(side, stage):
-        done = orders[side][: stage - 1]
-        return [u for u in range(size // 2) if all(not u >> bit & 1 for bit in done)]
-
-    def later_copies(p, side, stage):
-        bit = orders[side][stage - 1]
-        stay = kept(side, stage + 1)
-        columns = pl.ds(side * half, half)
-        send_sem, recv_sem = sems[2 * (stage - 1)], sems[2 * (stage - 1) + 1]
-        return [
-            send(
-                arrived[0].at[p, u | 1 << bit, :, columns],
-                arrived[stage].at[p, rank, :, columns],
-                send_sem.at[p, side, rank],
-                recv_sem.at[p, side, rank],
-                bit + 1,
-            )
-            for rank, u in enumerate(stay)
-        ]
+    def first_copy(p):
+        return send(sent.at[lax.rem(p, 2)], arrived[0].at[p], sems[0].at[p], sems[1].at[p], 0)
+
+    def places(side, stage, at):
+        found = [slice(None)] * (bits - 1)
+        for done in orders[side][: stage - 1]:
+            found[done] = 0
+        found[orders[side][stage - 1]] = at
+        return tuple(found)
+
+    def later_copy(p, side, stage):
+        columns = (slice(None), pl.ds(side * half, half))
+        return send(
+            arrived[0].at[(p, *places(side, stage, 1), *columns)],
+            arrived[stage].at[(p, *[slice(None)] * (bits - 1 - stage), *columns)],
+            sems[2 * stage].at[p, side],
+            sems[2 * stage + 1].at[p, side],
+            orders[side][stage - 1] + 1,
+        )
 
     def multiply(p, u, odd):
         owner = me
         for bit in range(bits):
-            set_bit = odd if bit == 0 else lax.rem(u // (1 << (bit - 1)), 2)
-            owner = owner + set_bit * (1 << bit) * (1 - 2 * lax.rem(me // (1 << bit), 2))
+            set_bit = odd if bit == 0 else u[bits - 1 - bit]
+            if set_bit:
+                owner = flipped(owner, bit)
         block = turned[pl.ds(pl.multiple_of(owner * rows, rows), rows)]
         columns = left[:, pl.ds(pl.multiple_of(p * wide, wide), wide)]
-        return jnp.dot(block, columns, preferred_element_type=jnp.float32).astype(own.dtype)
+        return jnp.dot(block, columns, preferred_element_type=jnp.float32)
+
+    blocks = [tuple(u >> bit & 1 for bit in range(bits - 1))[::-1] for u in range(size // 2)]
 
     def also(s):
         @pl.when(s < pairs)
@@ -377,20 +380,11 @@
 
             @pl.when(p >= 2)
             def _():
-                for u in range(size // 2):
-                    first_copy(p - 2, u).wait_send()
-
-            def to_send(u, _):
-                sent[lax.rem(p, 2), u] = multiply(p, u, 1)
-                first_copy(p, u).start()
-                return 0
-
-            def to_keep(u, _):
-                own[lax.rem(p, 2), u] = multiply(p, u, 0)
-                return 0
-
-            lax.fori_loop(0, size // 2, to_send, 0)
-            lax.fori_loop(0, size // 2, to_keep, 0)
+                first_copy(p - 2).wait_send()
+
+            for u in blocks:
+                sent[(lax.rem(p, 2), *u[::-1])] = multiply(p, u, 1).astype(sent.dtype)
+            first_copy(p).start()
 
         for stage in range(1, bits + 1):
 
@@ -398,26 +392,22 @@
             def _(stage=stage):
                 p = s - stage
                 if stage == 1:
-                    for u in range(size // 2):
-                        first_copy(p, u).wait_recv()
-                        summed = arrived[0][p, u].astype(jnp.float32) + own[lax.rem(p, 2), u].astype(jnp.float32)
-                        arrived[0][p, u] = summed.astype(own.dtype)
+                    first_copy(p).wait_recv()
+                    for u in blocks:
+                        at = (p, *u[::-1])
+                        arrived[0][at] = (multiply(p, u, 0) + arrived[0][at].astype(jnp.float32)).astype(sent.dtype)
                 for side in range(2):
-                    columns = pl.ds(side * half, half)
+                    columns = (slice(None), pl.ds(side * half, half))
                     if stage > 1:
-                        for copy in later_copies(p, side, stage - 1):
-                            copy.wait_recv()
-                        for rank, u in enumerate(kept(side, stage)):
-                            summed = arrived[0][p, u, :, columns].astype(jnp.float32) + arrived[stage - 1][
-                                p, rank, :, columns
-                            ].astype(jnp.float32)
-                            if stage < bits:
-                                arrived[0][p, u, :, columns] = summed.astype(own.dtype)
-                            else:
-                                result(p, side, summed)
+                        later_copy(p, side, stage - 1).wait_recv()
+                        at = (p, *places(side, stage - 1, 0), *columns)
+                        came = (p, *[slice(None)] * (bits - stage), *columns)
+                        if stage < bits:
+                            arrived[0][at] += arrived[stage - 1][came]
+                        else:
+                            result(p, side, arrived[0][at].astype(jnp.float32) + arrived[stage - 1][came].astype(jnp.float32))
                     if stage < bits:
-                        for copy in later_copies(p, side, stage):
-                            copy.start()
+                        later_copy(p, side, stage).start()
 
         for bit in range(line_bits + 1):
 
@@ -426,6 +416,9 @@
                 if bit:
                     sums_copy(bit - 1).wait()
                     sums[bit] = sums[bit - 1] + sums_in[bit - 1]
+                else:
+                    sums[0, 0] = terms_one[...].T[: sums.shape[2]]
+                    sums[0, 1] = other_terms[...].T[: sums.shape[2]]
                 if bit < line_bits:
                     sums_copy(bit).start()
                 else:
@@ -434,18 +427,18 @@
     def result(p, side, summed):
         at = pl.ds(pl.multiple_of(p * wide + side * half, half), half)
         terms = jnp.sum(summed * weights[:, at].astype(jnp.float32), axis=1, keepdims=True)
-        terms = jnp.broadcast_to(terms, sums.shape[1:])
+        terms = jnp.broadcast_to(terms, terms_one.shape)
         if side:
-            sums[0] += terms
+            terms_one[...] += terms
         else:
 
             @pl.when(p == 0)
             def _():
-                sums[0] = terms
+                terms_one[...] = terms
 
             @pl.when(p > 0)
             def _():
-                sums[0] += terms
+                terms_one[...] += terms
 
         summed = summed * gain[...]
         for found in range(pairs):
@@ -459,14 +452,12 @@
 
     def finish():
         for p in range(max(pairs - 2, 0), pairs):
-            for u in range(size // 2):
-                first_copy(p, u).wait_send()
+            first_copy(p).wait_send()
 
         def drain(p, _):
             for side in range(2):
                 for stage in range(1, bits):
-                    for copy in later_copies(p, side, stage):
-                        copy.wait_send()
+                    later_copy(p, side, stage).wait_send()
             return 0
 
         lax.fori_loop(0, pairs, drain, 0)
@@ -479,21 +470,23 @@
     bits = size.bit_length() - 1
     wide = 2 * KD
     pairs = columns // wide
-    sums = [pltpu.VMEM((pairs, size >> (stage + 1), rows, wide), jnp.bfloat16) for stage in range(bits)]
-    sems = [pltpu.SemaphoreType.DMA((pairs, size // 2))] * 2
-    for stage in range(1, bits):
-        sems += [pltpu.SemaphoreType.DMA((pairs, 2, size >> (stage + 1)))] * 2
-    outs = [jax.ShapeDtypeStruct((rows, 128), jnp.float32)]
+    twos = [2] * (bits - 1)
+    sums = [pltpu.VMEM((pairs, *twos[stage:], rows, wide), jnp.bfloat16) for stage in range(bits)]
+    sems = [pltpu.SemaphoreType.DMA((pairs,))] * 2
+    for _ in range(1, bits):
+        sems += [pltpu.SemaphoreType.DMA((pairs, 2))] * 2
+    outs = [jax.ShapeDtypeStruct((2, 8, rows), jnp.float32)]
     line_bits = lax.axis_size(AXIS).bit_length() - 1
     line_sems = pltpu.SemaphoreType.DMA((max(line_bits, 1),))
     line_scratch = [
-        pltpu.VMEM((line_bits + 1, rows, 128), jnp.float32),
-        pltpu.VMEM((max(line_bits, 1), rows, 128), jnp.float32),
+        pltpu.VMEM((rows, 128), jnp.float32),
+        pltpu.VMEM((line_bits + 1, 2, 8, rows), jnp.float32),
+        pltpu.VMEM((max(line_bits, 1), 2, 8, rows), jnp.float32),
         line_sems,
         line_sems,
     ]
     outs += [jax.ShapeDtypeStruct((rows, heads * cols), jnp.float32) for cols in (KD, KD, VD, VD)]
-    return outs, line_scratch + [pltpu.VMEM((2, size // 2, rows, wide), jnp.bfloat16)] * 2 + sums + sems
+    return outs, line_scratch + [pltpu.VMEM((2, *twos, rows, wide), jnp.bfloat16)] + sums + sems
 
 
 def turn_parts(blocks, left, ins, outs, scratch):
@@ -615,6 +608,194 @@
     d_in[:, 2 * KD : 2 * KD + VD] = d_vals[here].astype(jnp.bfloat16)
 
 
+def hop_valid(kind, t, device, up):
+    last = lax.axis_size(AXIS) - 1
+    passed = device if up else last - device
+    inside = (passed >= 0) & (passed < last)
+    return inside & ((passed >= t) if kind == "gather" else (passed <= t))
+
+
+def hop_call(body, hop, collective_id, *, grid, in_specs, out_specs, out_shape, scratch_shapes=(), cost, name):
+    def params(**more):
+        return pltpu.CompilerParams(vmem_limit_bytes=VMEM, **more)
+
+    if hop is None:
+        return pl.pallas_call(
+            body,
+            grid=grid,
+            in_specs=in_specs,
+            out_specs=out_specs,
+            out_shape=out_shape,
+            scratch_shapes=list(scratch_shapes),
+            compiler_params=params(),
+            cost_estimate=cost,
+            name=name,
+        )
+    kind, t, up, down = hop
+    n_in, n_out = len(in_specs), len(out_specs)
+
+    def with_hop(*refs):
+        ins, sources = refs[:n_in], refs[n_in : n_in + 2]
+        outs, targets = refs[n_in + 2 : n_in + 2 + n_out], refs[n_in + 2 + n_out : n_in + 4 + n_out]
+        *scratch, send_sems, recv_sems = refs[n_in + 4 + n_out :]
+        me = lax.axis_index(AXIS)
+        last = lax.axis_size(AXIS) - 1
+        steps = [pl.program_id(i) for i in range(len(grid))]
+        at_first = functools.reduce(jnp.logical_and, [step == 0 for step in steps])
+        at_last = functools.reduce(jnp.logical_and, [step == size - 1 for step, size in zip(steps, grid)])
+
+        def copy(way):
+            return pltpu.make_async_remote_copy(
+                src_ref=sources[way],
+                dst_ref=targets[way],
+                send_sem=send_sems.at[way],
+                recv_sem=recv_sems.at[way],
+                device_id={AXIS: me - 1 if way else me + 1},
+                device_id_type=pl.DeviceIdType.MESH,
+            )
+
+        @pl.when(at_first)
+        def _():
+            barrier = pltpu.get_barrier_semaphore()
+            for way in range(2):
+
+                @pl.when((me > 0) if way else (me < last))
+                def _(way=way):
+                    to = me - 1 if way else me + 1
+                    pl.semaphore_signal(barrier, inc=1, device_id={AXIS: to}, device_id_type=pl.DeviceIdType.MESH)
+
+            pl.semaphore_wait(barrier, jnp.where((me > 0) & (me < last), 2, 1))
+            for way in range(2):
+
+                @pl.when(hop_valid(kind, t, me, way == 0))
+                def _(way=way):
+                    copy(way).start()
+
+        body(*ins, *outs, *scratch)
+
+        @pl.when(at_last)
+        def _():
+            for way in range(2):
+
+                @pl.when(hop_valid(kind, t, me, way == 0))
+                def _(way=way):
+                    copy(way).wait_send()
+
+                @pl.when(hop_valid(kind, t, me + 1 if way else me - 1, way == 0))
+                def _(way=way):
+                    copy(way).wait_recv()
+
+    anywhere = [pl.BlockSpec(memory_space=pl.ANY)] * 2
+    call = pl.pallas_call(
+        with_hop,
+        grid=grid,
+        in_specs=[*in_specs, *anywhere],
+        out_specs=[*out_specs, *anywhere],
+        out_shape=[*out_shape, *[jax.ShapeDtypeStruct(up.shape, up.dtype)] * 2],
+        scratch_shapes=[*scratch_shapes, pltpu.SemaphoreType.DMA((2,)), pltpu.SemaphoreType.DMA((2,))],
+        compiler_params=params(collective_id=collective_id, has_side_effects=True),
+        cost_estimate=cost,
+        name=name,
+    )
+    return lambda *operands: call(*operands, up, down)
+
+
+def work(flops, moved):
+    return pl.CostEstimate(flops=flops, bytes_accessed=moved, transcendentals=0)
+
+
+def project_body(block, rows_in, weights, out):
+    def part(q, _):
+        at = pl.ds(pl.multiple_of(q * block, block), block)
+        out[at] = dot(rows_in[at], weights[...])
+        return 0
+
+    lax.fori_loop(0, rows_in.shape[0] // block, part, 0)
+
+
+def project(rows_in, weights, hop):
+    length, depth = rows_in.shape
+    columns = weights.shape[1]
+    tile = min(512, columns)
+    return hop_call(
+        functools.partial(project_body, ROWS),
+        hop,
+        4,
+        grid=(columns // tile,),
+        in_specs=[pl.BlockSpec((length, depth), lambda c: (0, 0)), pl.BlockSpec((depth, tile), lambda c: (0, c))],
+        out_specs=[pl.BlockSpec((length, tile), lambda c: (0, c))],
+        out_shape=[jax.ShapeDtypeStruct((length, columns), jnp.float32)],
+        cost=work(2 * length * weights.size, 2 * rows_in.size + 2 * weights.size + 4 * length * columns),
+        name="project",
+    )(rows_in, weights)
+
+
+def hidden_body(rows_in, w_pair, w_down, both, hidden, part):
+    found = dot(rows_in[...], w_pair[...])
+    both[...] = found
+    columns = hidden.shape[1]
+    hidden[...] = (jax.nn.gelu(found[:, :columns], approximate=True) * found[:, columns:]).astype(hidden.dtype)
+    part[...] = dot(hidden[...], w_down[...], CONTRACT_COLUMNS).astype(part.dtype)
+
+
+def hidden_layer(rows_in, mlp_full, hop):
+    length, width = rows_in.shape
+    columns = mlp_full.shape[1] // 3
+    once = pl.Buffered(1)
+    return hop_call(
+        hidden_body,
+        hop,
+        6,
+        grid=(length // ROWS,),
+        in_specs=[
+            pl.BlockSpec((ROWS, width), lambda r: (r, 0)),
+            pl.BlockSpec((width, 2 * columns), lambda r: (0, 0), pipeline_mode=once),
+            pl.BlockSpec((width, columns), lambda r: (0, 2), pipeline_mode=once),
+        ],
+        out_specs=[
+            pl.BlockSpec((ROWS, 2 * columns), lambda r: (r, 0)),
+            pl.BlockSpec((ROWS, columns), lambda r: (r, 0)),
+            pl.BlockSpec((ROWS, width), lambda r: (r, 0)),
+        ],
+        out_shape=[
+            jax.ShapeDtypeStruct((length, 2 * columns), jnp.float32),
+            jax.ShapeDtypeStruct((length, columns), jnp.bfloat16),
+            jax.ShapeDtypeStruct((length, width), jnp.bfloat16),
+        ],
+        cost=work(6 * length * width * columns, 2 * mlp_full.size + 14 * length * columns),
+        name="hidden_layer",
+    )(rows_in, mlp_full, mlp_full)
+
+
+def turned_body(*refs):
+    *pairs, out = refs
+    at = 0
+    for left, right in zip(pairs[::2], pairs[1::2]):
+        columns = right.shape[1]
+        out[:, at : at + columns] = dot(left[...], right[...], CONTRACT_ROWS).astype(out.dtype)
+        at += columns
+
+
+def turned_dots(pairs, hop, collective_id, name):
+    length, width = pairs[0][0].shape
+    columns = sum(right.shape[1] for _, right in pairs)
+    specs = []
+    for _, right in pairs:
+        specs.append(pl.BlockSpec((length, ROWS), lambda r: (0, r)))
+        specs.append(pl.BlockSpec(right.shape, lambda r: (0, 0), pipeline_mode=pl.Buffered(1)))
+    return hop_call(
+        turned_body,
+        hop,
+        collective_id,
+        grid=(width // ROWS,),
+        in_specs=specs,
+        out_specs=[pl.BlockSpec((ROWS, columns), lambda r: (r, 0))],
+        out_shape=[jax.ShapeDtypeStruct((width, columns), jnp.bfloat16)],
+        cost=work(2 * length * width * columns, 2 * (len(pairs) * length * width + length * columns + width * columns)),
+        name=name,
+    )(*[array for pair in pairs for array in pair])
+
+
 def retention_inputs(segments, heads):
     length = segments.shape[0]
     block = min(ROWS, length // 2)
@@ -625,14 +806,16 @@
     return block, reach, log_decay, segments[:, None], seg_line
 
 
-def retention(projected, segments, heads):
+def retention(projected, segments, heads, hop):
     length = projected.shape[0]
     block, reach, log_decay, seg_rows, seg_line = retention_inputs(segments, heads)
     cosine, sine = rotary_tables(length)
     per_head = projected.shape[1] // heads
     table = pl.BlockSpec((block, KD // 2), lambda h, r: (r, 0))
-    return pl.pallas_call(
+    return hop_call(
         functools.partial(retention_body, block, reach),
+        hop,
+        5,
         grid=(heads, length // block),
         in_specs=[
             pl.BlockSpec(memory_space=pltpu.SMEM),
@@ -655,15 +838,12 @@
             pltpu.VMEM((reach + length, VD), jnp.bfloat16),
             pltpu.VMEM((block, reach + block), jnp.float32),
         ],
-        compiler_params=pltpu.CompilerParams(vmem_limit_bytes=48 * 1024 * 1024),
-        cost_estimate=pl.CostEstimate(
-            flops=heads * length * (reach + block) * (KD + VD) * 2, bytes_accessed=projected.size * 6, transcendentals=0
-        ),
+        cost=work(2 * heads * length * (reach + block) * (KD + VD), projected.size * 6),
         name="retention",
     )(log_decay, projected, cosine, sine, seg_rows, seg_line)
 
 
-def retention_pull(kept, projected, d_branch, w_out, segments, heads):
+def retention_pull(kept, projected, d_branch, w_out, segments, heads, hop):
     length = kept.shape[0]
     block, reach, log_decay, seg_rows, seg_line = retention_inputs(segments, heads)
     cosine, sine = rotary_tables(length)
@@ -671,8 +851,10 @@
     last = length // block - 1
     gate_block = per_head // VD
     table = pl.BlockSpec((block, KD // 2), lambda h, r: (last - r, 0))
-    return pl.pallas_call(
+    return hop_call(
         functools.partial(retention_pull_body, block, reach),
+        hop,
+        9,
         grid=(heads, last + 1),
         in_specs=[
             pl.BlockSpec(memory_space=pltpu.SMEM),
@@ -685,8 +867,8 @@
             pl.BlockSpec((block, 1), lambda h, r: (last - r, 0)),
             pl.BlockSpec(seg_line.shape, lambda h, r: (0, 0)),
         ],
-        out_specs=pl.BlockSpec((block, per_head), lambda h, r: (last - r, h)),
-        out_shape=jax.ShapeDtypeStruct(projected.shape, jnp.bfloat16),
+        out_specs=[pl.BlockSpec((block, per_head), lambda h, r: (last - r, h))],
+        out_shape=[jax.ShapeDtypeStruct(projected.shape, jnp.bfloat16)],
         scratch_shapes=[
             pltpu.VMEM((reach + length, KD), jnp.bfloat16),
             pltpu.VMEM((reach + length, VD), jnp.bfloat16),
@@ -694,10 +876,7 @@
             pltpu.VMEM((reach + length, VD), jnp.float32),
             pltpu.VMEM((block, reach + block), jnp.float32),
         ],
-        compiler_params=pltpu.CompilerParams(vmem_limit_bytes=48 * 1024 * 1024),
-        cost_estimate=pl.CostEstimate(
-            flops=heads * length * (reach + block) * (3 * KD + 3 * VD) * 2, bytes_accessed=projected.size * 8, transcendentals=0
-        ),
+        cost=work(2 * heads * length * ((reach + block) * 3 * (KD + VD) + d_branch.shape[1] * VD), projected.size * 8),
         name="retention_pull",
     )(log_decay, kept, projected, d_branch, w_out, cosine, sine, seg_rows, seg_line)
 
@@ -752,14 +931,56 @@
         at += columns
 
 
+def join_parts(parts, plain, left, ins, outs, scratch):
+    def also(s):
+        @pl.when(s == 0)
+        def _():
+            joined_body(parts, plain, *ins, *outs)
+
+    return lambda barrier: 0, also, lambda: None, 1
+
+
 def joined(name, arrays, gain, parts, plain=0):
     columns = sum(part[2] for part in parts)
     return pl.pallas_call(
         functools.partial(joined_body, parts, plain),
         out_shape=jax.ShapeDtypeStruct((gain.shape[0], columns), arrays[0].dtype),
-        compiler_params=pltpu.CompilerParams(vmem_limit_bytes=16 * 1024 * 1024),
+        compiler_params=pltpu.CompilerParams(vmem_limit_bytes=VMEM),
         name=name,
     )(*arrays, gain)
+
+
+def hidden_pull_body(cotangent, w_down, both, d_pair):
+    columns = w_down.shape[1]
+    d_hidden = dot(cotangent[...], w_down[...])
+    gate, up = both[:, :columns], both[:, columns:]
+    slope = math.sqrt(2.0 / math.pi)
+    cubed = 0.044715 * gate * gate
+    bent = jnp.tanh(slope * gate * (1.0 + cubed))
+    half = 0.5 + 0.5 * bent
+    d_gelu = half + 0.5 * gate * (1.0 - bent * bent) * slope * (1.0 + 3.0 * cubed)
+    d_pair[:, :columns] = (d_hidden * up * d_gelu).astype(d_pair.dtype)
+    d_pair[:, columns:] = (d_hidden * gate * half).astype(d_pair.dtype)
+
+
+def hidden_pull(cotangent, mlp_full, both, hop):
+    length, width = cotangent.shape
+    columns = both.shape[1] // 2
+    return hop_call(
+        hidden_pull_body,
+        hop,
+        7,
+        grid=(length // ROWS,),
+        in_specs=[
+            pl.BlockSpec((ROWS, width), lambda r: (r, 0)),
+            pl.BlockSpec((width, columns), lambda r: (0, 2), pipeline_mode=pl.Buffered(1)),
+            pl.BlockSpec((ROWS, 2 * columns), lambda r: (r, 0)),
+        ],
+        out_specs=[pl.BlockSpec((ROWS, 2 * columns), lambda r: (r, 0))],
+        out_shape=[jax.ShapeDtypeStruct(both.shape, jnp.bfloat16)],
+        cost=work(2 * length * width * columns, both.size * 6 + cotangent.size * 4),
+        name="hidden_pull",
+    )(cotangent, mlp_full, both)
 
 
 def steps_of(part, parts):
@@ -767,11 +988,11 @@
     return range((n - 1) * part // parts, (n - 1) * (part + 1) // parts)
 
 
-def gather_steps(state, steps):
-    for _ in steps:
+def gather_hop(state, steps):
+    for _ in steps[:-1]:
         up, down = state[-2:]
         state = [*state, lax.ppermute(up, AXIS, hops(True)), lax.ppermute(down, AXIS, hops(False))]
-    return state
+    return state, ("gather", steps[-1], *state[-2:]) if len(steps) else None
 
 
 def gather_end(state):
@@ -780,23 +1001,27 @@
     return jnp.concatenate([ups[0]] + [jnp.where(me + k < n, downs[k], ups[n - k]) for k in range(1, n)], axis=0)
 
 
-def scatter_steps(state, part, steps):
+def scatter_masked(state, t):
+    n, me = lax.axis_size(AXIS), lax.axis_index(AXIS)
+    found = []
+    for sums, up in zip(state, (True, False)):
+        came = hop_valid("scatter", t - 1, me - 1 if up else me + 1, up)
+        found.append(jnp.where(came, sums, jnp.zeros_like(sums)).astype(jnp.float32))
+    return found
+
+
+def scatter_hop(state, part, steps):
     n = lax.axis_size(AXIS)
     rows = part.shape[0] // n
     for t in steps:
         mine = [part[k * rows : (k + 1) * rows].astype(jnp.float32) for k in (n - 1 - t, 1 + t)]
         if t:
-            mine = [own + sums.astype(jnp.float32) for own, sums in zip(mine, state)]
-        state = [lax.ppermute(sums.astype(part.dtype), AXIS, hops(way)) for sums, way in zip(mine, (True, False))]
-    return state
-
-
-def line_sum(value):
-    n, step = lax.axis_size(AXIS), 1
-    while step < n:
-        value = value + lax.ppermute(value, AXIS, [(i, i ^ step) for i in range(n)])
-        step *= 2
-    return value
+            mine = [own + sums for own, sums in zip(mine, scatter_masked(state, t))]
+        mine = [sums.astype(part.dtype) for sums in mine]
+        if t == steps[-1]:
+            return ("scatter", t, *mine)
+        state = [lax.ppermute(sums, AXIS, hops(way)) for sums, way in zip(mine, (True, False))]
+    return None
 
 
 def shards(tokens,
@@ -832,18 +1057,29 @@
 
     in_parts = [(array, head, columns) for head in range(heads) for array, columns in enumerate((KD, KD, VD, VD))]
     w_in_own = joined("join_in", [w_query, w_key, w_value, w_gate], gain_one, in_parts)
-    mlp_own = joined("join_mlp", [w_mlp_gate, w_mlp_up, w_down], gain_two, [(i, 0, hidden_cols) for i in range(3)], 1)
     w_in = gather(w_in_own)
-    (unit_one,) = line_pass(
-        "gather_one", None, [tokens], [], unit_step, True, 4, 0, local_rows, width
+    unit_one, mlp_own = line_pass(
+        "gather_one",
+        None,
+        [tokens],
+        [],
+        unit_step,
+        True,
+        4,
+        0,
+        local_rows,
+        width,
+        square=functools.partial(join_parts, [(i, 0, hidden_cols) for i in range(3)], 1),
+        square_ins=[w_mlp_gate, w_mlp_up, w_down, gain_two],
+        square_outs=[jax.ShapeDtypeStruct((gain_two.shape[0], 3 * hidden_cols), jnp.bfloat16)],
     )
     w_in, unit_one, w_out, cot_own, mlp_own = after((w_in, unit_one, w_out, cotangent, mlp_own))
     out_full = gather(w_out)
-    cot = gather_steps([cot_own, cot_own], steps_of(0, 3))
-    projected = dot(unit_one, w_in)
-    projected, *cot = after((projected, *cot))
-    cot = gather_steps(cot, steps_of(1, 3))
-    kept, mixed = retention(projected, segments, heads)
+    cot, hop = gather_hop([cot_own, cot_own], steps_of(0, 3))
+    projected, *came = project(unit_one, w_in, hop)
+    cot, hop = gather_hop([*cot, *came], steps_of(1, 3))
+    kept, mixed, *came = retention(projected, segments, heads, hop)
+    cot = [*cot, *came]
     mixed, out_full, mlp_send, *cot = after((mixed, out_full, mlp_own, *cot))
     mlp_full = gather(mlp_send)
     unit_two, residual, unit_turned = line_pass(
@@ -863,51 +1099,33 @@
         square_outs=[jax.ShapeDtypeStruct(unit_one.shape[::-1], unit_one.dtype)],
     )
     unit_two, mlp_full, *cot = after((unit_two, mlp_full, *cot))
-    w_pair, down_full = mlp_full[:, : 2 * hidden_cols], mlp_full[:, 2 * hidden_cols :]
-
-    cot = gather_steps(cot, steps_of(2, 3))
-    both_hidden = dot(unit_two, w_pair)
-    hidden_gate, hidden_up = both_hidden[:, :hidden_cols], both_hidden[:, hidden_cols:]
-    hidden = (jax.nn.gelu(hidden_gate, approximate=True) * hidden_up).astype(jnp.bfloat16)
-    part_down = dot(hidden, down_full, CONTRACT_COLUMNS).astype(jnp.bfloat16)
-    part_down, *cot = after((part_down, *cot))
-    cot_full = gather_end(cot)
-
-    sums = scatter_steps(None, part_down, steps_of(0, 3))
-    grad_down = dot(cot_full, hidden, CONTRACT_ROWS).astype(jnp.bfloat16)
-    d_hidden = dot(cot_full, down_full)
-    _, gelu_pull = jax.vjp(
-        lambda gate_part, up_part: jax.nn.gelu(gate_part, approximate=True) * up_part,
-        hidden_gate,
-        hidden_up,
-    )
-    d_pair = jnp.concatenate(gelu_pull(d_hidden), axis=1).astype(jnp.bfloat16)
-    d_pair, grad_down, *sums = after((d_pair, grad_down, *sums))
-    down_grad = scatter(grad_down)
-    sums = scatter_steps(sums, part_down, steps_of(1, 3))
-    grad_pair = dot(unit_two, d_pair, CONTRACT_ROWS).astype(jnp.bfloat16)
-    d_pair, grad_pair, *sums = after((d_pair, grad_pair, *sums))
-    pair_grad = scatter(grad_pair)
+    cot, hop = gather_hop(cot, steps_of(2, 3))
+    both_hidden, hidden, part_down, *came = hidden_layer(unit_two, mlp_full, hop)
+    cot_full = gather_end([*cot, *came])
+    (d_pair,) = hidden_pull(cot_full, mlp_full, both_hidden, None)
+    hop = scatter_hop(None, part_down, steps_of(0, 3))
+    grad_mlp, *sums = turned_dots([(unit_two, d_pair), (cot_full, hidden)], hop, 8, "mlp_grads")
+    mlp_grad = scatter(grad_mlp)
     d_branch_one, d_residual = line_pass(
         "d_residual", (d_pair, mlp_full), [residual, cotangent], [jnp.float32], d_residual_step, True, 16, 2, local_rows, width, (True, False)
     )
-    d_branch_one, d_residual, pair_grad, down_grad, *sums = after((d_branch_one, d_residual, pair_grad, down_grad, *sums))
-
-    sums = scatter_steps(sums, part_down, steps_of(2, 3))
-    grad_out = dot(d_branch_one, mixed, CONTRACT_ROWS).astype(jnp.bfloat16)
+    d_branch_one, d_residual, mlp_grad = after((d_branch_one, d_residual, mlp_grad))
+    hop = scatter_hop(sums, part_down, steps_of(1, 3))
+    grad_out, *sums = turned_dots([(d_branch_one, mixed)], hop, 10, "out_grads")
     out_grad = scatter(grad_out)
-    d_in = retention_pull(kept, projected, d_branch_one, out_full, segments, heads)
-    result = residual + part_down[:local_rows].astype(jnp.float32) + sum(arrived.astype(jnp.float32) for arrived in sums)
+    hop = scatter_hop(sums, part_down, steps_of(2, 3))
+    d_in, *sums = retention_pull(kept, projected, d_branch_one, out_full, segments, heads, hop)
+    sums = scatter_masked(sums, lax.axis_size(AXIS) - 1)
+    result = residual + part_down[:local_rows].astype(jnp.float32) + sum(sums)
     result = result.astype(jnp.bfloat16)
-    gain_sum_two = line_sum(gain_terms(mlp_own[:, : 2 * hidden_cols], pair_grad)) / gain_two[:, 0]
+    pair_grad, down_grad = mlp_grad[:, : 2 * hidden_cols], mlp_grad[:, 2 * hidden_cols :].astype(jnp.float32)
+    terms_two = gain_terms(mlp_own[:, : 2 * hidden_cols], pair_grad)
+    terms_two = jnp.broadcast_to(terms_two[:, None], (terms_two.shape[0], 128))
     pair_grad = pair_grad.astype(jnp.float32) * gain_two
     gate_grad, up_grad = pair_grad[:, :hidden_cols], pair_grad[:, hidden_cols:]
-    down_grad = down_grad.astype(jnp.float32)
-    d_in, result, gain_sum_two, gate_grad, up_grad, down_grad = after(
-        (d_in, result, gain_sum_two, gate_grad, up_grad, down_grad)
-    )
+    d_in, result, gate_grad, up_grad, down_grad = after((d_in, result, gate_grad, up_grad, down_grad))
     square_outs, square_scratch = square_shapes(gain_one.shape[0], heads, w_in.shape[1])
-    tokens_grad, gain_sum_one, *in_grads = line_pass(
+    tokens_grad, gain_sums, *in_grads = line_pass(
         "tokens_grad",
         (d_in, w_in),
         [tokens, d_residual],
@@ -919,11 +1137,11 @@
         local_rows,
         width,
         square=functools.partial(square_parts, heads),
-        square_ins=[unit_turned, gain_one, w_in_own],
+        square_ins=[unit_turned, gain_one, w_in_own, terms_two],
         square_outs=square_outs,
         square_scratch=square_scratch,
     )
-    gain_sum_one = gain_sum_one[:, 0] / gain_one[:, 0]
+    gain_sum_one, gain_sum_two = gain_sums[0, 0] / gain_one[:, 0], gain_sums[1, 0] / gain_two[:, 0]
     return (
         result,
         tokens_grad,

time: 651 us -> 613 us (0.942); the launches traced: 643 us -> 613 us
  Pallas kernels: 440 us -> 562 us
  matrix products: 78.6 us -> 0 us
  starting transfers between devices: 42.8 us -> 0.2 us
  waiting for transfers between devices: 14.3 us -> 0.15 us
  local copies, waits for them, and re-layouts: 26.4 us -> 15.4 us
    pallas_call x2 -> x7, Pallas kernels: 33.5 us -> 162 us  [the longest x6 150 us: hop_call(): return lambda *operands: call(*operands, up, down)]
    dot_general x7 -> x0, matrix products: 78.6 us -> none  [dot(): lax.dot_general(left, right, dims, preferred_element_type=jnp.float32)]
    ppermute x14 -> x0, starting transfers between devices: 42.6 us -> none  [the longest x6 19.8 us: scatter_steps(): lax.ppermute(sums.astype(part.dtype), AXIS, hops(way))]
    ppermute x14 -> x0, waiting for transfers between devices: 14.1 us -> none  [the longest x3 6.45 us: gather_steps(): lax.ppermute(up, AXIS, hops(True))]
    unnamed x75 -> x43, local copies, waits for them, and re-layouts: 21.6 us -> 9.12 us
    pallas_call x4, Pallas kernels: 404 us -> 397 us  [line_pass(): pl.pallas_call(functools.partial(line_body, n, chunks, rs, ag, rolled, mi...]
  transfers between devices with their start and end apart: 20 -> 5, of which waited for: 6 -> 0; matrix products, arithmetic and copies ran while one was open for 15% -> 3% of each run, Pallas kernels for 68% -> 78%
where the time goes in v4:
time: 613 us
  Pallas kernels  562 us (92%)
  other arithmetic  21.2 us (3%)
  local copies, waits for them, and re-layouts  15.4 us (3%)
  between operations  14.1 us (2%)
    pallas_call x4, Pallas kernels, line_pass(): pl.pallas_call(functools.partial(line_body, n, chunks, rs, ag, rolled, mi...  397 us
    pallas_call x6, Pallas kernels, hop_call(): return lambda *operands: call(*operands, up, down)  150 us
  transfers between devices with their start and end apart: 5, of which 0 were waited for; matrix products, arithmetic and copies ran while one was open for 3% of the time, Pallas kernels for 78%

profile of v4, /device:TPU:0, one launch (start us, length us, event | category | flops | bytes accessed | tf_op | source)
XLA Modules:
  0.0 612.7 jit_solution(11684997776069484964)
XLA Ops:
  7.2 0.0 all-gather.4.cloned.1.call-start
  7.2 0.7 convert_element_type.74
  7.9 0.8 copy.29.refs_4_.refs_5_
  8.7 3.0 join_in.1.refs_6_
  11.7 0.0 all-gather.6.cloned.1.call-start
  11.7 0.8 copy.30.refs_4_
  12.6 76.2 %gather_one.1 = (bf16[1024,2048]{1,0:T(8,128)(2,1)}, bf16[256,3072]{1,0:T(8,128)(2,1)}) custom-call(bf16[256,2048]{1,0:T(8,128)(2,1)} %refs_2_.9, bf16[256,1024]{1,0:T(8,128)(2,1)} %refs_1_.3, bf16[256,1024]{1,0:T(8,128)(2,1)} %refs_2_.6, bf16[256,1024]{1,0:T(8,128)(2,1)} %refs_3_.5, f32[256,1]{1,0:T(8,128)} %copy.30.refs_4_), custom_call_target="tpu_custom_call" | custom-call | bytes 125829120 | tf_op jit(solution)/shard_map/gather_one/pallas_call | solution.py:282
  88.9 0.0 all-gather.8.cloned.1.call-start
  88.9 1.0 copy.31.refs_4_.refs_7_
  89.9 0.6 broadcast_in_dim.18.refs_5_.refs_8_
  90.5 0.5 subtract_log_fusion.refs_0_
  91.1 28.7 %project.1 = (f32[1024,3072]{1,0:T(8,128)}, bf16[256,2048]{1,0:T(8,128)(2,1)}, bf16[256,2048]{1,0:T(8,128)(2,1)}) custom-call(bf16[1024,2048]{1,0:T(8,128)(2,1)} %get-tuple-element.76.refs_0_.refs_3_, bf16[2048,3072]{1,0:T(8,128)(2,1)} %all-gather.4.cloned.1.call-done.refs_1_, bf16[256,2048]{1,0:T(8,128)(2,1)} %refs_3_.7, bf16[256,2048]{1,0:T(8,128)(2,1)} %refs_3_.7), custom_call_target="tpu_custom_call" | custom-call | flops 12884901888 | bytes 29360128 | tf_op jit(solution)/shard_map/project/pallas_call | solution.py:700
  119.8 26.4 %retention.1 = (bf16[1024,2048]{1,0:T(8,128)(2,1)}, bf16[1024,1024]{1,0:T(8,128)(2,1)}, bf16[256,2048]{1,0:T(8,128)(2,1)}, bf16[256,2048]{1,0:T(8,128)(2,1)}) custom-call(f32[2]{0:T(128)} %subtract_log_fusion.refs_0_, f32[1024,3072]{1,0:T(8,128)} %get-tuple-element.79.refs_1_.refs_2_, f32[1024,128]{1,0:T(8,128)} %constant.31.clone.refs_2_.refs_5_, ...), custom_call_target="tpu_custom_call" | custom-call | flops 2415919104 | bytes 18874368 | tf_op jit(solution)/shard_map/retention/pallas_call | solution.py:700
  146.3 0.0 reduce-scatter.3.cloned.1.call-start
  146.4 116.9 %residual.1 = (bf16[1024,2048]{1,0:T(8,128)(2,1)}, f32[256,2048]{1,0:T(8,128)}, bf16[2048,1024]{1,0:T(8,128)(2,1)}) custom-call(bf16[1024,1024]{1,0:T(8,128)(2,1)} %get-tuple-element.88.refs_0_.refs_1_, bf16[2048,1024]{1,0:T(8,128)(2,1)} %all-gather.6.cloned.1.call-done.refs_1_.refs_4_, bf16[256,2048]{1,0:T(8,128)(2,1)} %refs_2_.9, ...), custom_call_target="tpu_custom_call" | custom-call | bytes 125829120 | tf_op jit(solution)/shard_map/residual/pallas_call | solution.py:282
  263.3 0.0 all-gather.8.cloned.1.call-done.refs_1_.refs_2_.w_down
  263.4 27.7 %hidden_layer.1 = (f32[1024,2048]{1,0:T(8,128)}, bf16[1024,1024]{1,0:T(8,128)(2,1)}, bf16[1024,2048]{1,0:T(8,128)(2,1)}, bf16[256,2048]{1,0:T(8,128)(2,1)}, bf16[256,2048]{1,0:T(8,128)(2,1)}) custom-call(bf16[1024,2048]{1,0:T(8,128)(2,1)} %get-tuple-element.99.refs_0_, bf16[2048,3072]{1,0:T(8,128)(2,1)} %all-gather.8.cloned.1.call-done.refs_1_.refs_2_.w_down, ...), custom_call_target="tpu_custom_call" | custom-call | flops 12884901888 | bytes 27262976 | tf_op jit(solution)/shard_map/hidden_layer/pallas_call | solution.py:700
  291.1 1.9 broadcast_select_fusion
  293.0 0.9 copy-done
  293.9 0.3 copy-done.5
  294.2 0.3 copy-done.13
  294.5 1.6 fusion.3
  296.1 2.3 pad_maximum_fusion.cotangent.refs_2_
  298.4 11.9 %hidden_pull.1.refs_0_.refs_1_ = bf16[1024,2048]{1,0:T(8,128)(2,1)} custom-call(bf16[1024,2048]{1,0:T(8,128)(2,1)} %pad_maximum_fusion.cotangent.refs_2_, bf16[2048,3072]{1,0:T(8,128)(2,1)} %all-gather.8.cloned.1.call-done.refs_1_.refs_2_.w_down, f32[1024,2048]{1,0:T(8,128)} %get-tuple-element.106.both), custom_call_target="tpu_custom_call" | custom-call | flops 4294967296 | bytes 20971520 | tf_op jit(solution)/shard_map/hidden_pull/pallas_call | solution.py:969
  310.3 22.2 %mlp_grads.1 = (bf16[2048,3072]{1,0:T(8,128)(2,1)}, bf16[256,2048]{1,0:T(8,128)(2,1)}, bf16[256,2048]{1,0:T(8,128)(2,1)}) custom-call(bf16[1024,2048]{1,0:T(8,128)(2,1)} %get-tuple-element.99.refs_0_, bf16[1024,2048]{1,0:T(8,128)(2,1)} %hidden_pull.1.refs_0_.refs_1_, bf16[1024,2048]{1,0:T(8,128)(2,1)} %pad_maximum_fusion.cotangent.refs_2_, ...), custom_call_target="tpu_custom_call" | custom-call | flops 12884901888 | bytes 27262976 | tf_op jit(solution)/shard_map/mlp_grads/pallas_call | solution.py:700
  332.5 0.0 reduce-scatter.5.cloned.1.call-start
  332.6 116.6 %d_residual.1 = (bf16[1024,2048]{1,0:T(8,128)(2,1)}, f32[256,2048]{1,0:T(8,128)}) custom-call(bf16[1024,2048]{1,0:T(8,128)(2,1)} %hidden_pull.1.refs_0_.refs_1_, bf16[2048,3072]{1,0:T(8,128)(2,1)} %all-gather.8.cloned.1.call-done.refs_1_.refs_2_.w_down, f32[256,2048]{1,0:T(8,128)} %get-tuple-element.107.refs_2_, bf16[256,2048]{1,0:T(8,128)(2,1)} %refs_3_.7), custom_call_target="tpu_custom_call" | custom-call | bytes 125829120 | tf_op jit(solution)/shard_map/d_residual/pallas_call | solution.py:282
  449.1 3.3 fusion.1
  452.4 16.3 %out_grads.1 = (bf16[2048,1024]{1,0:T(8,128)(2,1)}, bf16[256,2048]{1,0:T(8,128)(2,1)}, bf16[256,2048]{1,0:T(8,128)(2,1)}) custom-call(bf16[1024,2048]{1,0:T(8,128)(2,1)} %get-tuple-element.113.refs_0_.refs_3_, bf16[1024,1024]{1,0:T(8,128)(2,1)} %get-tuple-element.88.refs_0_.refs_1_, bf16[256,2048]{1,0:T(8,128)(2,1)} %get-tuple-element.139.refs_2_, ...), custom_call_target="tpu_custom_call" | custom-call | flops 4294967296 | bytes 10485760 | tf_op jit(solution)/shard_map/out_grads/pallas_call | solution.py:700
  468.8 1.3 copy-done.6
  470.2 1.1 slice_convert_fusion
  471.3 0.5 fusion.2
  471.8 1.5 fusion.4
  473.3 1.7 copy-done.1
  475.0 2.2 add_convert_fusion.1
  477.1 28.6 %retention_pull.1 = (bf16[1024,3072]{1,0:T(8,128)(2,1)}, bf16[256,2048]{1,0:T(8,128)(2,1)}, bf16[256,2048]{1,0:T(8,128)(2,1)}) custom-call(f32[2]{0:T(128)} %subtract_log_fusion.refs_0_, bf16[1024,2048]{1,0:T(8,128)(2,1)} %get-tuple-element.82.refs_1_, f32[1024,3072]{1,0:T(8,128)} %get-tuple-element.79.refs_1_.refs_2_, ...), custom_call_target="tpu_custom_call" | custom-call | flops 11542724608 | bytes 25165824 | tf_op jit(solution)/shard_map/retention_pull/pallas_call | solution.py:700
  505.7 3.9 add_convert_fusion
  509.7 0.8 broadcast_in_dim.19.refs_7_
  510.4 87.0 %tokens_grad.1 = (bf16[256,2048]{1,0:T(8,128)(2,1)}, f32[2,8,256]{2,1,0:T(8,128)}, f32[256,512]{1,0:T(8,128)}, f32[256,512]{1,0:T(8,128)}, f32[256,1024]{1,0:T(8,128)}, /*index=5*/f32[256,1024]{1,0:T(8,128)}) custom-call(bf16[1024,3072]{1,0:T(8,128)(2,1)} %get-tuple-element.123.refs_0_, bf16[2048,3072]{1,0:T(8,128)(2,1)} %all-gather.4.cloned.1.call-done.refs_1_, ...), custom_call_target="tpu_custom_call" | custom-call | bytes 125829120 | tf_op jit(solution)/shard_map/tokens_grad/pallas_call | solution.py:282
  597.5 0.8 fusion.5
  598.3 0.6 convert_divide_fusion.1
  598.9 0.6 convert_divide_fusion
  599.5 2.2 convert_element_type.94
  601.6 1.0 copy.39
  602.6 0.8 copy.40
  603.4 0.8 copy.41
  604.2 1.0 copy.42
  605.2 1.0 copy.43
  (44 shorter events, 0.2 us)
Async XLA Ops:
  7.2 81.6 %all-gather.4.cloned.1.call-start = ((), (), s32[]{:S(2)}) async-start(), calls=%async_computation.2 | async-start | bytes 14155776 | tf_op jit(solution)/shard_map/all_gather | solution.py:1050
  8.7 3.0 copy-start.18
  11.7 77.2 %copy-start.16 = (s32[1,1024]{1,0:T(1,128)S(1)}, s32[1,1024]{1,0:T(1,128)}, u32[]{:S(2)}) copy-start(s32[1,1024]{1,0:T(1,128)} %param.18) | copy-start | bytes 12292
  11.7 134.6 %all-gather.6.cloned.1.call-start = ((), (), s32[]{:S(2)}) async-start(), calls=%async_computation.3 | async-start | bytes 4718592 | tf_op jit(solution)/shard_map/all_gather | solution.py:1050
  88.9 174.5 %all-gather.8.cloned.1.call-start = ((), (), s32[]{:S(2)}) async-start(), calls=%async_computation.4 | async-start | bytes 14155776 | tf_op jit(solution)/shard_map/all_gather | solution.py:1050
  146.3 306.1 %reduce-scatter.3.cloned.1.call-start = ((), (), s32[]{:S(2)}) async-start(), calls=%async_computation.5 | async-start | bytes 14155776 | tf_op jit(solution)/shard_map/reduce_scatter | solution.py:1053
  263.3 27.7 %copy-start.3 = (bf16[256,2048]{1,0:T(8,128)(2,1)S(1)}, bf16[256,2048]{1,0:T(8,128)(2,1)}, u32[]{:S(2)}) copy-start(bf16[256,2048]{1,0:T(8,128)(2,1)} %get-tuple-element.105.refs_6_) | copy-start | bytes 3145732
  291.1 2.8 copy-start
  291.1 3.1 copy-start.5
  291.1 3.4 copy-start.13
  294.5 1.6 copy-start.4
  332.5 267.0 %reduce-scatter.5.cloned.1.call-start = ((), (), s32[]{:S(2)}) async-start(), calls=%async_computation.6 | async-start | bytes 4718592 | tf_op jit(solution)/shard_map/reduce_scatter | solution.py:1053
  332.6 116.6 %copy-start.10 = (bf16[256,2048]{1,0:T(8,128)(2,1)S(1)}, bf16[256,2048]{1,0:T(8,128)(2,1)}, u32[]{:S(2)}) copy-start(bf16[256,2048]{1,0:T(8,128)(2,1)} %get-tuple-element.114) | copy-start | bytes 3145732
  468.8 1.4 copy-start.6
  468.8 2.5 copy-start.2
  471.3 2.0 copy-start.11
  471.3 2.0 copy-start.12
  471.8 3.2 copy-start.1
  510.4 87.9 %copy-start.17 = (bf16[256]{0:T(256)(128)(2,1)S(1)}, bf16[256]{0:T(256)(128)(2,1)}, u32[]{:S(2)}) copy-start(bf16[256]{0:T(256)(128)(2,1)} %param.19) | copy-start | bytes 1540
  597.5 4.2 copy-start.9
  597.5 5.2 copy-start.15
  599.5 4.0 copy-start.14
  601.6 2.6 copy-start.8
  602.6 2.6 copy-start.7
Sparse Core Ops, SparseCore 0:
  11.8 74.8 all-gather.3
  89.0 36.8 all-gather.5
  146.4 71.6 all-gather.7
  332.6 91.5 reduce-scatter.2
  468.9 52.3 reduce-scatter.4

commit v5 on v4

--- a/solution.py
+++ b/solution.py
@@ -19,7 +19,7 @@
     me = lax.axis_index(AXIS)
     last = n - 1
     lag = last if rs else 0
-    greet, also, finish, steps = lambda barrier: 0, lambda s: None, lambda: None, 0
+    greet, also, finish, steps, early = lambda barrier: 0, lambda s: None, lambda: None, 0, False
     if rs:
         here, load_sems, left_sems, right_sems = scratch[:n_in], *scratch[n_in : n_in + 3]
         scratch = scratch[n_in + 3 :]
@@ -35,24 +35,35 @@
             at = pl.ds(pl.multiple_of(q * wide, wide), wide)
             return pltpu.make_async_copy(outside[1].at[at, pl.ds(0, right.shape[1])], right.at[at], right_sems.at[q])
 
-        def later_copies():
-            return [left_copy(g, j) for g in range(1, groups) for j in range(n)] + [
-                pltpu.make_async_copy(outside[i], here[i], load_sems.at[i]) for i in range(2, n_in)
-            ]
-
-        for j in range(n):
-            left_copy(0, j).start()
-        for q in range(right.shape[0] // wide):
-            right_copy(q).start()
-        for copy in later_copies():
-            copy.start()
+        def other_copy(i):
+            return pltpu.make_async_copy(outside[i], here[i], load_sems.at[i])
+
+        soon = n_in - square[1] if square is not None else n_in
+        others = [i for i in range(2, n_in) if i != soon]
+
+        def start_loads():
+            starts = [left_copy(0, j) for j in range(n)]
+            later = [left_copy(g, j) for g in range(1, groups) for j in range(n)]
+            later += [other_copy(soon)] if soon < n_in else []
+            tiles = [right_copy(q) for q in range(right.shape[0] // wide)]
+            for copy in starts + (later + tiles if early else tiles + later) + [other_copy(i) for i in others]:
+                copy.start()
+
+        def wait_soon():
+            for g in range(1, groups):
+                for j in range(n):
+                    left_copy(g, j).wait()
+            if soon < n_in:
+                other_copy(soon).wait()
+
         ins = here
     if square is not None:
         counts = square[1:]
         square_refs = ins[n_in - counts[0] :], outs[n_out - counts[1] :], scratch[len(scratch) - counts[2] :]
         ins, outs, scratch = ins[: n_in - counts[0]], outs[: n_out - counts[1]], scratch[: len(scratch) - counts[2]]
-        greet, also, finish, steps = square[0](ins[0], *square_refs)
+        greet, also, finish, steps, early = square[0](ins[0], *square_refs)
     if rs:
+        start_loads()
         ins = ins[2:]
         part, up_buf, dn_buf, total, up_send, up_recv, dn_send, dn_recv = scratch[:8]
         scratch = scratch[8:]
@@ -106,8 +117,8 @@
     def _():
         pl.semaphore_signal(barrier, inc=1, device_id={AXIS: me + 1}, device_id_type=pl.DeviceIdType.MESH)
 
-    others = greet(barrier)
-    pl.semaphore_wait(barrier, jnp.where((me > 0) & (me < last), 2, 1) + others)
+    greeted = greet(barrier)
+    pl.semaphore_wait(barrier, jnp.where((me > 0) & (me < last), 2, 1) + greeted)
 
     def sum_copy(up, d, c):
         buf, s, r, to = (up_buf, up_send, up_recv, me + 1) if up else (dn_buf, dn_send, dn_recv, me - 1)
@@ -149,12 +160,15 @@
                     def _(up=up, c=c, d=d):
                         sum_step(up, d, c)
 
-            @pl.when(s == 0)
+            if not early:
+                pl.when(s == 0)(wait_soon)
+
+            @pl.when(s == 1)
             def _():
-                for copy in later_copies():
-                    copy.wait()
-
-        also(s)
+                for i in others:
+                    other_copy(i).wait()
+
+        also(s + 1 if early else s)
         if rs:
             per_group = chunks // groups
 
@@ -211,8 +225,11 @@
     if rs:
         for j in range(n):
             left_copy(0, j).wait()
+        if early:
+            wait_soon()
+            also(0)
         product(0)
-    lax.fori_loop(0, max(chunks + lag + (last - 1 if ag else 0), steps), step, 0)
+    lax.fori_loop(0, max(chunks + lag + (last - 1 if ag else 0), steps - early), step, 0)
     finish()
 
     def drain(c, _):
@@ -300,7 +317,7 @@
 
 
 def square_parts(heads, left, ins, outs, scratch):
-    turned, gain, weights, other_terms = ins
+    turned, gain, weights, other_terms, other_gain = ins
     gain_sum, grads = outs[0], outs[1:]
     terms_one, sums, sums_in, sums_send, sums_recv, sent, *rest = scratch
     line = lax.axis_index(AXIS)
@@ -422,7 +439,8 @@
                 if bit < line_bits:
                     sums_copy(bit).start()
                 else:
-                    gain_sum[...] = sums[bit]
+                    gain_sum[0] = sums[bit, 0] / gain[...]
+                    gain_sum[1] = sums[bit, 1] / other_gain[...]
 
     def result(p, side, summed):
         at = pl.ds(pl.multiple_of(p * wide + side * half, half), half)
@@ -440,7 +458,7 @@
             def _():
                 terms_one[...] += terms
 
-        summed = summed * gain[...]
+        summed = summed * as_column(gain[...])
         for found in range(pairs):
             head, kind = found // (pairs // heads), found % (pairs // heads)
             where = grads[side] if kind == 0 else grads[1 + kind]
@@ -462,7 +480,7 @@
 
         lax.fori_loop(0, pairs, drain, 0)
 
-    return greet, also, finish, pairs + bits + line_bits + 1
+    return greet, also, finish, pairs + bits + line_bits + 1, False
 
 
 def square_shapes(rows, heads, columns):
@@ -501,7 +519,7 @@
                 at = pl.ds(block * columns, columns)
                 turned[at] = rows_in[:, at].T
 
-    return lambda barrier: 0, also, lambda: None, blocks
+    return lambda barrier: 0, also, lambda: None, blocks, False
 
 
 HEADS = 8
@@ -532,10 +550,11 @@
     return lax.dot_general(left, right, dims, preferred_element_type=jnp.float32)
 
 
-def head_decay(decay_ref, log_ref, head, reach):
+def head_decay(decay_ref, log_ref, heads, head, reach):
     ahead = lax.broadcasted_iota(jnp.int32, decay_ref.shape, 0) - lax.broadcasted_iota(jnp.int32, decay_ref.shape, 1)
     distance = ahead + reach
-    value = jnp.exp(log_ref[head] * jnp.maximum(distance, 0).astype(jnp.float32))
+    mine = lax.axis_index(AXIS) * heads + head
+    value = jnp.exp(log_ref[mine] * jnp.maximum(distance, 0).astype(jnp.float32))
     decay_ref[...] = jnp.where(distance >= 0, value, 0.0)
 
 
@@ -545,16 +564,18 @@
     return centred * inverse, inverse
 
 
-def retention_body(block, reach, log_ref, proj, cosine, sine, seg_rows, seg_line, kept, mixed, keys, vals, decay):
+def retention_body(block, reach, log_ref, proj, cosine, sine, segments, kept, mixed, keys, vals, decay, seg_line):
     head, row = pl.program_id(0), pl.program_id(1)
     here = pl.ds(pl.multiple_of(reach + row * block, block), block)
     window = pl.ds(pl.multiple_of(row * block, block), reach + block)
 
     @pl.when(row == 0)
     def _():
-        head_decay(decay, log_ref, head, reach)
+        head_decay(decay, log_ref, pl.num_programs(0), head, reach)
         keys[:reach] = jnp.zeros((reach, KD), keys.dtype)
         vals[:reach] = jnp.zeros((reach, VD), vals.dtype)
+        seg_line[:, :reach] = jnp.full((1, reach), -1, jnp.int32)
+        seg_line[:, reach:] = segments[...]
 
     query = turn(proj[:, :KD], cosine[...], sine[...]).astype(jnp.bfloat16)
     key = (turn(proj[:, KD : 2 * KD], cosine[...], sine[...]) * KD ** (-0.5)).astype(jnp.bfloat16)
@@ -564,14 +585,14 @@
     kept[:, :KD] = query
     kept[:, KD : 2 * KD] = key
     kept[:, 2 * KD :] = value
-    weight = jnp.where(seg_rows[...] == seg_line[:, window], decay[...], 0.0)
+    weight = jnp.where(as_column(seg_line[:, here]) == seg_line[:, window], decay[...], 0.0)
     probs = (dot(query, keys[window], CONTRACT_COLUMNS) * weight).astype(jnp.bfloat16)
     normed, _ = normed_heads(dot(probs, vals[window]))
     mixed[...] = (jax.nn.silu(proj[:, 2 * KD + VD :]) * normed).astype(jnp.bfloat16)
 
 
 def retention_pull_body(
-    block, reach, log_ref, kept, gate, d_branch, w_out, cosine, sine, seg_rows, seg_line, d_in, keys, vals, d_keys, d_vals, decay
+    block, reach, log_ref, kept, gate, d_branch, w_out, cosine, sine, segments, d_in, keys, vals, d_keys, d_vals, decay, seg_line
 ):
     head, row = pl.program_id(0), pl.num_programs(1) - 1 - pl.program_id(1)
     mine = pl.ds(pl.multiple_of(row * block, block), block)
@@ -580,16 +601,18 @@
 
     @pl.when(pl.program_id(1) == 0)
     def _():
-        head_decay(decay, log_ref, head, reach)
+        head_decay(decay, log_ref, pl.num_programs(0), head, reach)
         keys[:reach] = jnp.zeros((reach, KD), keys.dtype)
         vals[:reach] = jnp.zeros((reach, VD), vals.dtype)
+        seg_line[:, :reach] = jnp.full((1, reach), -1, jnp.int32)
+        seg_line[:, reach:] = segments[...]
         keys[reach:] = kept[:, KD : 2 * KD]
         vals[reach:] = kept[:, 2 * KD :]
         d_keys[...] = jnp.zeros_like(d_keys)
         d_vals[...] = jnp.zeros_like(d_vals)
 
     query = kept[mine, :KD]
-    weight = jnp.where(seg_rows[...] == seg_line[:, window], decay[...], 0.0)
+    weight = jnp.where(as_column(seg_line[:, here]) == seg_line[:, window], decay[...], 0.0)
     probs = (dot(query, keys[window], CONTRACT_COLUMNS) * weight).astype(jnp.bfloat16)
     normed, inverse = normed_heads(dot(probs, vals[window]))
     gate_pre, upstream = gate[...], dot(d_branch[...], w_out[...])
@@ -615,7 +638,7 @@
     return inside & ((passed >= t) if kind == "gather" else (passed <= t))
 
 
-def hop_call(body, hop, collective_id, *, grid, in_specs, out_specs, out_shape, scratch_shapes=(), cost, name):
+def hop_call(body, hop, collective_id, then=None, *, grid, in_specs, out_specs, out_shape, scratch_shapes=(), cost, name):
     def params(**more):
         return pltpu.CompilerParams(vmem_limit_bytes=VMEM, **more)
 
@@ -631,22 +654,34 @@
             cost_estimate=cost,
             name=name,
         )
-    kind, t, up, down = hop
-    n_in, n_out = len(in_specs), len(out_specs)
+    kind, t, *arrays = hop
+    n = lax.axis_size(AXIS)
+    n_in, n_out, n_sent = len(in_specs), len(out_specs), len(arrays)
+    rows, width = arrays[0].shape[0] // (n if n_sent == 1 else 1), arrays[0].shape[1]
+    shape = jax.ShapeDtypeStruct((rows, width), arrays[0].dtype)
+    added = [] if then is None else list(then)
+    n_got = 1 if len(added) == 2 else 2
 
     def with_hop(*refs):
-        ins, sources = refs[:n_in], refs[n_in : n_in + 2]
-        outs, targets = refs[n_in + 2 : n_in + 2 + n_out], refs[n_in + 2 + n_out : n_in + 4 + n_out]
-        *scratch, send_sems, recv_sems = refs[n_in + 4 + n_out :]
+        ins, sources, refs = refs[:n_in], refs[n_in : n_in + n_sent], refs[n_in + n_sent :]
+        terms, outs, refs = refs[: len(added)], refs[len(added) : len(added) + n_out], refs[len(added) + n_out :]
+        targets, (*scratch, send_sems, recv_sems) = refs[:n_got], refs[n_got:]
+        found = targets
+        if added:
+            *scratch, came, mine, mine_sems = scratch
+            targets = [came.at[0], came.at[1]]
+        if len(added) == 2:
+            *scratch, kept, kept_sem = scratch
         me = lax.axis_index(AXIS)
-        last = lax.axis_size(AXIS) - 1
+        last = n - 1
         steps = [pl.program_id(i) for i in range(len(grid))]
         at_first = functools.reduce(jnp.logical_and, [step == 0 for step in steps])
         at_last = functools.reduce(jnp.logical_and, [step == size - 1 for step, size in zip(steps, grid)])
 
         def copy(way):
+            source = sources[way] if n_sent == 2 else sources[0].at[pl.ds((1 if way else last) * rows, rows)]
             return pltpu.make_async_remote_copy(
-                src_ref=sources[way],
+                src_ref=source,
                 dst_ref=targets[way],
                 send_sem=send_sems.at[way],
                 recv_sem=recv_sems.at[way],
@@ -654,6 +689,16 @@
                 device_id_type=pl.DeviceIdType.MESH,
             )
 
+        def term_copies():
+            if not added:
+                return []
+            slots = [0] if len(added) == 2 else [last - t - 1, 2 + t]
+            copies = [
+                pltpu.make_async_copy(terms[0].at[pl.ds(slot * rows, rows)], mine.at[way], mine_sems.at[way])
+                for way, slot in enumerate(slots)
+            ]
+            return copies + ([pltpu.make_async_copy(terms[1], kept, kept_sem)] if len(added) == 2 else [])
+
         @pl.when(at_first)
         def _():
             barrier = pltpu.get_barrier_semaphore()
@@ -671,10 +716,20 @@
                 def _(way=way):
                     copy(way).start()
 
+            for term in term_copies():
+                term.start()
+
         body(*ins, *outs, *scratch)
 
         @pl.when(at_last)
         def _():
+            for term in term_copies():
+                term.wait()
+            if len(added) == 1:
+                for way in range(2):
+                    found[way][...] = mine[way]
+            if len(added) == 2:
+                kept[...] += mine[0].astype(jnp.float32)
             for way in range(2):
 
                 @pl.when(hop_valid(kind, t, me, way == 0))
@@ -684,20 +739,33 @@
                 @pl.when(hop_valid(kind, t, me + 1 if way else me - 1, way == 0))
                 def _(way=way):
                     copy(way).wait_recv()
-
-    anywhere = [pl.BlockSpec(memory_space=pl.ANY)] * 2
+                    if len(added) == 1:
+                        found[way][...] += came[way]
+                    if len(added) == 2:
+                        kept[...] += came[way].astype(jnp.float32)
+
+            if len(added) == 2:
+                found[0][...] = kept[...].astype(shape.dtype)
+
+    anywhere = pl.BlockSpec(memory_space=pl.ANY)
+    got = pl.BlockSpec((rows, width), lambda *_: (0, 0)) if added else anywhere
+    more = []
+    if len(added) == 2:
+        more += [pltpu.VMEM((rows, width), jnp.float32), pltpu.SemaphoreType.DMA]
+    if added:
+        more += [pltpu.VMEM((2, rows, width), shape.dtype)] * 2 + [pltpu.SemaphoreType.DMA((2,))]
     call = pl.pallas_call(
         with_hop,
         grid=grid,
-        in_specs=[*in_specs, *anywhere],
-        out_specs=[*out_specs, *anywhere],
-        out_shape=[*out_shape, *[jax.ShapeDtypeStruct(up.shape, up.dtype)] * 2],
-        scratch_shapes=[*scratch_shapes, pltpu.SemaphoreType.DMA((2,)), pltpu.SemaphoreType.DMA((2,))],
+        in_specs=[*in_specs, *[anywhere] * (n_sent + len(added))],
+        out_specs=[*out_specs, *[got] * n_got],
+        out_shape=[*out_shape, *[shape] * n_got],
+        scratch_shapes=[*scratch_shapes, *more, pltpu.SemaphoreType.DMA((2,)), pltpu.SemaphoreType.DMA((2,))],
         compiler_params=params(collective_id=collective_id, has_side_effects=True),
         cost_estimate=cost,
         name=name,
     )
-    return lambda *operands: call(*operands, up, down)
+    return lambda *operands: call(*operands, *arrays, *added)
 
 
 def work(flops, moved):
@@ -776,7 +844,7 @@
         at += columns
 
 
-def turned_dots(pairs, hop, collective_id, name):
+def turned_dots(pairs, hop, collective_id, then, name):
     length, width = pairs[0][0].shape
     columns = sum(right.shape[1] for _, right in pairs)
     specs = []
@@ -787,6 +855,7 @@
         turned_body,
         hop,
         collective_id,
+        then,
         grid=(width // ROWS,),
         in_specs=specs,
         out_specs=[pl.BlockSpec((ROWS, columns), lambda r: (r, 0))],
@@ -796,19 +865,17 @@
     )(*[array for pair in pairs for array in pair])
 
 
-def retention_inputs(segments, heads):
-    length = segments.shape[0]
+def retention_inputs(segments):
+    length = segments.shape[1]
     block = min(ROWS, length // 2)
     reach = length // 2
-    head_ids = lax.axis_index("tensor") * heads + jnp.arange(heads)
-    log_decay = jnp.log(1.0 - 2.0 ** (-5.0 - head_ids.astype(jnp.float32)))
-    seg_line = jnp.concatenate([jnp.full((reach,), -1, jnp.int32), segments])[None, :]
-    return block, reach, log_decay, segments[:, None], seg_line
+    log_decay = np.log(1.0 - 2.0 ** (-5.0 - np.arange(HEADS))).astype(np.float32)
+    return block, reach, log_decay
 
 
 def retention(projected, segments, heads, hop):
     length = projected.shape[0]
-    block, reach, log_decay, seg_rows, seg_line = retention_inputs(segments, heads)
+    block, reach, log_decay = retention_inputs(segments)
     cosine, sine = rotary_tables(length)
     per_head = projected.shape[1] // heads
     table = pl.BlockSpec((block, KD // 2), lambda h, r: (r, 0))
@@ -822,8 +889,7 @@
             pl.BlockSpec((block, per_head), lambda h, r: (r, h)),
             table,
             table,
-            pl.BlockSpec((block, 1), lambda h, r: (r, 0)),
-            pl.BlockSpec(seg_line.shape, lambda h, r: (0, 0)),
+            pl.BlockSpec(segments.shape, lambda h, r: (0, 0)),
         ],
         out_specs=[
             pl.BlockSpec((block, 2 * KD + VD), lambda h, r: (r, h)),
@@ -837,15 +903,16 @@
             pltpu.VMEM((reach + length, KD), jnp.bfloat16),
             pltpu.VMEM((reach + length, VD), jnp.bfloat16),
             pltpu.VMEM((block, reach + block), jnp.float32),
+            pltpu.VMEM((1, reach + length), jnp.int32),
         ],
         cost=work(2 * heads * length * (reach + block) * (KD + VD), projected.size * 6),
         name="retention",
-    )(log_decay, projected, cosine, sine, seg_rows, seg_line)
-
-
-def retention_pull(kept, projected, d_branch, w_out, segments, heads, hop):
+    )(log_decay, projected, cosine, sine, segments)
+
+
+def retention_pull(kept, projected, d_branch, w_out, segments, heads, hop, then):
     length = kept.shape[0]
-    block, reach, log_decay, seg_rows, seg_line = retention_inputs(segments, heads)
+    block, reach, log_decay = retention_inputs(segments)
     cosine, sine = rotary_tables(length)
     per_head = projected.shape[1] // heads
     last = length // block - 1
@@ -855,6 +922,7 @@
         functools.partial(retention_pull_body, block, reach),
         hop,
         9,
+        then,
         grid=(heads, last + 1),
         in_specs=[
             pl.BlockSpec(memory_space=pltpu.SMEM),
@@ -864,8 +932,7 @@
             pl.BlockSpec((w_out.shape[0], VD), lambda h, r: (0, h)),
             table,
             table,
-            pl.BlockSpec((block, 1), lambda h, r: (last - r, 0)),
-            pl.BlockSpec(seg_line.shape, lambda h, r: (0, 0)),
+            pl.BlockSpec(segments.shape, lambda h, r: (0, 0)),
         ],
         out_specs=[pl.BlockSpec((block, per_head), lambda h, r: (last - r, h))],
         out_shape=[jax.ShapeDtypeStruct(projected.shape, jnp.bfloat16)],
@@ -875,10 +942,11 @@
             pltpu.VMEM((reach + length, KD), jnp.float32),
             pltpu.VMEM((reach + length, VD), jnp.float32),
             pltpu.VMEM((block, reach + block), jnp.float32),
+            pltpu.VMEM((1, reach + length), jnp.int32),
         ],
         cost=work(2 * heads * length * ((reach + block) * 3 * (KD + VD) + d_branch.shape[1] * VD), projected.size * 8),
         name="retention_pull",
-    )(log_decay, kept, projected, d_branch, w_out, cosine, sine, seg_rows, seg_line)
+    )(log_decay, kept, projected, d_branch, w_out, cosine, sine, segments)
 
 
 def inverse_rms(rows):
@@ -920,67 +988,129 @@
     return [(i, i + 1) if up else (i + 1, i) for i in range(n - 1)]
 
 
+def as_column(row):
+    return jnp.broadcast_to(row, (128, row.shape[1])).T[:, :1]
+
+
 def joined_body(parts, plain, *refs):
-    *arrays, gain, out = refs
+    *arrays, gain_row, out = refs
+    gain = as_column(gain_row[...].astype(jnp.float32))
     at = 0
     for array, index, columns in parts:
         found = arrays[array][:, index * columns : (index + 1) * columns]
         if array < len(arrays) - plain:
-            found = (found.astype(jnp.float32) * gain[...]).astype(out.dtype)
+            found = (found.astype(jnp.float32) * gain).astype(out.dtype)
         out[:, at : at + columns] = found
         at += columns
 
 
 def join_parts(parts, plain, left, ins, outs, scratch):
     def also(s):
-        @pl.when(s == 0)
+        @pl.when(s == 4)
         def _():
             joined_body(parts, plain, *ins, *outs)
 
-    return lambda barrier: 0, also, lambda: None, 1
+    return lambda barrier: 0, also, lambda: None, 5, False
 
 
 def joined(name, arrays, gain, parts, plain=0):
     columns = sum(part[2] for part in parts)
     return pl.pallas_call(
         functools.partial(joined_body, parts, plain),
-        out_shape=jax.ShapeDtypeStruct((gain.shape[0], columns), arrays[0].dtype),
+        out_shape=jax.ShapeDtypeStruct((gain.shape[1], columns), arrays[0].dtype),
         compiler_params=pltpu.CompilerParams(vmem_limit_bytes=VMEM),
         name=name,
     )(*arrays, gain)
 
 
-def hidden_pull_body(cotangent, w_down, both, d_pair):
+def mlp_pull_body(count, n, *refs):
+    pieces, refs = refs[: 2 * n - 1], refs[2 * n - 1 :]
+    w_down, both, hidden, unit, d_pair_out, grads, cotangent, d_pair, sems = refs
+    ups, downs = pieces[:1] + pieces[1::2], pieces[:1] + pieces[2::2]
+    step, me = pl.program_id(0), lax.axis_index(AXIS)
     columns = w_down.shape[1]
-    d_hidden = dot(cotangent[...], w_down[...])
-    gate, up = both[:, :columns], both[:, columns:]
-    slope = math.sqrt(2.0 / math.pi)
-    cubed = 0.044715 * gate * gate
-    bent = jnp.tanh(slope * gate * (1.0 + cubed))
-    half = 0.5 + 0.5 * bent
-    d_gelu = half + 0.5 * gate * (1.0 - bent * bent) * slope * (1.0 + 3.0 * cubed)
-    d_pair[:, :columns] = (d_hidden * up * d_gelu).astype(d_pair.dtype)
-    d_pair[:, columns:] = (d_hidden * gate * half).astype(d_pair.dtype)
-
-
-def hidden_pull(cotangent, mlp_full, both, hop):
-    length, width = cotangent.shape
-    columns = both.shape[1] // 2
+    rows = cotangent.shape[0] // n
+
+    def load(k, source):
+        return pltpu.make_async_copy(source, cotangent.at[pl.ds(k * rows, rows)], sems.at[k])
+
+    @pl.when(step == 0)
+    def _():
+        load(0, ups[0]).start()
+        for k in range(1, n):
+
+            @pl.when(me + k < n)
+            def _(k=k):
+                load(k, downs[k]).start()
+
+            @pl.when(me + k >= n)
+            def _(k=k):
+                load(k, ups[n - k]).start()
+
+    for k in range(n):
+
+        @pl.when(step == k * rows // ROWS)
+        def _(k=k):
+            load(k, ups[0]).wait()
+
+    @pl.when(step < count)
+    def _():
+        mine = pl.ds(pl.multiple_of(step * ROWS, ROWS), ROWS)
+        d_hidden = dot(cotangent[mine], w_down[...])
+        gate, up = both[:, :columns], both[:, columns:]
+        slope = math.sqrt(2.0 / math.pi)
+        cubed = 0.044715 * gate * gate
+        bent = jnp.tanh(slope * gate * (1.0 + cubed))
+        half = 0.5 + 0.5 * bent
+        d_gelu = half + 0.5 * gate * (1.0 - bent * bent) * slope * (1.0 + 3.0 * cubed)
+        d_gate = (d_hidden * up * d_gelu).astype(d_pair.dtype)
+        d_up = (d_hidden * gate * half).astype(d_pair.dtype)
+        for out in (d_pair_out, d_pair.at[mine]):
+            out[:, :columns] = d_gate
+            out[:, columns:] = d_up
+
+    @pl.when(step >= count)
+    def _():
+        at = pl.ds(pl.multiple_of((step - count) * ROWS, ROWS), ROWS)
+        grads[:, : 2 * columns] = dot(unit[...], d_pair[...], CONTRACT_ROWS).astype(grads.dtype)
+        grads[:, 2 * columns :] = dot(cotangent[:, at], hidden[...], CONTRACT_ROWS).astype(grads.dtype)
+
+
+def mlp_pull(pieces, mlp_full, both, hidden, unit, hop, then):
+    n = lax.axis_size(AXIS)
+    length, width = unit.shape
+    columns = hidden.shape[1]
+    count = length // ROWS
+    once = pl.Buffered(1)
     return hop_call(
-        hidden_pull_body,
+        functools.partial(mlp_pull_body, count, n),
         hop,
         7,
-        grid=(length // ROWS,),
-        in_specs=[
-            pl.BlockSpec((ROWS, width), lambda r: (r, 0)),
-            pl.BlockSpec((width, columns), lambda r: (0, 2), pipeline_mode=pl.Buffered(1)),
-            pl.BlockSpec((ROWS, 2 * columns), lambda r: (r, 0)),
+        then,
+        grid=(count + width // ROWS,),
+        in_specs=[pl.BlockSpec(memory_space=pl.ANY)] * len(pieces)
+        + [
+            pl.BlockSpec((width, columns), lambda i: (0, 2), pipeline_mode=once),
+            pl.BlockSpec((ROWS, 2 * columns), lambda i: (jnp.minimum(i, count - 1), 0)),
+            pl.BlockSpec((length, columns), lambda i: (0, 0), pipeline_mode=once),
+            pl.BlockSpec((length, ROWS), lambda i: (0, jnp.maximum(i - count, 0))),
         ],
-        out_specs=[pl.BlockSpec((ROWS, 2 * columns), lambda r: (r, 0))],
-        out_shape=[jax.ShapeDtypeStruct(both.shape, jnp.bfloat16)],
-        cost=work(2 * length * width * columns, both.size * 6 + cotangent.size * 4),
-        name="hidden_pull",
-    )(cotangent, mlp_full, both)
+        out_specs=[
+            pl.BlockSpec((ROWS, 2 * columns), lambda i: (jnp.minimum(i, count - 1), 0)),
+            pl.BlockSpec((ROWS, 3 * columns), lambda i: (jnp.maximum(i - count, 0), 0)),
+        ],
+        out_shape=[
+            jax.ShapeDtypeStruct((length, 2 * columns), jnp.bfloat16),
+            jax.ShapeDtypeStruct((width, 3 * columns), jnp.bfloat16),
+        ],
+        scratch_shapes=[
+            pltpu.VMEM((length, width), jnp.bfloat16),
+            pltpu.VMEM((length, 2 * columns), jnp.bfloat16),
+            pltpu.SemaphoreType.DMA((n,)),
+        ],
+        cost=work(8 * length * width * columns, 2 * (3 * length * width + 4 * width * columns + 8 * length * columns)),
+        name="mlp_pull",
+    )(*pieces, mlp_full, both, hidden, unit)
 
 
 def steps_of(part, parts):
@@ -995,33 +1125,15 @@
     return state, ("gather", steps[-1], *state[-2:]) if len(steps) else None
 
 
-def gather_end(state):
+def scatter_hop(part, steps, sums=None):
     n, me = lax.axis_size(AXIS), lax.axis_index(AXIS)
-    ups, downs = state[::2], state[1::2]
-    return jnp.concatenate([ups[0]] + [jnp.where(me + k < n, downs[k], ups[n - k]) for k in range(1, n)], axis=0)
-
-
-def scatter_masked(state, t):
-    n, me = lax.axis_size(AXIS), lax.axis_index(AXIS)
-    found = []
-    for sums, up in zip(state, (True, False)):
-        came = hop_valid("scatter", t - 1, me - 1 if up else me + 1, up)
-        found.append(jnp.where(came, sums, jnp.zeros_like(sums)).astype(jnp.float32))
-    return found
-
-
-def scatter_hop(state, part, steps):
-    n = lax.axis_size(AXIS)
     rows = part.shape[0] // n
-    for t in steps:
-        mine = [part[k * rows : (k + 1) * rows].astype(jnp.float32) for k in (n - 1 - t, 1 + t)]
-        if t:
-            mine = [own + sums for own, sums in zip(mine, scatter_masked(state, t))]
-        mine = [sums.astype(part.dtype) for sums in mine]
-        if t == steps[-1]:
-            return ("scatter", t, *mine)
-        state = [lax.ppermute(sums, AXIS, hops(way)) for sums, way in zip(mine, (True, False))]
-    return None
+    if sums is None:
+        sums = [part[k * rows : (k + 1) * rows] for k in (n - 1, 1)] if len(steps) > 1 else [part]
+    for t in steps[:-1]:
+        came = [lax.ppermute(rows_out, AXIS, hops(way)) for rows_out, way in zip(sums, (True, False))]
+        sums = [part[k * rows : (k + 1) * rows] + rows_in for k, rows_in in zip((n - 2 - t, 2 + t), came)]
+    return ("scatter", steps[-1], *sums)
 
 
 def shards(tokens,
@@ -1041,9 +1153,8 @@
     local_rows, width = tokens.shape
     heads = HEADS // lax.axis_size(AXIS)
     hidden_cols = w_mlp_gate.shape[1]
-    segments = segment_ids[0]
-    gain_one = attn_gain.astype(jnp.float32)[:, None]
-    gain_two = mlp_gain.astype(jnp.float32)[:, None]
+    gain_one = attn_gain.astype(jnp.float32)[None, :]
+    gain_two = mlp_gain.astype(jnp.float32)[None, :]
     after = lax.optimization_barrier
 
     def gather(own):
@@ -1056,7 +1167,7 @@
         return jnp.sum(weights.astype(jnp.float32) * grads.astype(jnp.float32), axis=1)
 
     in_parts = [(array, head, columns) for head in range(heads) for array, columns in enumerate((KD, KD, VD, VD))]
-    w_in_own = joined("join_in", [w_query, w_key, w_value, w_gate], gain_one, in_parts)
+    w_in_own = joined("join_in", [w_query, w_key, w_value, w_gate], attn_gain[None, :], in_parts)
     w_in = gather(w_in_own)
     unit_one, mlp_own = line_pass(
         "gather_one",
@@ -1070,15 +1181,15 @@
         local_rows,
         width,
         square=functools.partial(join_parts, [(i, 0, hidden_cols) for i in range(3)], 1),
-        square_ins=[w_mlp_gate, w_mlp_up, w_down, gain_two],
-        square_outs=[jax.ShapeDtypeStruct((gain_two.shape[0], 3 * hidden_cols), jnp.bfloat16)],
+        square_ins=[w_mlp_gate, w_mlp_up, w_down, mlp_gain[None, :]],
+        square_outs=[jax.ShapeDtypeStruct((gain_two.shape[1], 3 * hidden_cols), jnp.bfloat16)],
     )
     w_in, unit_one, w_out, cot_own, mlp_own = after((w_in, unit_one, w_out, cotangent, mlp_own))
     out_full = gather(w_out)
     cot, hop = gather_hop([cot_own, cot_own], steps_of(0, 3))
     projected, *came = project(unit_one, w_in, hop)
     cot, hop = gather_hop([*cot, *came], steps_of(1, 3))
-    kept, mixed, *came = retention(projected, segments, heads, hop)
+    kept, mixed, *came = retention(projected, segment_ids, heads, hop)
     cot = [*cot, *came]
     mixed, out_full, mlp_send, *cot = after((mixed, out_full, mlp_own, *cot))
     mlp_full = gather(mlp_send)
@@ -1101,30 +1212,37 @@
     unit_two, mlp_full, *cot = after((unit_two, mlp_full, *cot))
     cot, hop = gather_hop(cot, steps_of(2, 3))
     both_hidden, hidden, part_down, *came = hidden_layer(unit_two, mlp_full, hop)
-    cot_full = gather_end([*cot, *came])
-    (d_pair,) = hidden_pull(cot_full, mlp_full, both_hidden, None)
-    hop = scatter_hop(None, part_down, steps_of(0, 3))
-    grad_mlp, *sums = turned_dots([(unit_two, d_pair), (cot_full, hidden)], hop, 8, "mlp_grads")
+    hop = scatter_hop(part_down, steps_of(0, 3))
+    d_pair, grad_mlp, *sums = mlp_pull([*cot, *came][1:], mlp_full, both_hidden, hidden, unit_two, hop, (part_down,))
     mlp_grad = scatter(grad_mlp)
     d_branch_one, d_residual = line_pass(
-        "d_residual", (d_pair, mlp_full), [residual, cotangent], [jnp.float32], d_residual_step, True, 16, 2, local_rows, width, (True, False)
+        "d_residual",
+        (d_pair, mlp_full),
+        [residual, cotangent],
+        [jnp.float32],
+        d_residual_step,
+        True,
+        16,
+        2,
+        local_rows,
+        width,
+        (True, False),
     )
     d_branch_one, d_residual, mlp_grad = after((d_branch_one, d_residual, mlp_grad))
-    hop = scatter_hop(sums, part_down, steps_of(1, 3))
-    grad_out, *sums = turned_dots([(d_branch_one, mixed)], hop, 10, "out_grads")
+    hop = scatter_hop(part_down, steps_of(1, 3), sums)
+    grad_out, *sums = turned_dots([(d_branch_one, mixed)], hop, 10, (part_down,), "out_grads")
     out_grad = scatter(grad_out)
-    hop = scatter_hop(sums, part_down, steps_of(2, 3))
-    d_in, *sums = retention_pull(kept, projected, d_branch_one, out_full, segments, heads, hop)
-    sums = scatter_masked(sums, lax.axis_size(AXIS) - 1)
-    result = residual + part_down[:local_rows].astype(jnp.float32) + sum(sums)
-    result = result.astype(jnp.bfloat16)
+    hop = scatter_hop(part_down, steps_of(2, 3), sums)
+    d_in, result = retention_pull(
+        kept, projected, d_branch_one, out_full, segment_ids, heads, hop, (part_down, residual)
+    )
     pair_grad, down_grad = mlp_grad[:, : 2 * hidden_cols], mlp_grad[:, 2 * hidden_cols :].astype(jnp.float32)
     terms_two = gain_terms(mlp_own[:, : 2 * hidden_cols], pair_grad)
     terms_two = jnp.broadcast_to(terms_two[:, None], (terms_two.shape[0], 128))
-    pair_grad = pair_grad.astype(jnp.float32) * gain_two
+    pair_grad = pair_grad.astype(jnp.float32) * gain_two.T
     gate_grad, up_grad = pair_grad[:, :hidden_cols], pair_grad[:, hidden_cols:]
     d_in, result, gate_grad, up_grad, down_grad = after((d_in, result, gate_grad, up_grad, down_grad))
-    square_outs, square_scratch = square_shapes(gain_one.shape[0], heads, w_in.shape[1])
+    square_outs, square_scratch = square_shapes(gain_one.shape[1], heads, w_in.shape[1])
     tokens_grad, gain_sums, *in_grads = line_pass(
         "tokens_grad",
         (d_in, w_in),
@@ -1137,11 +1255,11 @@
         local_rows,
         width,
         square=functools.partial(square_parts, heads),
-        square_ins=[unit_turned, gain_one, w_in_own, terms_two],
+        square_ins=[unit_turned, gain_one, w_in_own, terms_two, gain_two],
         square_outs=square_outs,
         square_scratch=square_scratch,
     )
-    gain_sum_one, gain_sum_two = gain_sums[0, 0] / gain_one[:, 0], gain_sums[1, 0] / gain_two[:, 0]
+    gain_sum_one, gain_sum_two = gain_sums[0, 0], gain_sums[1, 0]
     return (
         result,
         tokens_grad,

time: 613 us -> 595 us (0.971)
  other arithmetic: 21.2 us -> 4.3 us
    convert_element_type x5 -> x1, other arithmetic: 10.1 us -> 0.01 us  [shards(): gain_two = mlp_gain.astype(jnp.float32)[None, :]]
    pallas_call x7 -> x6, Pallas kernels: 162 us -> 162 us  [hop_call(): return lambda *operands: call(*operands, *arrays, *added)]
  transfers between devices with their start and end apart: 5 -> 5, of which waited for: 0 -> 0; matrix products, arithmetic and copies ran while one was open for 3% -> 1% of each run, Pallas kernels for 78% -> 81%
where the time goes in v5:
time: 595 us; the launch traced here: 594 us
  Pallas kernels  564 us (95%)
  between operations  14 us (2%)
  local copies, waits for them, and re-layouts  11.7 us (2%)
    pallas_call x4, Pallas kernels, line_pass(): pl.pallas_call(functools.partial(line_body, n, chunks, rs, ag, rolled, mi...  399 us
    pallas_call x6, Pallas kernels, hop_call(): return lambda *operands: call(*operands, *arrays, *added)  162 us
  transfers between devices with their start and end apart: 5, of which 0 were waited for; matrix products, arithmetic and copies ran while one was open for 1% of the time, Pallas kernels for 81%

profile of v5, /device:TPU:0, one launch (start us, length us, event | category | flops | bytes accessed | tf_op | source)
XLA Modules:
  0.0 594.1 jit_solution(15261101762792279254)
XLA Ops:
  7.2 0.0 all-gather.4.cloned.1.call-start
  7.2 1.2 broadcast_in_dim.18.refs_4_
  8.4 2.9 join_in.1.refs_6_
  11.3 0.0 all-gather.4.cloned.1.call-update
  11.4 0.0 all-gather.6.cloned.1.call-start
  11.4 0.0 copy-done.9
  11.4 0.6 broadcast_in_dim.19.refs_4_
  12.0 76.0 %gather_one.1 = (bf16[1024,2048]{1,0:T(8,128)(2,1)}, bf16[256,3072]{1,0:T(8,128)(2,1)}) custom-call(bf16[256,2048]{1,0:T(8,128)(2,1)} %refs_2_.9, bf16[256,1024]{1,0:T(8,128)(2,1)} %refs_1_.3, bf16[256,1024]{1,0:T(8,128)(2,1)} %refs_2_.6, bf16[256,1024]{1,0:T(8,128)(2,1)} %refs_3_.5, bf16[1,256]{1,0:T(2,128)(2,1)} %broadcast_in_dim.19.refs_4_), custom_call_target="tpu_custom_call" | custom-call | bytes 125829120 | tf_op jit(solution)/shard_map/gather_one/pallas_call | solution.py:299
  88.0 0.0 all-gather.4.cloned.1.call-done.refs_1_
  88.0 0.0 all-gather.6.cloned.1.call-update
  88.1 0.0 all-gather.8.cloned.1.call-start
  88.1 29.3 %project.1 = (f32[1024,3072]{1,0:T(8,128)}, bf16[256,2048]{1,0:T(8,128)(2,1)}, bf16[256,2048]{1,0:T(8,128)(2,1)}) custom-call(bf16[1024,2048]{1,0:T(8,128)(2,1)} %get-tuple-element.76.refs_0_.refs_3_, bf16[2048,3072]{1,0:T(8,128)(2,1)} %all-gather.4.cloned.1.call-done.refs_1_, bf16[256,2048]{1,0:T(8,128)(2,1)} %refs_3_.7, bf16[256,2048]{1,0:T(8,128)(2,1)} %refs_3_.7), custom_call_target="tpu_custom_call" | custom-call | flops 12884901888 | bytes 29360128 | tf_op jit(solution)/shard_map/project/pallas_call | solution.py:768
  117.4 27.0 %retention.1 = (bf16[1024,2048]{1,0:T(8,128)(2,1)}, bf16[1024,1024]{1,0:T(8,128)(2,1)}, bf16[256,2048]{1,0:T(8,128)(2,1)}, bf16[256,2048]{1,0:T(8,128)(2,1)}) custom-call(f32[8]{0:T(128)} %constant.8.clone.refs_0_, f32[1024,3072]{1,0:T(8,128)} %get-tuple-element.79.refs_1_.refs_2_, f32[1024,128]{1,0:T(8,128)} %constant.9.clone.refs_2_.refs_5_, ...), custom_call_target="tpu_custom_call" | custom-call | flops 2415919104 | bytes 18874368 | tf_op jit(solution)/shard_map/retention/pallas_call | solution.py:768
  144.4 0.0 all-gather.6.cloned.1.call-done.refs_1_.refs_4_
  144.5 0.0 all-gather.8.cloned.1.call-update
  144.5 0.0 reduce-scatter.3.cloned.1.call-start
  144.5 117.7 %residual.1 = (bf16[1024,2048]{1,0:T(8,128)(2,1)}, f32[256,2048]{1,0:T(8,128)}, bf16[2048,1024]{1,0:T(8,128)(2,1)}) custom-call(bf16[1024,1024]{1,0:T(8,128)(2,1)} %get-tuple-element.88.refs_0_.refs_1_, bf16[2048,1024]{1,0:T(8,128)(2,1)} %all-gather.6.cloned.1.call-done.refs_1_.refs_4_, bf16[256,2048]{1,0:T(8,128)(2,1)} %refs_2_.9, ...), custom_call_target="tpu_custom_call" | custom-call | bytes 125829120 | tf_op jit(solution)/shard_map/residual/pallas_call | solution.py:299
  262.2 0.0 all-gather.8.cloned.1.call-done.refs_1_.refs_2_.refs_7_
  262.2 28.7 %hidden_layer.1 = (f32[1024,2048]{1,0:T(8,128)}, bf16[1024,1024]{1,0:T(8,128)(2,1)}, bf16[1024,2048]{1,0:T(8,128)(2,1)}, bf16[256,2048]{1,0:T(8,128)(2,1)}, bf16[256,2048]{1,0:T(8,128)(2,1)}) custom-call(bf16[1024,2048]{1,0:T(8,128)(2,1)} %get-tuple-element.102.refs_0_.refs_10_, bf16[2048,3072]{1,0:T(8,128)(2,1)} %all-gather.8.cloned.1.call-done.refs_1_.refs_2_.refs_7_, ...), custom_call_target="tpu_custom_call" | custom-call | flops 12884901888 | bytes 27262976 | tf_op jit(solution)/shard_map/hidden_layer/pallas_call | solution.py:768
  290.9 31.0 %mlp_pull.1 = (bf16[1024,2048]{1,0:T(8,128)(2,1)}, bf16[2048,3072]{1,0:T(8,128)(2,1)}, bf16[256,2048]{1,0:T(8,128)(2,1)}, bf16[256,2048]{1,0:T(8,128)(2,1)}) custom-call(bf16[256,2048]{1,0:T(8,128)(2,1)} %refs_3_.7, bf16[256,2048]{1,0:T(8,128)(2,1)} %get-tuple-element.98.refs_5_.refs_1_, bf16[256,2048]{1,0:T(8,128)(2,1)} %get-tuple-element.99.refs_6_.refs_2_, ...), custom_call_target="tpu_custom_call" | custom-call | flops 17179869184 | bytes 46137344 | tf_op jit(solution)/shard_map/mlp_pull/pallas_call | solution.py:768
  321.9 0.0 reduce-scatter.3.cloned.1.call-update
  322.0 0.0 reduce-scatter.5.cloned.1.call-start
  322.0 118.0 %d_residual.1 = (bf16[1024,2048]{1,0:T(8,128)(2,1)}, f32[256,2048]{1,0:T(8,128)}) custom-call(bf16[1024,2048]{1,0:T(8,128)(2,1)} %get-tuple-element.109.refs_0_, bf16[2048,3072]{1,0:T(8,128)(2,1)} %all-gather.8.cloned.1.call-done.refs_1_.refs_2_.refs_7_, f32[256,2048]{1,0:T(8,128)} %get-tuple-element.110.refs_2_.refs_11_, bf16[256,2048]{1,0:T(8,128)(2,1)} %refs_3_.7), custom_call_target="tpu_custom_call" | custom-call | bytes 125829120 | tf_op jit(solution)/shard_map/d_residual/pallas_call | solution.py:299
  440.1 0.0 reduce-scatter.3.cloned.1.call-done
  440.1 18.4 %out_grads.1 = (bf16[2048,1024]{1,0:T(8,128)(2,1)}, bf16[256,2048]{1,0:T(8,128)(2,1)}, bf16[256,2048]{1,0:T(8,128)(2,1)}) custom-call(bf16[1024,2048]{1,0:T(8,128)(2,1)} %get-tuple-element.114.refs_0_.refs_3_, bf16[1024,1024]{1,0:T(8,128)(2,1)} %get-tuple-element.88.refs_0_.refs_1_, bf16[256,2048]{1,0:T(8,128)(2,1)} %get-tuple-element.115.refs_2_, ...), custom_call_target="tpu_custom_call" | custom-call | flops 4294967296 | bytes 10485760 | tf_op jit(solution)/shard_map/out_grads/pallas_call | solution.py:768
  458.5 0.0 copy-start.10
  458.5 0.0 copy-start.1
  458.5 0.0 reduce-scatter.5.cloned.1.call-update
  458.5 0.6 copy-done.10
  459.1 0.6 reshape_convert_fusion.refs_5_
  459.7 0.2 copy-done.1
  459.9 1.1 slice_convert_fusion
  461.0 0.5 fusion
  461.5 0.0 copy-done.8
  461.5 1.5 fusion.1
  463.0 27.5 %retention_pull.1 = (bf16[1024,3072]{1,0:T(8,128)(2,1)}, bf16[256,2048]{1,0:T(8,128)(2,1)}) custom-call(f32[8]{0:T(128)} %constant.8.clone.refs_0_, bf16[1024,2048]{1,0:T(8,128)(2,1)} %get-tuple-element.82.refs_1_, f32[1024,3072]{1,0:T(8,128)} %get-tuple-element.79.refs_1_.refs_2_, bf16[1024,2048]{1,0:T(8,128)(2,1)} %get-tuple-element.114.refs_0_.refs_3_, ...), custom_call_target="tpu_custom_call" | custom-call | flops 11542724608 | bytes 25165824 | tf_op jit(solution)/shard_map/retention_pull/pallas_call | solution.py:768
  490.5 0.8 broadcast_in_dim.21.refs_7_
  491.2 87.2 %tokens_grad.1 = (bf16[256,2048]{1,0:T(8,128)(2,1)}, f32[2,8,256]{2,1,0:T(8,128)}, f32[256,512]{1,0:T(8,128)}, f32[256,512]{1,0:T(8,128)}, f32[256,1024]{1,0:T(8,128)}, /*index=5*/f32[256,1024]{1,0:T(8,128)}) custom-call(bf16[1024,3072]{1,0:T(8,128)(2,1)} %get-tuple-element.123.refs_0_, bf16[2048,3072]{1,0:T(8,128)(2,1)} %all-gather.4.cloned.1.call-done.refs_1_, ...), custom_call_target="tpu_custom_call" | custom-call | bytes 125829120 | tf_op jit(solution)/shard_map/tokens_grad/pallas_call | solution.py:299
  578.5 1.4 fusion.2
  579.9 2.1 convert_element_type.21
  582.1 1.0 copy.37
  583.0 1.0 copy.38
  584.0 0.8 copy.39
  584.8 0.8 copy.40
  585.6 0.0 copy-done.4
  585.6 1.0 copy.41
  586.6 0.0 copy-done.3
  586.6 1.0 copy.42
  (16 shorter events, 0.0 us)
Async XLA Ops:
  7.2 80.9 %all-gather.4.cloned.1.call-start = ((), (), s32[]{:S(2)}) async-start(), calls=%async_computation.2 | async-start | bytes 14155776 | tf_op jit(solution)/shard_map/all_gather | solution.py:1161
  8.4 3.0 copy-start.9
  11.4 133.1 %all-gather.6.cloned.1.call-start = ((), (), s32[]{:S(2)}) async-start(), calls=%async_computation.3 | async-start | bytes 4718592 | tf_op jit(solution)/shard_map/all_gather | solution.py:1161
  88.1 174.2 %all-gather.8.cloned.1.call-start = ((), (), s32[]{:S(2)}) async-start(), calls=%async_computation.4 | async-start | bytes 14155776 | tf_op jit(solution)/shard_map/all_gather | solution.py:1161
  144.5 295.6 %reduce-scatter.3.cloned.1.call-start = ((), (), s32[]{:S(2)}) async-start(), calls=%async_computation.5 | async-start | bytes 14155776 | tf_op jit(solution)/shard_map/reduce_scatter | solution.py:1164
  322.0 258.0 %reduce-scatter.5.cloned.1.call-start = ((), (), s32[]{:S(2)}) async-start(), calls=%async_computation.6 | async-start | bytes 4718592 | tf_op jit(solution)/shard_map/reduce_scatter | solution.py:1164
  458.5 0.7 copy-start.10
  458.5 1.4 copy-start.1
  458.5 2.5 copy-start
  459.1 2.4 copy-start.8
  578.5 3.6 copy-start.2
  578.5 4.5 copy-start.5
  582.1 2.0 copy-start.7
  583.0 1.8 copy-start.6
  583.0 2.6 copy-start.4
  584.0 2.6 copy-start.3
Sparse Core Ops, SparseCore 0:
  11.5 74.8 all-gather.3
  88.2 36.7 all-gather.5
  144.6 70.6 all-gather.7
  322.1 90.9 reduce-scatter.2
  458.6 54.4 reduce-scatter.4

commit v6 on v5

--- a/solution.py
+++ b/solution.py
@@ -439,8 +439,8 @@
                 if bit < line_bits:
                     sums_copy(bit).start()
                 else:
-                    gain_sum[0] = sums[bit, 0] / gain[...]
-                    gain_sum[1] = sums[bit, 1] / other_gain[...]
+                    gain_sum[0] = sums[bit, 0] / as_row(gain)
+                    gain_sum[1] = sums[bit, 1] / as_row(other_gain)
 
     def result(p, side, summed):
         at = pl.ds(pl.multiple_of(p * wide + side * half, half), half)
@@ -458,7 +458,7 @@
             def _():
                 terms_one[...] += terms
 
-        summed = summed * as_column(gain[...])
+        summed = summed * as_column(as_row(gain))
         for found in range(pairs):
             head, kind = found // (pairs // heads), found % (pairs // heads)
             where = grads[side] if kind == 0 else grads[1 + kind]
@@ -564,10 +564,15 @@
     return centred * inverse, inverse
 
 
-def retention_body(block, reach, log_ref, proj, cosine, sine, segments, kept, mixed, keys, vals, decay, seg_line):
+def retention_body(block, reach, log_ref, proj, cosine, sine, segments, *refs):
+    *arrays, kept, mixed, joined, keys, vals, decay, seg_line = refs
     head, row = pl.program_id(0), pl.program_id(1)
     here = pl.ds(pl.multiple_of(reach + row * block, block), block)
     window = pl.ds(pl.multiple_of(row * block, block), reach + block)
+
+    @pl.when((head == 0) & (row == 0))
+    def _():
+        joined_body([(i, 0, arrays[i].shape[1]) for i in range(len(arrays) - 1)], 1, *arrays, joined)
 
     @pl.when(row == 0)
     def _():
@@ -638,7 +643,7 @@
     return inside & ((passed >= t) if kind == "gather" else (passed <= t))
 
 
-def hop_call(body, hop, collective_id, then=None, *, grid, in_specs, out_specs, out_shape, scratch_shapes=(), cost, name):
+def hop_call(body, hop, collective_id, then=None, resident=(), *, grid, in_specs, out_specs, out_shape, scratch_shapes=(), cost, name):
     def params(**more):
         return pltpu.CompilerParams(vmem_limit_bytes=VMEM, **more)
 
@@ -665,7 +670,8 @@
     def with_hop(*refs):
         ins, sources, refs = refs[:n_in], refs[n_in : n_in + n_sent], refs[n_in + n_sent :]
         terms, outs, refs = refs[: len(added)], refs[len(added) : len(added) + n_out], refs[len(added) + n_out :]
-        targets, (*scratch, send_sems, recv_sems) = refs[:n_got], refs[n_got:]
+        targets, (*scratch, send_sems, recv_sems, load_sems) = refs[:n_got], refs[n_got:]
+        held, scratch = scratch[: len(resident)], scratch[len(resident) :]
         found = targets
         if added:
             *scratch, came, mine, mine_sems = scratch
@@ -716,10 +722,21 @@
                 def _(way=way):
                     copy(way).start()
 
+            loads = [
+                pltpu.make_async_copy(ins[i].at[:, pl.ds(column, ref.shape[1])], ref, load_sems.at[k])
+                for k, (i, column, ref) in enumerate(zip(resident, columns, held))
+            ]
+            for load in loads:
+                load.start()
             for term in term_copies():
                 term.start()
-
-        body(*ins, *outs, *scratch)
+            for load in loads:
+                load.wait()
+
+        inside = list(ins)
+        for i, ref in zip(resident, held):
+            inside[i] = ref
+        body(*inside, *outs, *scratch)
 
         @pl.when(at_last)
         def _():
@@ -748,6 +765,9 @@
                 found[0][...] = kept[...].astype(shape.dtype)
 
     anywhere = pl.BlockSpec(memory_space=pl.ANY)
+    blocks = [in_specs[i].block_shape for i in resident]
+    columns = [in_specs[i].index_map(*[0] * len(grid))[1] * block[1] for i, block in zip(resident, blocks)]
+    in_specs = [anywhere if i in resident else spec for i, spec in enumerate(in_specs)]
     got = pl.BlockSpec((rows, width), lambda *_: (0, 0)) if added else anywhere
     more = []
     if len(added) == 2:
@@ -760,7 +780,14 @@
         in_specs=[*in_specs, *[anywhere] * (n_sent + len(added))],
         out_specs=[*out_specs, *[got] * n_got],
         out_shape=[*out_shape, *[shape] * n_got],
-        scratch_shapes=[*scratch_shapes, *more, pltpu.SemaphoreType.DMA((2,)), pltpu.SemaphoreType.DMA((2,))],
+        scratch_shapes=[
+            *[pltpu.VMEM(block, jnp.bfloat16) for block in blocks],
+            *scratch_shapes,
+            *more,
+            pltpu.SemaphoreType.DMA((2,)),
+            pltpu.SemaphoreType.DMA((2,)),
+            pltpu.SemaphoreType.DMA((max(len(blocks), 1),)),
+        ],
         compiler_params=params(collective_id=collective_id, has_side_effects=True),
         cost_estimate=cost,
         name=name,
@@ -789,6 +816,7 @@
         functools.partial(project_body, ROWS),
         hop,
         4,
+        resident=(0,),
         grid=(columns // tile,),
         in_specs=[pl.BlockSpec((length, depth), lambda c: (0, 0)), pl.BlockSpec((depth, tile), lambda c: (0, c))],
         out_specs=[pl.BlockSpec((length, tile), lambda c: (0, c))],
@@ -814,6 +842,7 @@
         hidden_body,
         hop,
         6,
+        resident=(1, 2),
         grid=(length // ROWS,),
         in_specs=[
             pl.BlockSpec((ROWS, width), lambda r: (r, 0)),
@@ -856,6 +885,7 @@
         hop,
         collective_id,
         then,
+        tuple(range(1, 2 * len(pairs), 2)),
         grid=(width // ROWS,),
         in_specs=specs,
         out_specs=[pl.BlockSpec((ROWS, columns), lambda r: (r, 0))],
@@ -873,16 +903,18 @@
     return block, reach, log_decay
 
 
-def retention(projected, segments, heads, hop):
+def retention(projected, segments, heads, hop, to_join):
     length = projected.shape[0]
     block, reach, log_decay = retention_inputs(segments)
     cosine, sine = rotary_tables(length)
     per_head = projected.shape[1] // heads
+    joined = (to_join[0].shape[0], sum(array.shape[1] for array in to_join[:-1]))
     table = pl.BlockSpec((block, KD // 2), lambda h, r: (r, 0))
     return hop_call(
         functools.partial(retention_body, block, reach),
         hop,
         5,
+        resident=tuple(range(5, 4 + len(to_join))),
         grid=(heads, length // block),
         in_specs=[
             pl.BlockSpec(memory_space=pltpu.SMEM),
@@ -890,14 +922,18 @@
             table,
             table,
             pl.BlockSpec(segments.shape, lambda h, r: (0, 0)),
+            *[pl.BlockSpec(array.shape, lambda h, r: (0, 0)) for array in to_join[:-1]],
+            pl.BlockSpec(to_join[-1].shape, lambda h, r: (0,)),
         ],
         out_specs=[
             pl.BlockSpec((block, 2 * KD + VD), lambda h, r: (r, h)),
             pl.BlockSpec((block, VD), lambda h, r: (r, h)),
+            pl.BlockSpec(joined, lambda h, r: (0, 0)),
         ],
         out_shape=[
             jax.ShapeDtypeStruct((length, heads * (2 * KD + VD)), jnp.bfloat16),
             jax.ShapeDtypeStruct((length, heads * VD), jnp.bfloat16),
+            jax.ShapeDtypeStruct(joined, jnp.bfloat16),
         ],
         scratch_shapes=[
             pltpu.VMEM((reach + length, KD), jnp.bfloat16),
@@ -907,7 +943,7 @@
         ],
         cost=work(2 * heads * length * (reach + block) * (KD + VD), projected.size * 6),
         name="retention",
-    )(log_decay, projected, cosine, sine, segments)
+    )(log_decay, projected, cosine, sine, segments, *to_join)
 
 
 def retention_pull(kept, projected, d_branch, w_out, segments, heads, hop, then):
@@ -988,13 +1024,17 @@
     return [(i, i + 1) if up else (i + 1, i) for i in range(n - 1)]
 
 
+def as_row(ref):
+    return ref[...].astype(jnp.float32).reshape(1, -1)
+
+
 def as_column(row):
     return jnp.broadcast_to(row, (128, row.shape[1])).T[:, :1]
 
 
 def joined_body(parts, plain, *refs):
     *arrays, gain_row, out = refs
-    gain = as_column(gain_row[...].astype(jnp.float32))
+    gain = as_column(as_row(gain_row))
     at = 0
     for array, index, columns in parts:
         found = arrays[array][:, index * columns : (index + 1) * columns]
@@ -1004,20 +1044,11 @@
         at += columns
 
 
-def join_parts(parts, plain, left, ins, outs, scratch):
-    def also(s):
-        @pl.when(s == 4)
-        def _():
-            joined_body(parts, plain, *ins, *outs)
-
-    return lambda barrier: 0, also, lambda: None, 5, False
-
-
 def joined(name, arrays, gain, parts, plain=0):
     columns = sum(part[2] for part in parts)
     return pl.pallas_call(
         functools.partial(joined_body, parts, plain),
-        out_shape=jax.ShapeDtypeStruct((gain.shape[1], columns), arrays[0].dtype),
+        out_shape=jax.ShapeDtypeStruct((gain.shape[0], columns), arrays[0].dtype),
         compiler_params=pltpu.CompilerParams(vmem_limit_bytes=VMEM),
         name=name,
     )(*arrays, gain)
@@ -1087,6 +1118,7 @@
         hop,
         7,
         then,
+        (len(pieces), len(pieces) + 2),
         grid=(count + width // ROWS,),
         in_specs=[pl.BlockSpec(memory_space=pl.ANY)] * len(pieces)
         + [
@@ -1153,8 +1185,6 @@
     local_rows, width = tokens.shape
     heads = HEADS // lax.axis_size(AXIS)
     hidden_cols = w_mlp_gate.shape[1]
-    gain_one = attn_gain.astype(jnp.float32)[None, :]
-    gain_two = mlp_gain.astype(jnp.float32)[None, :]
     after = lax.optimization_barrier
 
     def gather(own):
@@ -1167,29 +1197,17 @@
         return jnp.sum(weights.astype(jnp.float32) * grads.astype(jnp.float32), axis=1)
 
     in_parts = [(array, head, columns) for head in range(heads) for array, columns in enumerate((KD, KD, VD, VD))]
-    w_in_own = joined("join_in", [w_query, w_key, w_value, w_gate], attn_gain[None, :], in_parts)
+    w_in_own = joined("join_in", [w_query, w_key, w_value, w_gate], attn_gain, in_parts)
     w_in = gather(w_in_own)
-    unit_one, mlp_own = line_pass(
-        "gather_one",
-        None,
-        [tokens],
-        [],
-        unit_step,
-        True,
-        4,
-        0,
-        local_rows,
-        width,
-        square=functools.partial(join_parts, [(i, 0, hidden_cols) for i in range(3)], 1),
-        square_ins=[w_mlp_gate, w_mlp_up, w_down, mlp_gain[None, :]],
-        square_outs=[jax.ShapeDtypeStruct((gain_two.shape[1], 3 * hidden_cols), jnp.bfloat16)],
-    )
-    w_in, unit_one, w_out, cot_own, mlp_own = after((w_in, unit_one, w_out, cotangent, mlp_own))
+    (unit_one,) = line_pass("gather_one", None, [tokens], [], unit_step, True, 4, 0, local_rows, width)
+    w_in, unit_one, w_out, cot_own = after((w_in, unit_one, w_out, cotangent))
     out_full = gather(w_out)
     cot, hop = gather_hop([cot_own, cot_own], steps_of(0, 3))
     projected, *came = project(unit_one, w_in, hop)
     cot, hop = gather_hop([*cot, *came], steps_of(1, 3))
-    kept, mixed, *came = retention(projected, segment_ids, heads, hop)
+    kept, mixed, mlp_own, *came = retention(
+        projected, segment_ids, heads, hop, [w_mlp_gate, w_mlp_up, w_down, mlp_gain]
+    )
     cot = [*cot, *came]
     mixed, out_full, mlp_send, *cot = after((mixed, out_full, mlp_own, *cot))
     mlp_full = gather(mlp_send)
@@ -1239,10 +1257,10 @@
     pair_grad, down_grad = mlp_grad[:, : 2 * hidden_cols], mlp_grad[:, 2 * hidden_cols :].astype(jnp.float32)
     terms_two = gain_terms(mlp_own[:, : 2 * hidden_cols], pair_grad)
     terms_two = jnp.broadcast_to(terms_two[:, None], (terms_two.shape[0], 128))
-    pair_grad = pair_grad.astype(jnp.float32) * gain_two.T
+    pair_grad = pair_grad.astype(jnp.float32) * mlp_gain.astype(jnp.float32)[:, None]
     gate_grad, up_grad = pair_grad[:, :hidden_cols], pair_grad[:, hidden_cols:]
     d_in, result, gate_grad, up_grad, down_grad = after((d_in, result, gate_grad, up_grad, down_grad))
-    square_outs, square_scratch = square_shapes(gain_one.shape[1], heads, w_in.shape[1])
+    square_outs, square_scratch = square_shapes(attn_gain.shape[0], heads, w_in.shape[1])
     tokens_grad, gain_sums, *in_grads = line_pass(
         "tokens_grad",
         (d_in, w_in),
@@ -1255,7 +1273,7 @@
         local_rows,
         width,
         square=functools.partial(square_parts, heads),
-        square_ins=[unit_turned, gain_one, w_in_own, terms_two, gain_two],
+        square_ins=[unit_turned, attn_gain, w_in_own, terms_two, mlp_gain],
         square_outs=square_outs,
         square_scratch=square_scratch,
     )

time: 595 us -> 593 us (level)
  transfers between devices with their start and end apart: 5 -> 5, of which waited for: 0 -> 1; matrix products, arithmetic and copies ran while one was open for 1% -> 1% of each run, Pallas kernels for 81% -> 82%
where the time goes in v6:
time: 593 us; the launch traced here: 592 us
  Pallas kernels  563 us (95%)
  between operations  14 us (2%)
  local copies, waits for them, and re-layouts  10.5 us (2%)
    pallas_call x4, Pallas kernels, line_pass(): pl.pallas_call(functools.partial(line_body, n, chunks, rs, ag, rolled, mi...  399 us
    pallas_call x6, Pallas kernels, hop_call(): return lambda *operands: call(*operands, *arrays, *added)  161 us
  transfers between devices with their start and end apart: 5, of which 1 were waited for; matrix products, arithmetic and copies ran while one was open for 1% of the time, Pallas kernels for 82%

profile of v6, /device:TPU:0, one launch (start us, length us, event | category | flops | bytes accessed | tf_op | source)
XLA Modules:
  0.0 591.8 jit_solution(1479756423359480960)
XLA Ops:
  7.2 0.0 all-gather.4.cloned.1.call-start
  7.2 2.9 join_in.1.refs_6_
  10.1 0.0 all-gather.4.cloned.1.call-update
  10.1 0.0 all-gather.6.cloned.1.call-start
  10.2 74.4 %gather_one.1.refs_0_.refs_3_ = bf16[1024,2048]{1,0:T(8,128)(2,1)} custom-call(bf16[256,2048]{1,0:T(8,128)(2,1)} %refs_2_.7), custom_call_target="tpu_custom_call" | custom-call | bytes 125829120 | tf_op jit(solution)/shard_map/gather_one/pallas_call | solution.py:299
  84.6 0.5 all-gather.4.cloned.1.call-done.refs_1_
  85.1 0.0 all-gather.6.cloned.1.call-update
  85.1 0.0 all-gather.8.cloned.1.call-start
  85.2 29.7 %project.1 = (f32[1024,3072]{1,0:T(8,128)}, bf16[256,2048]{1,0:T(8,128)(2,1)}, bf16[256,2048]{1,0:T(8,128)(2,1)}) custom-call(bf16[1024,2048]{1,0:T(8,128)(2,1)} %gather_one.1.refs_0_.refs_3_, bf16[2048,3072]{1,0:T(8,128)(2,1)} %all-gather.4.cloned.1.call-done.refs_1_, bf16[256,2048]{1,0:T(8,128)(2,1)} %refs_3_.5, bf16[256,2048]{1,0:T(8,128)(2,1)} %refs_3_.5), custom_call_target="tpu_custom_call" | custom-call | flops 12884901888 | bytes 29360128 | tf_op jit(solution)/shard_map/project/pallas_call | solution.py:795
  114.9 28.1 %retention.1 = (bf16[1024,2048]{1,0:T(8,128)(2,1)}, bf16[1024,1024]{1,0:T(8,128)(2,1)}, bf16[256,3072]{1,0:T(8,128)(2,1)}, bf16[256,2048]{1,0:T(8,128)(2,1)}, bf16[256,2048]{1,0:T(8,128)(2,1)}) custom-call(f32[8]{0:T(128)} %constant.8.clone.refs_0_, f32[1024,3072]{1,0:T(8,128)} %get-tuple-element.75.refs_1_.refs_2_, ...), custom_call_target="tpu_custom_call" | custom-call | flops 2415919104 | bytes 18874368 | tf_op jit(solution)/shard_map/retention/pallas_call | solution.py:795
  142.9 0.0 all-gather.6.cloned.1.call-done.refs_1_.refs_4_
  143.0 0.0 all-gather.8.cloned.1.call-update
  143.0 0.0 reduce-scatter.3.cloned.1.call-start
  143.0 117.6 %residual.1 = (bf16[1024,2048]{1,0:T(8,128)(2,1)}, f32[256,2048]{1,0:T(8,128)}, bf16[2048,1024]{1,0:T(8,128)(2,1)}) custom-call(bf16[1024,1024]{1,0:T(8,128)(2,1)} %get-tuple-element.84.refs_0_.refs_1_, bf16[2048,1024]{1,0:T(8,128)(2,1)} %all-gather.6.cloned.1.call-done.refs_1_.refs_4_, bf16[256,2048]{1,0:T(8,128)(2,1)} %refs_2_.7, ...), custom_call_target="tpu_custom_call" | custom-call | bytes 125829120 | tf_op jit(solution)/shard_map/residual/pallas_call | solution.py:299
  260.6 0.0 all-gather.8.cloned.1.call-done.refs_1_.refs_2_.refs_7_
  260.7 25.8 %hidden_layer.1 = (f32[1024,2048]{1,0:T(8,128)}, bf16[1024,1024]{1,0:T(8,128)(2,1)}, bf16[1024,2048]{1,0:T(8,128)(2,1)}, bf16[256,2048]{1,0:T(8,128)(2,1)}, bf16[256,2048]{1,0:T(8,128)(2,1)}) custom-call(bf16[1024,2048]{1,0:T(8,128)(2,1)} %get-tuple-element.98.refs_0_.refs_10_, bf16[2048,3072]{1,0:T(8,128)(2,1)} %all-gather.8.cloned.1.call-done.refs_1_.refs_2_.refs_7_, ...), custom_call_target="tpu_custom_call" | custom-call | flops 12884901888 | bytes 27262976 | tf_op jit(solution)/shard_map/hidden_layer/pallas_call | solution.py:795
  286.5 31.5 %mlp_pull.1 = (bf16[1024,2048]{1,0:T(8,128)(2,1)}, bf16[2048,3072]{1,0:T(8,128)(2,1)}, bf16[256,2048]{1,0:T(8,128)(2,1)}, bf16[256,2048]{1,0:T(8,128)(2,1)}) custom-call(bf16[256,2048]{1,0:T(8,128)(2,1)} %refs_3_.5, bf16[256,2048]{1,0:T(8,128)(2,1)} %get-tuple-element.94.refs_9_.refs_1_, bf16[256,2048]{1,0:T(8,128)(2,1)} %get-tuple-element.95.refs_10_.refs_2_, ...), custom_call_target="tpu_custom_call" | custom-call | flops 17179869184 | bytes 46137344 | tf_op jit(solution)/shard_map/mlp_pull/pallas_call | solution.py:795
  318.0 0.0 reduce-scatter.3.cloned.1.call-update
  318.0 0.0 reduce-scatter.5.cloned.1.call-start
  318.0 118.3 %d_residual.1 = (bf16[1024,2048]{1,0:T(8,128)(2,1)}, f32[256,2048]{1,0:T(8,128)}) custom-call(bf16[1024,2048]{1,0:T(8,128)(2,1)} %get-tuple-element.105.refs_0_, bf16[2048,3072]{1,0:T(8,128)(2,1)} %all-gather.8.cloned.1.call-done.refs_1_.refs_2_.refs_7_, f32[256,2048]{1,0:T(8,128)} %get-tuple-element.106.refs_2_.refs_11_, bf16[256,2048]{1,0:T(8,128)(2,1)} %refs_3_.5), custom_call_target="tpu_custom_call" | custom-call | bytes 125829120 | tf_op jit(solution)/shard_map/d_residual/pallas_call | solution.py:299
  436.3 0.0 reduce-scatter.3.cloned.1.call-done
  436.3 19.1 %out_grads.1 = (bf16[2048,1024]{1,0:T(8,128)(2,1)}, bf16[256,2048]{1,0:T(8,128)(2,1)}, bf16[256,2048]{1,0:T(8,128)(2,1)}) custom-call(bf16[1024,2048]{1,0:T(8,128)(2,1)} %get-tuple-element.110.refs_0_.refs_3_, bf16[1024,1024]{1,0:T(8,128)(2,1)} %get-tuple-element.84.refs_0_.refs_1_, bf16[256,2048]{1,0:T(8,128)(2,1)} %get-tuple-element.111.refs_2_, ...), custom_call_target="tpu_custom_call" | custom-call | flops 4294967296 | bytes 10485760 | tf_op jit(solution)/shard_map/out_grads/pallas_call | solution.py:795
  455.4 0.0 copy-start.8
  455.4 0.0 copy-start.1
  455.4 0.0 copy-start
  455.4 0.0 reduce-scatter.5.cloned.1.call-update
  455.5 0.6 copy-done.8
  456.1 0.8 copy-done.1
  456.8 1.1 slice_convert_fusion
  457.9 0.0 copy-done
  457.9 0.5 fusion
  458.5 1.5 fusion.1
  459.9 26.6 %retention_pull.1 = (bf16[1024,3072]{1,0:T(8,128)(2,1)}, bf16[256,2048]{1,0:T(8,128)(2,1)}) custom-call(f32[8]{0:T(128)} %constant.8.clone.refs_0_, bf16[1024,2048]{1,0:T(8,128)(2,1)} %get-tuple-element.78.refs_1_, f32[1024,3072]{1,0:T(8,128)} %get-tuple-element.75.refs_1_.refs_2_, bf16[1024,2048]{1,0:T(8,128)(2,1)} %get-tuple-element.110.refs_0_.refs_3_, ...), custom_call_target="tpu_custom_call" | custom-call | flops 11542724608 | bytes 25165824 | tf_op jit(solution)/shard_map/retention_pull/pallas_call | solution.py:795
  486.6 0.8 broadcast_in_dim.2.refs_7_
  487.3 88.9 %tokens_grad.1 = (bf16[256,2048]{1,0:T(8,128)(2,1)}, f32[2,8,256]{2,1,0:T(8,128)}, f32[256,512]{1,0:T(8,128)}, f32[256,512]{1,0:T(8,128)}, f32[256,1024]{1,0:T(8,128)}, /*index=5*/f32[256,1024]{1,0:T(8,128)}) custom-call(bf16[1024,3072]{1,0:T(8,128)(2,1)} %get-tuple-element.119.refs_0_, bf16[2048,3072]{1,0:T(8,128)(2,1)} %all-gather.4.cloned.1.call-done.refs_1_, ...), custom_call_target="tpu_custom_call" | custom-call | bytes 125829120 | tf_op jit(solution)/shard_map/tokens_grad/pallas_call | solution.py:299
  576.2 0.0 copy-start.2
  576.2 0.0 copy-start.5
  576.2 1.4 fusion.2
  577.7 2.1 convert_element_type.20
  579.8 0.0 copy-done.2
  579.8 1.0 copy.37
  580.8 1.0 copy.38
  581.7 0.0 copy-done.7
  581.7 0.8 copy.39
  582.5 0.0 copy-done.6
  582.5 0.8 copy.40
  583.3 1.0 copy.41
  584.3 1.0 copy.42
  (9 shorter events, 0.0 us)
Async XLA Ops:
  7.2 77.9 %all-gather.4.cloned.1.call-start = ((), (), s32[]{:S(2)}) async-start(), calls=%async_computation.2 | async-start | bytes 14155776 | tf_op jit(solution)/shard_map/all_gather | solution.py:1191
  10.1 132.8 %all-gather.6.cloned.1.call-start = ((), (), s32[]{:S(2)}) async-start(), calls=%async_computation.3 | async-start | bytes 4718592 | tf_op jit(solution)/shard_map/all_gather | solution.py:1191
  85.1 175.5 %all-gather.8.cloned.1.call-start = ((), (), s32[]{:S(2)}) async-start(), calls=%async_computation.4 | async-start | bytes 14155776 | tf_op jit(solution)/shard_map/all_gather | solution.py:1191
  143.0 293.3 %reduce-scatter.3.cloned.1.call-start = ((), (), s32[]{:S(2)}) async-start(), calls=%async_computation.5 | async-start | bytes 14155776 | tf_op jit(solution)/shard_map/reduce_scatter | solution.py:1194
  318.0 259.7 %reduce-scatter.5.cloned.1.call-start = ((), (), s32[]{:S(2)}) async-start(), calls=%async_computation.6 | async-start | bytes 4718592 | tf_op jit(solution)/shard_map/reduce_scatter | solution.py:1194
  455.4 0.7 copy-start.8
  455.4 1.4 copy-start.1
  455.4 2.5 copy-start
  576.2 3.6 copy-start.2
  576.2 4.5 copy-start.5
  579.8 2.0 copy-start.7
  580.8 1.8 copy-start.6
  580.8 2.6 copy-start.4
  581.7 2.6 copy-start.3
Sparse Core Ops, SparseCore 0:
  10.3 74.8 all-gather.3
  87.0 36.7 all-gather.5
  143.1 71.2 all-gather.7
  318.1 91.1 reduce-scatter.2
  455.6 53.2 reduce-scatter.4

commit v7 on v6

--- a/solution.py
+++ b/solution.py
@@ -234,11 +234,13 @@
 
     def drain(c, _):
         if rs:
-            for d in range(n):
+            for d in range(1, n):
 
                 @pl.when(me < d)
                 def _(d=d):
                     sum_copy(True, d, c).wait_send()
+
+            for d in range(last):
 
                 @pl.when(me > d)
                 def _(d=d):

time: 593 us -> 593 us (level)
  no operation moved by 1% of the time
where the time goes in v7:
time: 593 us; the launch traced here: 592 us
  Pallas kernels  563 us (95%)
  between operations  14 us (2%)
  local copies, waits for them, and re-layouts  10.5 us (2%)
    pallas_call x4, Pallas kernels, line_pass(): pl.pallas_call(functools.partial(line_body, n, chunks, rs, ag, rolled, mi...  399 us
    pallas_call x6, Pallas kernels, hop_call(): return lambda *operands: call(*operands, *arrays, *added)  161 us
  transfers between devices with their start and end apart: 5, of which 1 were waited for; matrix products, arithmetic and copies ran while one was open for 1% of the time, Pallas kernels for 82%

profile of v7, /device:TPU:0, one launch (start us, length us, event | category | flops | bytes accessed | tf_op | source)
XLA Modules:
  0.0 591.8 jit_solution(15172970839068510503)
XLA Ops:
  7.2 0.0 all-gather.4.cloned.1.call-start
  7.2 2.9 join_in.1.refs_6_
  10.1 0.0 all-gather.4.cloned.1.call-update
  10.1 0.0 all-gather.6.cloned.1.call-start
  10.2 74.4 %gather_one.1.refs_0_.refs_3_ = bf16[1024,2048]{1,0:T(8,128)(2,1)} custom-call(bf16[256,2048]{1,0:T(8,128)(2,1)} %refs_2_.7), custom_call_target="tpu_custom_call" | custom-call | bytes 125829120 | tf_op jit(solution)/shard_map/gather_one/pallas_call | solution.py:301
  84.6 0.5 all-gather.4.cloned.1.call-done.refs_1_
  85.1 0.0 all-gather.6.cloned.1.call-update
  85.1 0.0 all-gather.8.cloned.1.call-start
  85.2 29.7 %project.1 = (f32[1024,3072]{1,0:T(8,128)}, bf16[256,2048]{1,0:T(8,128)(2,1)}, bf16[256,2048]{1,0:T(8,128)(2,1)}) custom-call(bf16[1024,2048]{1,0:T(8,128)(2,1)} %gather_one.1.refs_0_.refs_3_, bf16[2048,3072]{1,0:T(8,128)(2,1)} %all-gather.4.cloned.1.call-done.refs_1_, bf16[256,2048]{1,0:T(8,128)(2,1)} %refs_3_.5, bf16[256,2048]{1,0:T(8,128)(2,1)} %refs_3_.5), custom_call_target="tpu_custom_call" | custom-call | flops 12884901888 | bytes 29360128 | tf_op jit(solution)/shard_map/project/pallas_call | solution.py:797
  114.9 28.1 %retention.1 = (bf16[1024,2048]{1,0:T(8,128)(2,1)}, bf16[1024,1024]{1,0:T(8,128)(2,1)}, bf16[256,3072]{1,0:T(8,128)(2,1)}, bf16[256,2048]{1,0:T(8,128)(2,1)}, bf16[256,2048]{1,0:T(8,128)(2,1)}) custom-call(f32[8]{0:T(128)} %constant.8.clone.refs_0_, f32[1024,3072]{1,0:T(8,128)} %get-tuple-element.75.refs_1_.refs_2_, ...), custom_call_target="tpu_custom_call" | custom-call | flops 2415919104 | bytes 18874368 | tf_op jit(solution)/shard_map/retention/pallas_call | solution.py:797
  142.9 0.0 all-gather.6.cloned.1.call-done.refs_1_.refs_4_
  143.0 0.0 all-gather.8.cloned.1.call-update
  143.0 0.0 reduce-scatter.3.cloned.1.call-start
  143.0 117.6 %residual.1 = (bf16[1024,2048]{1,0:T(8,128)(2,1)}, f32[256,2048]{1,0:T(8,128)}, bf16[2048,1024]{1,0:T(8,128)(2,1)}) custom-call(bf16[1024,1024]{1,0:T(8,128)(2,1)} %get-tuple-element.84.refs_0_.refs_1_, bf16[2048,1024]{1,0:T(8,128)(2,1)} %all-gather.6.cloned.1.call-done.refs_1_.refs_4_, bf16[256,2048]{1,0:T(8,128)(2,1)} %refs_2_.7, ...), custom_call_target="tpu_custom_call" | custom-call | bytes 125829120 | tf_op jit(solution)/shard_map/residual/pallas_call | solution.py:301
  260.6 0.0 all-gather.8.cloned.1.call-done.refs_1_.refs_2_.refs_7_
  260.7 25.8 %hidden_layer.1 = (f32[1024,2048]{1,0:T(8,128)}, bf16[1024,1024]{1,0:T(8,128)(2,1)}, bf16[1024,2048]{1,0:T(8,128)(2,1)}, bf16[256,2048]{1,0:T(8,128)(2,1)}, bf16[256,2048]{1,0:T(8,128)(2,1)}) custom-call(bf16[1024,2048]{1,0:T(8,128)(2,1)} %get-tuple-element.98.refs_0_.refs_10_, bf16[2048,3072]{1,0:T(8,128)(2,1)} %all-gather.8.cloned.1.call-done.refs_1_.refs_2_.refs_7_, ...), custom_call_target="tpu_custom_call" | custom-call | flops 12884901888 | bytes 27262976 | tf_op jit(solution)/shard_map/hidden_layer/pallas_call | solution.py:797
  286.5 31.5 %mlp_pull.1 = (bf16[1024,2048]{1,0:T(8,128)(2,1)}, bf16[2048,3072]{1,0:T(8,128)(2,1)}, bf16[256,2048]{1,0:T(8,128)(2,1)}, bf16[256,2048]{1,0:T(8,128)(2,1)}) custom-call(bf16[256,2048]{1,0:T(8,128)(2,1)} %refs_3_.5, bf16[256,2048]{1,0:T(8,128)(2,1)} %get-tuple-element.94.refs_9_.refs_1_, bf16[256,2048]{1,0:T(8,128)(2,1)} %get-tuple-element.95.refs_10_.refs_2_, ...), custom_call_target="tpu_custom_call" | custom-call | flops 17179869184 | bytes 46137344 | tf_op jit(solution)/shard_map/mlp_pull/pallas_call | solution.py:797
  318.0 0.0 reduce-scatter.3.cloned.1.call-update
  318.0 0.0 reduce-scatter.5.cloned.1.call-start
  318.0 118.3 %d_residual.1 = (bf16[1024,2048]{1,0:T(8,128)(2,1)}, f32[256,2048]{1,0:T(8,128)}) custom-call(bf16[1024,2048]{1,0:T(8,128)(2,1)} %get-tuple-element.105.refs_0_, bf16[2048,3072]{1,0:T(8,128)(2,1)} %all-gather.8.cloned.1.call-done.refs_1_.refs_2_.refs_7_, f32[256,2048]{1,0:T(8,128)} %get-tuple-element.106.refs_2_.refs_11_, bf16[256,2048]{1,0:T(8,128)(2,1)} %refs_3_.5), custom_call_target="tpu_custom_call" | custom-call | bytes 125829120 | tf_op jit(solution)/shard_map/d_residual/pallas_call | solution.py:301
  436.3 0.0 reduce-scatter.3.cloned.1.call-done
  436.3 19.1 %out_grads.1 = (bf16[2048,1024]{1,0:T(8,128)(2,1)}, bf16[256,2048]{1,0:T(8,128)(2,1)}, bf16[256,2048]{1,0:T(8,128)(2,1)}) custom-call(bf16[1024,2048]{1,0:T(8,128)(2,1)} %get-tuple-element.110.refs_0_.refs_3_, bf16[1024,1024]{1,0:T(8,128)(2,1)} %get-tuple-element.84.refs_0_.refs_1_, bf16[256,2048]{1,0:T(8,128)(2,1)} %get-tuple-element.111.refs_2_, ...), custom_call_target="tpu_custom_call" | custom-call | flops 4294967296 | bytes 10485760 | tf_op jit(solution)/shard_map/out_grads/pallas_call | solution.py:797
  455.4 0.0 copy-start.8
  455.4 0.0 copy-start.1
  455.4 0.0 copy-start
  455.4 0.0 reduce-scatter.5.cloned.1.call-update
  455.5 0.6 copy-done.8
  456.1 0.8 copy-done.1
  456.8 1.1 slice_convert_fusion
  457.9 0.0 copy-done
  457.9 0.5 fusion
  458.5 1.5 fusion.1
  459.9 26.6 %retention_pull.1 = (bf16[1024,3072]{1,0:T(8,128)(2,1)}, bf16[256,2048]{1,0:T(8,128)(2,1)}) custom-call(f32[8]{0:T(128)} %constant.8.clone.refs_0_, bf16[1024,2048]{1,0:T(8,128)(2,1)} %get-tuple-element.78.refs_1_, f32[1024,3072]{1,0:T(8,128)} %get-tuple-element.75.refs_1_.refs_2_, bf16[1024,2048]{1,0:T(8,128)(2,1)} %get-tuple-element.110.refs_0_.refs_3_, ...), custom_call_target="tpu_custom_call" | custom-call | flops 11542724608 | bytes 25165824 | tf_op jit(solution)/shard_map/retention_pull/pallas_call | solution.py:797
  486.6 0.8 broadcast_in_dim.2.refs_7_
  487.3 88.9 %tokens_grad.1 = (bf16[256,2048]{1,0:T(8,128)(2,1)}, f32[2,8,256]{2,1,0:T(8,128)}, f32[256,512]{1,0:T(8,128)}, f32[256,512]{1,0:T(8,128)}, f32[256,1024]{1,0:T(8,128)}, /*index=5*/f32[256,1024]{1,0:T(8,128)}) custom-call(bf16[1024,3072]{1,0:T(8,128)(2,1)} %get-tuple-element.119.refs_0_, bf16[2048,3072]{1,0:T(8,128)(2,1)} %all-gather.4.cloned.1.call-done.refs_1_, ...), custom_call_target="tpu_custom_call" | custom-call | bytes 125829120 | tf_op jit(solution)/shard_map/tokens_grad/pallas_call | solution.py:301
  576.2 0.0 copy-start.2
  576.2 0.0 copy-start.5
  576.2 1.4 fusion.2
  577.6 2.1 convert_element_type.20
  579.8 0.0 copy-done.2
  579.8 1.0 copy.37
  580.7 0.0 copy-done.5
  580.8 1.0 copy.38
  581.7 0.8 copy.39
  582.5 0.8 copy.40
  583.3 1.0 copy.41
  584.3 0.0 copy-done.3
  584.3 1.0 copy.42
  (9 shorter events, 0.0 us)
Async XLA Ops:
  7.2 77.9 %all-gather.4.cloned.1.call-start = ((), (), s32[]{:S(2)}) async-start(), calls=%async_computation.2 | async-start | bytes 14155776 | tf_op jit(solution)/shard_map/all_gather | solution.py:1193
  10.1 132.8 %all-gather.6.cloned.1.call-start = ((), (), s32[]{:S(2)}) async-start(), calls=%async_computation.3 | async-start | bytes 4718592 | tf_op jit(solution)/shard_map/all_gather | solution.py:1193
  85.1 175.5 %all-gather.8.cloned.1.call-start = ((), (), s32[]{:S(2)}) async-start(), calls=%async_computation.4 | async-start | bytes 14155776 | tf_op jit(solution)/shard_map/all_gather | solution.py:1193
  143.0 293.3 %reduce-scatter.3.cloned.1.call-start = ((), (), s32[]{:S(2)}) async-start(), calls=%async_computation.5 | async-start | bytes 14155776 | tf_op jit(solution)/shard_map/reduce_scatter | solution.py:1196
  318.0 259.7 %reduce-scatter.5.cloned.1.call-start = ((), (), s32[]{:S(2)}) async-start(), calls=%async_computation.6 | async-start | bytes 4718592 | tf_op jit(solution)/shard_map/reduce_scatter | solution.py:1196
  455.4 0.7 copy-start.8
  455.4 1.4 copy-start.1
  455.4 2.5 copy-start
  576.2 3.6 copy-start.2
  576.2 4.5 copy-start.5
  579.8 2.0 copy-start.7
  580.7 1.8 copy-start.6
  580.8 2.6 copy-start.4
  581.7 2.6 copy-start.3
Sparse Core Ops, SparseCore 0:
  10.3 74.8 all-gather.3
  87.0 36.7 all-gather.5
  143.1 71.2 all-gather.7
  318.1 91.1 reduce-scatter.2
  455.6 53.2 reduce-scatter.4

commit v8 on v7

--- a/solution.py
+++ b/solution.py
@@ -437,7 +437,7 @@
                     sums[bit] = sums[bit - 1] + sums_in[bit - 1]
                 else:
                     sums[0, 0] = terms_one[...].T[: sums.shape[2]]
-                    sums[0, 1] = other_terms[...].T[: sums.shape[2]]
+                    sums[0, 1] = jnp.broadcast_to(as_row(other_terms), sums.shape[2:])
                 if bit < line_bits:
                     sums_copy(bit).start()
                 else:
@@ -1258,7 +1258,6 @@
     )
     pair_grad, down_grad = mlp_grad[:, : 2 * hidden_cols], mlp_grad[:, 2 * hidden_cols :].astype(jnp.float32)
     terms_two = gain_terms(mlp_own[:, : 2 * hidden_cols], pair_grad)
-    terms_two = jnp.broadcast_to(terms_two[:, None], (terms_two.shape[0], 128))
     pair_grad = pair_grad.astype(jnp.float32) * mlp_gain.astype(jnp.float32)[:, None]
     gate_grad, up_grad = pair_grad[:, :hidden_cols], pair_grad[:, hidden_cols:]
     d_in, result, gate_grad, up_grad, down_grad = after((d_in, result, gate_grad, up_grad, down_grad))

time: 593 us -> 592 us (level)
  no operation moved by 1% of the time
where the time goes in v8:
time: 592 us; the launch traced here: 591 us
  Pallas kernels  562 us (95%)
  between operations  13.9 us (2%)
  local copies, waits for them, and re-layouts  9.74 us (2%)
    pallas_call x4, Pallas kernels, line_pass(): pl.pallas_call(functools.partial(line_body, n, chunks, rs, ag, rolled, mi...  399 us
    pallas_call x6, Pallas kernels, hop_call(): return lambda *operands: call(*operands, *arrays, *added)  161 us
  transfers between devices with their start and end apart: 5, of which 1 were waited for; matrix products, arithmetic and copies ran while one was open for 1% of the time, Pallas kernels for 82%

profile of v8, /device:TPU:0, one launch (start us, length us, event | category | flops | bytes accessed | tf_op | source)
XLA Modules:
  0.0 591.2 jit_solution(5672972235228487696)
XLA Ops:
  7.2 0.0 all-gather.4.cloned.1.call-start
  7.2 2.9 join_in.1.refs_6_
  10.1 0.0 all-gather.4.cloned.1.call-update
  10.1 0.0 all-gather.6.cloned.1.call-start
  10.2 74.4 %gather_one.1.refs_0_.refs_3_ = bf16[1024,2048]{1,0:T(8,128)(2,1)} custom-call(bf16[256,2048]{1,0:T(8,128)(2,1)} %refs_2_.7), custom_call_target="tpu_custom_call" | custom-call | bytes 125829120 | tf_op jit(solution)/shard_map/gather_one/pallas_call | solution.py:301
  84.6 0.5 all-gather.4.cloned.1.call-done.refs_1_
  85.1 0.0 all-gather.6.cloned.1.call-update
  85.1 0.0 all-gather.8.cloned.1.call-start
  85.2 29.7 %project.1 = (f32[1024,3072]{1,0:T(8,128)}, bf16[256,2048]{1,0:T(8,128)(2,1)}, bf16[256,2048]{1,0:T(8,128)(2,1)}) custom-call(bf16[1024,2048]{1,0:T(8,128)(2,1)} %gather_one.1.refs_0_.refs_3_, bf16[2048,3072]{1,0:T(8,128)(2,1)} %all-gather.4.cloned.1.call-done.refs_1_, bf16[256,2048]{1,0:T(8,128)(2,1)} %refs_3_.5, bf16[256,2048]{1,0:T(8,128)(2,1)} %refs_3_.5), custom_call_target="tpu_custom_call" | custom-call | flops 12884901888 | bytes 29360128 | tf_op jit(solution)/shard_map/project/pallas_call | solution.py:797
  114.9 28.1 %retention.1 = (bf16[1024,2048]{1,0:T(8,128)(2,1)}, bf16[1024,1024]{1,0:T(8,128)(2,1)}, bf16[256,3072]{1,0:T(8,128)(2,1)}, bf16[256,2048]{1,0:T(8,128)(2,1)}, bf16[256,2048]{1,0:T(8,128)(2,1)}) custom-call(f32[8]{0:T(128)} %constant.8.clone.refs_0_, f32[1024,3072]{1,0:T(8,128)} %get-tuple-element.75.refs_1_.refs_2_, ...), custom_call_target="tpu_custom_call" | custom-call | flops 2415919104 | bytes 18874368 | tf_op jit(solution)/shard_map/retention/pallas_call | solution.py:797
  142.9 0.0 all-gather.6.cloned.1.call-done.refs_1_.refs_4_
  143.0 0.0 all-gather.8.cloned.1.call-update
  143.0 0.0 reduce-scatter.3.cloned.1.call-start
  143.0 117.6 %residual.1 = (bf16[1024,2048]{1,0:T(8,128)(2,1)}, f32[256,2048]{1,0:T(8,128)}, bf16[2048,1024]{1,0:T(8,128)(2,1)}) custom-call(bf16[1024,1024]{1,0:T(8,128)(2,1)} %get-tuple-element.84.refs_0_.refs_1_, bf16[2048,1024]{1,0:T(8,128)(2,1)} %all-gather.6.cloned.1.call-done.refs_1_.refs_4_, bf16[256,2048]{1,0:T(8,128)(2,1)} %refs_2_.7, ...), custom_call_target="tpu_custom_call" | custom-call | bytes 125829120 | tf_op jit(solution)/shard_map/residual/pallas_call | solution.py:301
  260.6 0.0 all-gather.8.cloned.1.call-done.refs_1_.refs_2_.refs_7_
  260.7 25.8 %hidden_layer.1 = (f32[1024,2048]{1,0:T(8,128)}, bf16[1024,1024]{1,0:T(8,128)(2,1)}, bf16[1024,2048]{1,0:T(8,128)(2,1)}, bf16[256,2048]{1,0:T(8,128)(2,1)}, bf16[256,2048]{1,0:T(8,128)(2,1)}) custom-call(bf16[1024,2048]{1,0:T(8,128)(2,1)} %get-tuple-element.98.refs_0_.refs_10_, bf16[2048,3072]{1,0:T(8,128)(2,1)} %all-gather.8.cloned.1.call-done.refs_1_.refs_2_.refs_7_, ...), custom_call_target="tpu_custom_call" | custom-call | flops 12884901888 | bytes 27262976 | tf_op jit(solution)/shard_map/hidden_layer/pallas_call | solution.py:797
  286.5 31.5 %mlp_pull.1 = (bf16[1024,2048]{1,0:T(8,128)(2,1)}, bf16[2048,3072]{1,0:T(8,128)(2,1)}, bf16[256,2048]{1,0:T(8,128)(2,1)}, bf16[256,2048]{1,0:T(8,128)(2,1)}) custom-call(bf16[256,2048]{1,0:T(8,128)(2,1)} %refs_3_.5, bf16[256,2048]{1,0:T(8,128)(2,1)} %get-tuple-element.94.refs_9_.refs_1_, bf16[256,2048]{1,0:T(8,128)(2,1)} %get-tuple-element.95.refs_10_.refs_2_, ...), custom_call_target="tpu_custom_call" | custom-call | flops 17179869184 | bytes 46137344 | tf_op jit(solution)/shard_map/mlp_pull/pallas_call | solution.py:797
  318.0 0.0 reduce-scatter.3.cloned.1.call-update
  318.0 0.0 reduce-scatter.5.cloned.1.call-start
  318.0 118.3 %d_residual.1 = (bf16[1024,2048]{1,0:T(8,128)(2,1)}, f32[256,2048]{1,0:T(8,128)}) custom-call(bf16[1024,2048]{1,0:T(8,128)(2,1)} %get-tuple-element.105.refs_0_, bf16[2048,3072]{1,0:T(8,128)(2,1)} %all-gather.8.cloned.1.call-done.refs_1_.refs_2_.refs_7_, f32[256,2048]{1,0:T(8,128)} %get-tuple-element.106.refs_2_.refs_11_, bf16[256,2048]{1,0:T(8,128)(2,1)} %refs_3_.5), custom_call_target="tpu_custom_call" | custom-call | bytes 125829120 | tf_op jit(solution)/shard_map/d_residual/pallas_call | solution.py:301
  436.3 0.0 reduce-scatter.3.cloned.1.call-done
  436.3 19.1 %out_grads.1 = (bf16[2048,1024]{1,0:T(8,128)(2,1)}, bf16[256,2048]{1,0:T(8,128)(2,1)}, bf16[256,2048]{1,0:T(8,128)(2,1)}) custom-call(bf16[1024,2048]{1,0:T(8,128)(2,1)} %get-tuple-element.110.refs_0_.refs_3_, bf16[1024,1024]{1,0:T(8,128)(2,1)} %get-tuple-element.84.refs_0_.refs_1_, bf16[256,2048]{1,0:T(8,128)(2,1)} %get-tuple-element.111.refs_2_, ...), custom_call_target="tpu_custom_call" | custom-call | flops 4294967296 | bytes 10485760 | tf_op jit(solution)/shard_map/out_grads/pallas_call | solution.py:797
  455.4 0.0 copy-start.8
  455.4 0.0 copy-start.1
  455.4 0.0 copy-start
  455.4 0.0 reduce-scatter.5.cloned.1.call-update
  455.5 0.6 copy-done.8
  456.1 0.8 copy-done.1
  456.8 1.1 slice_convert_fusion
  457.9 0.0 copy-done
  457.9 1.0 fusion
  458.9 1.4 fusion.1
  460.3 26.7 %retention_pull.1 = (bf16[1024,3072]{1,0:T(8,128)(2,1)}, bf16[256,2048]{1,0:T(8,128)(2,1)}) custom-call(f32[8]{0:T(128)} %constant.8.clone.refs_0_, bf16[1024,2048]{1,0:T(8,128)(2,1)} %get-tuple-element.78.refs_1_, f32[1024,3072]{1,0:T(8,128)} %get-tuple-element.75.refs_1_.refs_2_, bf16[1024,2048]{1,0:T(8,128)(2,1)} %get-tuple-element.110.refs_0_.refs_3_, ...), custom_call_target="tpu_custom_call" | custom-call | flops 11542724608 | bytes 25165824 | tf_op jit(solution)/shard_map/retention_pull/pallas_call | solution.py:797
  487.0 88.6 %tokens_grad.1 = (bf16[256,2048]{1,0:T(8,128)(2,1)}, f32[2,8,256]{2,1,0:T(8,128)}, f32[256,512]{1,0:T(8,128)}, f32[256,512]{1,0:T(8,128)}, f32[256,1024]{1,0:T(8,128)}, /*index=5*/f32[256,1024]{1,0:T(8,128)}) custom-call(bf16[1024,3072]{1,0:T(8,128)(2,1)} %get-tuple-element.119.refs_0_, bf16[2048,3072]{1,0:T(8,128)(2,1)} %all-gather.4.cloned.1.call-done.refs_1_, ...), custom_call_target="tpu_custom_call" | custom-call | bytes 125829120 | tf_op jit(solution)/shard_map/tokens_grad/pallas_call | solution.py:301
  575.6 0.0 copy-start.2
  575.6 0.0 copy-start.5
  575.6 1.4 fusion.2
  577.1 2.1 convert_element_type.20
  579.2 0.0 copy-done.2
  579.2 1.0 copy.37
  580.2 0.0 copy-done.5
  580.2 1.0 copy.38
  581.1 0.0 copy-done.7
  581.1 0.8 copy.39
  581.9 0.8 copy.40
  582.7 0.0 copy-done.4
  582.7 1.0 copy.41
  583.7 1.0 copy.42
  (8 shorter events, 0.0 us)
Async XLA Ops:
  7.2 77.9 %all-gather.4.cloned.1.call-start = ((), (), s32[]{:S(2)}) async-start(), calls=%async_computation.2 | async-start | bytes 14155776 | tf_op jit(solution)/shard_map/all_gather | solution.py:1193
  10.1 132.8 %all-gather.6.cloned.1.call-start = ((), (), s32[]{:S(2)}) async-start(), calls=%async_computation.3 | async-start | bytes 4718592 | tf_op jit(solution)/shard_map/all_gather | solution.py:1193
  85.1 175.5 %all-gather.8.cloned.1.call-start = ((), (), s32[]{:S(2)}) async-start(), calls=%async_computation.4 | async-start | bytes 14155776 | tf_op jit(solution)/shard_map/all_gather | solution.py:1193
  143.0 293.3 %reduce-scatter.3.cloned.1.call-start = ((), (), s32[]{:S(2)}) async-start(), calls=%async_computation.5 | async-start | bytes 14155776 | tf_op jit(solution)/shard_map/reduce_scatter | solution.py:1196
  318.0 259.1 %reduce-scatter.5.cloned.1.call-start = ((), (), s32[]{:S(2)}) async-start(), calls=%async_computation.6 | async-start | bytes 4718592 | tf_op jit(solution)/shard_map/reduce_scatter | solution.py:1196
  455.4 0.7 copy-start.8
  455.4 1.4 copy-start.1
  455.4 2.5 copy-start
  575.6 3.6 copy-start.2
  575.6 4.5 copy-start.5
  579.2 2.0 copy-start.7
  580.2 1.8 copy-start.6
  580.2 2.6 copy-start.4
  581.1 2.6 copy-start.3
Sparse Core Ops, SparseCore 0:
  10.3 74.8 all-gather.3
  87.0 36.7 all-gather.5
  143.1 71.2 all-gather.7
  318.1 91.1 reduce-scatter.2
  455.6 53.2 reduce-scatter.4
